TPU v7x, 256 devices: a whole 4x4x8 slice. The times are simulated.
256 devices in a mesh: ctx: 64 (over x, z, core), head: 4 (over y).
Axes of the slice: x: 4, y: 4, z: 8, core: 2. Of those that a mesh axis runs over, the one named last changes fastest.
Arguments:
- queries: bfloat16 [8192, 4096], P('ctx', 'head'), may hold values from -140 to 140
- keys: bfloat16 [8192, 4096], P('ctx', 'head'), may hold values from -5 to 5
- values: bfloat16 [8192, 4096], P('ctx', 'head'), may hold values from -22 to 22
- init_state: float32 [32, 128, 128], P('head'), may hold values from -48 to 48
- lin_gain: float32 [4096], P('head'), may hold values from 0.25 to 1.75
- rate_table: float32 [16], replicated, may hold values from 0 to 0.04
- rate_index: int32 [32], P('head'), may hold values from 0 to 15
- speed: float32 [8192, 32], P('ctx', 'head'), may hold values from 0.45 to 2
- drop: float32 [8192, 32], P('ctx', 'head'), may hold values from 0 to 1.4
- doc_id: int32 [8192], P('ctx'), may hold values from 0 to 3, as said below
Outputs:
- mixed: bfloat16 [8192, 4096], P('ctx', 'head')
Inputs may be any that keep to these rules, and one draw needn't show every extreme that they name: `doc_id`: never falling from token to token, every document present; each document has at most 4096 tokens, and one has exactly that many; document 0 continues the document of the carried state.
All inputs are finite; a program needn't handle non-finite values.
Results may differ from a plain program's by a relative error of at most 0.0095.
Values may be sent and summed in bfloat16 or wider, within the bound.
No kernel may reach another device: no remote copies, remote signals or barrier semaphores. Data moves between devices by JAX's collectives and lax.ppermute only.
A program may use at most 192 MiB of HBM per device.

v0:
```python
import math

import jax
import jax.numpy as jnp
from jax import lax
from jax.sharding import PartitionSpec as P

HEAD_TOTAL = 32
DH = 128
WINDOW = 4096


def entering_2(x, axis, combine, identity):
    peers, position = (lax.axis_size(axis), lax.axis_index(axis))
    everything = jax.tree.map(
        lambda part, kind: lax.all_gather(part.astype(kind), axis),
        x,
        (jnp.bfloat16, jnp.bfloat16, jnp.bfloat16),
    )
    start = jax.tree.map(
        lambda part, zero: jnp.broadcast_to(jnp.asarray(zero, part.dtype), part.shape), x, identity
    )

    def hop(k, before):
        reached = k < position
        new = combine(
            before, jax.tree.map(lambda part, own: part[k].astype(own.dtype), everything, x)
        )
        return jax.tree.map(lambda a, b: jnp.where(reached, a, b), new, before)

    return lax.fori_loop(0, peers, hop, start)


def from_behind(value, axis, steps):
    count = lax.axis_size(axis)
    leading, last = (max(0, -steps), min(count, count - steps))
    return lax.ppermute(value, axis, [(source, source + steps) for source in range(leading, last)])


def linear_block(query_part, key_part, value_part, cumulative, doc_part, score_scale):
    places = jnp.arange(query_part.shape[0])
    inside = (places[:, None] >= places[None, :]) & (doc_part[:, None] == doc_part[None, :])
    spread = cumulative.T[:, :, None] - cumulative.T[:, None, :]
    fading = jnp.exp(jnp.where(inside[None], spread, 0.0))
    affinity = jnp.einsum("thd,shd->hts", query_part, key_part, preferred_element_type=jnp.float32)
    weights = jnp.where(inside[None], fading * affinity * score_scale, 0.0).astype(jnp.bfloat16)
    within = jnp.einsum("hts,shd->thd", weights, value_part, preferred_element_type=jnp.float32)
    overall = cumulative[-1]
    keeping = doc_part == doc_part[-1]
    factor = jnp.where(keeping[:, None], jnp.exp(overall[None, :] - cumulative), 0.0)
    scaled = (key_part.astype(jnp.float32) * factor[:, :, None]).astype(jnp.bfloat16)
    summary = jnp.einsum("shd,she->hde", scaled, value_part, preferred_element_type=jnp.float32)
    return (within, overall, summary)


def link_states(earlier, later):
    early_decay, early_state, early_doc = earlier
    late_decay, late_state, late_doc = later
    joined = jnp.where((early_doc == late_doc) | (late_doc < 0.0), 1.0, 0.0)
    merged_state = jnp.exp(late_decay)[:, None, None] * early_state * joined[0] + late_state
    merged_doc = jnp.where(late_doc < 0.0, early_doc, late_doc)
    return (early_decay + late_decay, merged_state, merged_doc)


def body(queries, keys, values, init_state, lin_gain, rate_table, rate_index, speed, drop, doc_id):
    length = queries.shape[0]
    col_count = queries.shape[1]
    head_count = col_count // DH
    score_scale = 1.0 / math.sqrt(DH)
    my_index = lax.axis_index("ctx")
    query_heads = queries.reshape(length, head_count, DH)
    key_heads = keys.reshape(length, head_count, DH)
    value_heads = values.reshape(length, head_count, DH)
    doc_float = doc_id.astype(jnp.float32)
    picked = rate_index[:, None] == jnp.arange(rate_table.shape[0], dtype=jnp.int32)[None, :]
    head_rate = jnp.sum(jnp.where(picked, rate_table[None, :], 0.0), axis=1)
    log_decay = -head_rate[None, :] * speed - drop
    cumulative = jnp.cumsum(log_decay, axis=0)
    within, overall, summary = linear_block(
        query_heads, key_heads, value_heads, cumulative, doc_float, score_scale
    )
    neutral = (jnp.zeros_like(overall), jnp.zeros_like(summary), jnp.full((1,), -1.0, jnp.float32))
    prior_decay, prior_state, prior_doc = entering_2(
        (overall, summary, doc_float[-1:]), "ctx", link_states, neutral
    )
    carry_doc = jnp.where(prior_doc[0] < 0.0, 0.0, prior_doc[0])
    from_start = jnp.where(carry_doc == 0.0, 1.0, 0.0)
    entering = prior_state + jnp.exp(prior_decay)[:, None, None] * init_state * from_start
    projected = jnp.einsum(
        "thd,hde->the", query_heads.astype(jnp.float32), entering, precision=lax.Precision.HIGHEST
    )
    live = (doc_float == carry_doc)[:, None, None]
    outside = jnp.where(live, jnp.exp(cumulative)[:, :, None] * projected * score_scale, 0.0)
    linear_out = within + outside
    square_sum = jnp.sum(linear_out * linear_out, axis=(1, 2))
    square_total = lax.psum(square_sum, "head")
    inverse_rms = lax.rsqrt(square_total / (HEAD_TOTAL * DH) + 1e-06)
    places = jnp.arange(length, dtype=jnp.int32)
    my_place = my_index * length + places
    doc_half = doc_id.astype(jnp.bfloat16)

    def absorb_block(carry_state, key_block, value_block, doc_block, distance):
        key_place = (my_index - distance) * length + places
        allowed = (key_place[None, :] <= my_place[:, None]) & (
            key_place[None, :] > my_place[:, None] - WINDOW
        )
        allowed = allowed & (key_place[None, :] >= 0) & (doc_block[None, :] == doc_half[:, None])
        old_max, old_weight, old_output = carry_state
        scores = (
            jnp.einsum(
                "thd,shd->hts",
                query_heads,
                key_block.reshape(length, head_count, DH),
                preferred_element_type=jnp.float32,
            )
            * score_scale
        )
        scores = jnp.where(allowed[None], scores, -1e30)
        new_max = jnp.maximum(old_max, jnp.max(scores, axis=2))
        weights = jnp.exp(scores - new_max[:, :, None])
        shrink = jnp.exp(old_max - new_max)
        new_weight = old_weight * shrink + jnp.sum(weights, axis=2)
        gathered = jnp.einsum(
            "hts,shd->htd",
            weights.astype(jnp.bfloat16),
            value_block.reshape(length, head_count, DH),
            preferred_element_type=jnp.float32,
        )
        new_output = old_output * shrink[:, :, None] + gathered
        return (new_max, new_weight, new_output)

    running = (
        jnp.full((head_count, length), -1e30, jnp.float32),
        jnp.zeros((head_count, length), jnp.float32),
        jnp.zeros((head_count, length, DH), jnp.float32),
    )
    running = absorb_block(running, keys, values, doc_half, 0)
    back_count = min((WINDOW - 1) // length + 1, lax.axis_size("ctx") - 1)
    for distance in range(1, back_count + 1):
        arrived = from_behind((keys, values, doc_half), "ctx", distance)
        running = absorb_block(running, arrived[0], arrived[1], arrived[2], distance)
    top_score, weight_sum, output_sum = running
    window_out = (output_sum / weight_sum[:, :, None]).transpose(1, 0, 2)
    gain_heads = lin_gain.reshape(head_count, DH)
    mixed = gain_heads[None] * linear_out * inverse_rms[:, None, None] + window_out
    return mixed.astype(jnp.bfloat16).reshape(length, col_count)


def solution(mesh):
    placed = (
        P("ctx", "head"),
        P("ctx", "head"),
        P("ctx", "head"),
        P("head", None, None),
        P("head"),
        P(),
        P("head"),
        P("ctx", "head"),
        P("ctx", "head"),
        P("ctx"),
    )
    return jax.shard_map(
        body, mesh=mesh, in_specs=placed, out_specs=P("ctx", "head"), check_vma=False
    )
```

profile of v0, /device:TPU:4, one launch (start us, length us, event | category | flops | bytes accessed | tf_op | source)
XLA Modules:
  0.0 1402.2 jit_solution(16762112961273422001)
XLA Ops:
  17.0 9.3 collective-permute-start.75
  32.9 40.9 %all-gather.2 = bf16[64,1,8]{2,1,0:T(2,128)(2,1)S(1)} all-gather(bf16[1,1,8]{2,1,0:T(2,128)(2,1)S(1)} %convert_bitcast_fusion), channel_id=1, replica_groups=mesh['ctx'=64,'head'=4] {'ctx'}, dimensions={0}, use_global_device_ids=true | all-gather | bytes 1040 | tf_op jit(solution)/shard_map/all_gather | solution.py:16
  78.2 106.5 %all-reduce = bf16[64]{0:T(256)(128)(2,1)} all-reduce(bf16[64]{0:T(256)(128)(2,1)S(1)} %dynamic-update-slice), channel_id=2, replica_groups=mesh['ctx'=64,'head'=4] {'ctx'}, use_global_device_ids=true, to_apply=%add | all-reduce | flops 64 | bytes 256
  186.0 19.1 %collective-permute-start.87 = (bf16[128]{0:T(256)(128)(2,1)S(1)}, bf16[128]{0:T(256)(128)(2,1)S(1)}, u32[]{:S(2)}, u32[]{:S(2)}) collective-permute-start(bf16[128]{0:T(256)(128)(2,1)S(1)} %get-tuple-element.340), channel_id=1, source_target_pairs={{0,120},{4,124},{8,128},{12,132},{16,136},{20,140},{24,144},{28,14... | collective-permute-start | bytes 776 | tf_op jit(solution)/shard_map/ppermute | solution.py:37
  277.8 10.8 collective-permute-start.13
  288.6 13.1 collective-permute-start.10
  301.7 13.1 collective-permute-start.7
  345.2 44.4 %collective-permute-done.82 = bf16[128,1024]{0,1:T(8,128)(2,1)S(1)} collective-permute-done((bf16[128,1024]{0,1:T(8,128)(2,1)}, bf16[128,1024]{0,1:T(8,128)(2,1)S(1)}, u32[]{:S(2)}, u32[]{:S(2)}) %collective-permute-start.82) | collective-permute-done | bytes 262176 | tf_op jit(solution)/shard_map/ppermute | solution.py:37
  428.4 18.3 %collective-permute-done.58 = bf16[128,1024]{0,1:T(8,128)(2,1)S(1)} collective-permute-done((bf16[128,1024]{0,1:T(8,128)(2,1)}, bf16[128,1024]{0,1:T(8,128)(2,1)S(1)}, u32[]{:S(2)}, u32[]{:S(2)}) %collective-permute-start.58) | collective-permute-done | bytes 262176 | tf_op jit(solution)/shard_map/ppermute | solution.py:37
  463.6 16.4 %collective-permute-done.43 = bf16[128,1024]{0,1:T(8,128)(2,1)S(1)} collective-permute-done((bf16[128,1024]{0,1:T(8,128)(2,1)}, bf16[128,1024]{0,1:T(8,128)(2,1)S(1)}, u32[]{:S(2)}, u32[]{:S(2)}) %collective-permute-start.43) | collective-permute-done | bytes 262176 | tf_op jit(solution)/shard_map/ppermute | solution.py:37
  498.7 12.7 collective-permute-done.28
  526.8 9.4 collective-permute-start.11
  536.2 13.9 collective-permute-start.8
  570.7 16.9 %collective-permute-done.8 = bf16[128,1024]{1,0:T(8,128)(2,1)S(1)} collective-permute-done((bf16[128,1024]{1,0:T(8,128)(2,1)}, bf16[128,1024]{1,0:T(8,128)(2,1)S(1)}, u32[]{:S(2)}, u32[]{:S(2)}) %collective-permute-start.8) | collective-permute-done | bytes 262176 | tf_op jit(solution)/shard_map/ppermute | solution.py:37
  594.9 9.6 collective-permute-done.65
  618.3 13.2 collective-permute-done.59
  633.5 11.0 collective-permute-done.56
  648.2 9.4 collective-permute-done.53
  683.0 26.9 %collective-permute-start.23 = (bf16[128,1024]{1,0:T(8,128)(2,1)}, bf16[128,1024]{1,0:T(8,128)(2,1)S(1)}, u32[]{:S(2)}, u32[]{:S(2)}) collective-permute-start(bf16[128,1024]{1,0:T(8,128)(2,1)} %param.14), channel_id=1, source_target_pairs={{0,32},{4,36},{8,40},{12,44},{16,48},{20,52},{24,56},{28,60},{32,6... | collective-permute-start | bytes 786440 | tf_op jit(solution)/shard_map/ppermute | solution.py:37
  719.6 25.4 %collective-permute-done.29 = bf16[128,1024]{1,0:T(8,128)(2,1)S(1)} collective-permute-done((bf16[128,1024]{1,0:T(8,128)(2,1)}, bf16[128,1024]{1,0:T(8,128)(2,1)S(1)}, u32[]{:S(2)}, u32[]{:S(2)}) %collective-permute-start.29) | collective-permute-done | bytes 262176 | tf_op jit(solution)/shard_map/ppermute | solution.py:37
  758.2 40.6 %collective-permute-done.86 = bf16[128,1024]{1,0:T(8,128)(2,1)S(1)} collective-permute-done((bf16[128,1024]{1,0:T(8,128)(2,1)}, bf16[128,1024]{1,0:T(8,128)(2,1)S(1)}, u32[]{:S(2)}, u32[]{:S(2)}) %collective-permute-start.86) | collective-permute-done | bytes 262176 | tf_op jit(solution)/shard_map/ppermute | solution.py:37
  821.3 45.7 %collective-permute-start.92 = (bf16[128,1024]{1,0:T(8,128)(2,1)}, bf16[128,1024]{1,0:T(8,128)(2,1)}, u32[]{:S(2)}, u32[]{:S(2)}) collective-permute-start(bf16[128,1024]{1,0:T(8,128)(2,1)} %param.14), channel_id=1, source_target_pairs={{0,124},{4,128},{8,132},{12,136},{16,140},{20,144},{24,148},{28,15... | collective-permute-start | bytes 786440 | tf_op jit(solution)/shard_map/ppermute | solution.py:37
  1021.8 350.3 %while.18 = (s32[]{:T(128)}, f32[8]{0:T(128)}, f32[8,128,128]{2,1,0:T(8,128)S(1)}, f32[1]{0:T(128)}, s32[]{:T(128)}, /*index=5*/bf16[64,8]{1,0:T(8,128)(2,1)}, b...) while((s32[]{:T(128)}, f32[8]{0:T(128)}, ...), condition=%wide.region_3.4_spmd.clone, body=%wide.region_2.3_spmd.clone.sunk | while | flops 786474 | bytes 1311077 | solution.py:31
  1376.7 10.6 psum.7
  (812 shorter events, 728.8 us)
Async XLA Ops:
  6.5 1015.3 %all-gather.5.cloned.1.call-start = ((), (), s32[]{:S(2)}) async-start(), calls=%async_computation | async-start | bytes 17039360 | tf_op jit(solution)/shard_map/all_gather | solution.py:16
  15.1 262.7 %collective-permute-start = (bf16[128]{0:T(256)(128)(2,1)S(1)}, bf16[128]{0:T(256)(128)(2,1)S(1)}, u32[]{:S(2)}, u32[]{:S(2)}) collective-permute-start(bf16[128]{0:T(256)(128)(2,1)S(1)} %get-tuple-element.340), channel_id=1, source_target_pairs={{0,4},{4,8},{8,12},{12,16},{16,20},{20,24},{24,28},{28,32},{32,36}... | collective-permute-start | bytes 776 | tf_op jit(solution)/shard_map/ppermute | solution.py:37
  17.0 169.0 %collective-permute-start.75 = (bf16[128]{0:T(256)(128)(2,1)S(1)}, bf16[128]{0:T(256)(128)(2,1)S(1)}, u32[]{:S(2)}, u32[]{:S(2)}) collective-permute-start(bf16[128]{0:T(256)(128)(2,1)S(1)} %get-tuple-element.340), channel_id=1, source_target_pairs={{0,104},{4,108},{8,112},{12,116},{16,120},{20,124},{24,128},{28,13... | collective-permute-start | bytes 776 | tf_op jit(solution)/shard_map/ppermute | solution.py:37
  26.3 178.8 %collective-permute-start.78 = (bf16[128]{0:T(256)(128)(2,1)S(1)}, bf16[128]{0:T(256)(128)(2,1)S(1)}, u32[]{:S(2)}, u32[]{:S(2)}) collective-permute-start(bf16[128]{0:T(256)(128)(2,1)S(1)} %get-tuple-element.340), channel_id=1, source_target_pairs={{0,108},{4,112},{8,116},{12,120},{16,124},{20,128},{24,132},{28,13... | collective-permute-start | bytes 776 | tf_op jit(solution)/shard_map/ppermute | solution.py:37
  28.3 178.7 %collective-permute-start.81 = (bf16[128]{0:T(256)(128)(2,1)S(1)}, bf16[128]{0:T(256)(128)(2,1)S(1)}, u32[]{:S(2)}, u32[]{:S(2)}) collective-permute-start(bf16[128]{0:T(256)(128)(2,1)S(1)} %get-tuple-element.340), channel_id=1, source_target_pairs={{0,112},{4,116},{8,120},{12,124},{16,128},{20,132},{24,136},{28,14... | collective-permute-start | bytes 776 | tf_op jit(solution)/shard_map/ppermute | solution.py:37
  30.2 178.7 %collective-permute-start.84 = (bf16[128]{0:T(256)(128)(2,1)S(1)}, bf16[128]{0:T(256)(128)(2,1)S(1)}, u32[]{:S(2)}, u32[]{:S(2)}) collective-permute-start(bf16[128]{0:T(256)(128)(2,1)S(1)} %get-tuple-element.340), channel_id=1, source_target_pairs={{0,116},{4,120},{8,124},{12,128},{16,132},{20,136},{24,140},{28,14... | collective-permute-start | bytes 776 | tf_op jit(solution)/shard_map/ppermute | solution.py:37
  322.8 66.7 %collective-permute-start.82 = (bf16[128,1024]{0,1:T(8,128)(2,1)}, bf16[128,1024]{0,1:T(8,128)(2,1)S(1)}, u32[]{:S(2)}, u32[]{:S(2)}) collective-permute-start(bf16[128,1024]{0,1:T(8,128)(2,1)} %copy.1367), channel_id=1, source_target_pairs={{0,112},{4,116},{8,120},{12,124},{16,128},{20,132},{24,136},{28,14... | collective-permute-start | bytes 786440 | tf_op jit(solution)/shard_map/ppermute | solution.py:37
  330.7 64.4 %collective-permute-start.79 = (bf16[128,1024]{0,1:T(8,128)(2,1)}, bf16[128,1024]{0,1:T(8,128)(2,1)S(1)}, u32[]{:S(2)}, u32[]{:S(2)}) collective-permute-start(bf16[128,1024]{0,1:T(8,128)(2,1)} %copy.1367), channel_id=1, source_target_pairs={{0,108},{4,112},{8,116},{12,120},{16,124},{20,128},{24,132},{28,13... | collective-permute-start | bytes 786440 | tf_op jit(solution)/shard_map/ppermute | solution.py:37
  334.9 65.9 %collective-permute-start.76 = (bf16[128,1024]{0,1:T(8,128)(2,1)}, bf16[128,1024]{0,1:T(8,128)(2,1)S(1)}, u32[]{:S(2)}, u32[]{:S(2)}) collective-permute-start(bf16[128,1024]{0,1:T(8,128)(2,1)} %copy.1367), channel_id=1, source_target_pairs={{0,104},{4,108},{8,112},{12,116},{16,120},{20,124},{24,128},{28,13... | collective-permute-start | bytes 786440 | tf_op jit(solution)/shard_map/ppermute | solution.py:37
  338.5 65.1 %collective-permute-start.73 = (bf16[128,1024]{0,1:T(8,128)(2,1)}, bf16[128,1024]{0,1:T(8,128)(2,1)S(1)}, u32[]{:S(2)}, u32[]{:S(2)}) collective-permute-start(bf16[128,1024]{0,1:T(8,128)(2,1)} %copy.1367), channel_id=1, source_target_pairs={{0,100},{4,104},{8,108},{12,112},{16,116},{20,120},{24,124},{28,12... | collective-permute-start | bytes 786440 | tf_op jit(solution)/shard_map/ppermute | solution.py:37
  342.2 65.0 %collective-permute-start.70 = (bf16[128,1024]{0,1:T(8,128)(2,1)}, bf16[128,1024]{0,1:T(8,128)(2,1)S(1)}, u32[]{:S(2)}, u32[]{:S(2)}) collective-permute-start(bf16[128,1024]{0,1:T(8,128)(2,1)} %copy.1367), channel_id=1, source_target_pairs={{0,96},{4,100},{8,104},{12,108},{16,112},{20,116},{24,120},{28,124... | collective-permute-start | bytes 786440 | tf_op jit(solution)/shard_map/ppermute | solution.py:37
  591.3 66.3 %collective-permute-start.53 = (bf16[128,1024]{1,0:T(8,128)(2,1)}, bf16[128,1024]{1,0:T(8,128)(2,1)S(1)}, u32[]{:S(2)}, u32[]{:S(2)}) collective-permute-start(bf16[128,1024]{1,0:T(8,128)(2,1)} %param.14), channel_id=1, source_target_pairs={{0,72},{4,76},{8,80},{12,84},{16,88},{20,92},{24,96},{28,100},{32,... | collective-permute-start | bytes 786440 | tf_op jit(solution)/shard_map/ppermute | solution.py:37
  675.6 69.4 %collective-permute-start.29 = (bf16[128,1024]{1,0:T(8,128)(2,1)}, bf16[128,1024]{1,0:T(8,128)(2,1)S(1)}, u32[]{:S(2)}, u32[]{:S(2)}) collective-permute-start(bf16[128,1024]{1,0:T(8,128)(2,1)} %param.14), channel_id=1, source_target_pairs={{0,40},{4,44},{8,48},{12,52},{16,56},{20,60},{24,64},{28,68},{32,7... | collective-permute-start | bytes 786440 | tf_op jit(solution)/shard_map/ppermute | solution.py:37
  679.3 69.4 %collective-permute-start.26 = (bf16[128,1024]{1,0:T(8,128)(2,1)}, bf16[128,1024]{1,0:T(8,128)(2,1)S(1)}, u32[]{:S(2)}, u32[]{:S(2)}) collective-permute-start(bf16[128,1024]{1,0:T(8,128)(2,1)} %param.14), channel_id=1, source_target_pairs={{0,36},{4,40},{8,44},{12,48},{16,52},{20,56},{24,60},{28,64},{32,6... | collective-permute-start | bytes 786440 | tf_op jit(solution)/shard_map/ppermute | solution.py:37
  683.0 69.4 %collective-permute-start.23 = (bf16[128,1024]{1,0:T(8,128)(2,1)}, bf16[128,1024]{1,0:T(8,128)(2,1)S(1)}, u32[]{:S(2)}, u32[]{:S(2)}) collective-permute-start(bf16[128,1024]{1,0:T(8,128)(2,1)} %param.14), channel_id=1, source_target_pairs={{0,32},{4,36},{8,40},{12,44},{16,48},{20,52},{24,56},{28,60},{32,6... | collective-permute-start | bytes 786440 | tf_op jit(solution)/shard_map/ppermute | solution.py:37
  754.3 67.0 %collective-permute-start.77 = (bf16[128,1024]{1,0:T(8,128)(2,1)}, bf16[128,1024]{1,0:T(8,128)(2,1)S(1)}, u32[]{:S(2)}, u32[]{:S(2)}) collective-permute-start(bf16[128,1024]{1,0:T(8,128)(2,1)} %param.14), channel_id=1, source_target_pairs={{0,104},{4,108},{8,112},{12,116},{16,120},{20,124},{24,128},{28,13... | collective-permute-start | bytes 786440 | tf_op jit(solution)/shard_map/ppermute | solution.py:37
  756.3 110.8 %collective-permute-start.74 = (bf16[128,1024]{1,0:T(8,128)(2,1)}, bf16[128,1024]{1,0:T(8,128)(2,1)S(1)}, u32[]{:S(2)}, u32[]{:S(2)}) collective-permute-start(bf16[128,1024]{1,0:T(8,128)(2,1)} %param.14), channel_id=1, source_target_pairs={{0,100},{4,104},{8,108},{12,112},{16,116},{20,120},{24,124},{28,12... | collective-permute-start | bytes 786440 | tf_op jit(solution)/shard_map/ppermute | solution.py:37
  798.8 69.5 %collective-permute-start.71 = (bf16[128,1024]{1,0:T(8,128)(2,1)}, bf16[128,1024]{1,0:T(8,128)(2,1)S(1)}, u32[]{:S(2)}, u32[]{:S(2)}) collective-permute-start(bf16[128,1024]{1,0:T(8,128)(2,1)} %param.14), channel_id=1, source_target_pairs={{0,96},{4,100},{8,104},{12,108},{16,112},{20,116},{24,120},{28,124... | collective-permute-start | bytes 786440 | tf_op jit(solution)/shard_map/ppermute | solution.py:37
  804.4 67.6 %collective-permute-start.68 = (bf16[128,1024]{1,0:T(8,128)(2,1)}, bf16[128,1024]{1,0:T(8,128)(2,1)S(1)}, u32[]{:S(2)}, u32[]{:S(2)}) collective-permute-start(bf16[128,1024]{1,0:T(8,128)(2,1)} %param.14), channel_id=1, source_target_pairs={{0,92},{4,96},{8,100},{12,104},{16,108},{20,112},{24,116},{28,120}... | collective-permute-start | bytes 786440 | tf_op jit(solution)/shard_map/ppermute | solution.py:37
  815.7 121.5 %collective-permute-start.94 = (bf16[128,1024]{0,1:T(8,128)(2,1)}, bf16[128,1024]{0,1:T(8,128)(2,1)}, u32[]{:S(2)}, u32[]{:S(2)}) collective-permute-start(bf16[128,1024]{0,1:T(8,128)(2,1)} %copy.1367), channel_id=1, source_target_pairs={{0,128},{4,132},{8,136},{12,140},{16,144},{20,148},{24,152},{28,15... | collective-permute-start | bytes 786440 | tf_op jit(solution)/shard_map/ppermute | solution.py:37
  821.3 110.3 %collective-permute-start.92 = (bf16[128,1024]{1,0:T(8,128)(2,1)}, bf16[128,1024]{1,0:T(8,128)(2,1)}, u32[]{:S(2)}, u32[]{:S(2)}) collective-permute-start(bf16[128,1024]{1,0:T(8,128)(2,1)} %param.14), channel_id=1, source_target_pairs={{0,124},{4,128},{8,132},{12,136},{16,140},{20,144},{24,148},{28,15... | collective-permute-start | bytes 786440 | tf_op jit(solution)/shard_map/ppermute | solution.py:37
  867.0 66.4 %collective-permute-start.95 = (bf16[128,1024]{1,0:T(8,128)(2,1)}, bf16[128,1024]{1,0:T(8,128)(2,1)}, u32[]{:S(2)}, u32[]{:S(2)}) collective-permute-start(bf16[128,1024]{1,0:T(8,128)(2,1)} %param.14), channel_id=1, source_target_pairs={{0,128},{4,132},{8,136},{12,140},{16,144},{20,148},{24,152},{28,15... | collective-permute-start | bytes 786440 | tf_op jit(solution)/shard_map/ppermute | solution.py:37
  868.4 66.8 %collective-permute-start.2 = (bf16[128,1024]{1,0:T(8,128)(2,1)}, bf16[128,1024]{1,0:T(8,128)(2,1)}, u32[]{:S(2)}, u32[]{:S(2)}) collective-permute-start(bf16[128,1024]{1,0:T(8,128)(2,1)} %param.14), channel_id=1, source_target_pairs={{0,4},{4,8},{8,12},{12,16},{16,20},{20,24},{24,28},{28,32},{32,36}... | collective-permute-start | bytes 786440 | tf_op jit(solution)/shard_map/ppermute | solution.py:37
  872.1 66.6 %collective-permute-start.91 = (bf16[128,1024]{0,1:T(8,128)(2,1)}, bf16[128,1024]{0,1:T(8,128)(2,1)}, u32[]{:S(2)}, u32[]{:S(2)}) collective-permute-start(bf16[128,1024]{0,1:T(8,128)(2,1)} %copy.1367), channel_id=1, source_target_pairs={{0,124},{4,128},{8,132},{12,136},{16,140},{20,144},{24,148},{28,15... | collective-permute-start | bytes 786440 | tf_op jit(solution)/shard_map/ppermute | solution.py:37
  (189 other events, 18692.5 us)
Sparse Core Ops, SparseCore 0:
  15.2 101.3 all-gather.4
where the time goes:
time: 1420 us; the launch traced here: 1400 us
  starting transfers between devices  368 us (26%)
  waiting for transfers between devices  288 us (20%)
  other arithmetic  192 us (14%)
  blocking collectives  158 us (11%)
  local copies, waits for them, and re-layouts  146 us (10%)
  loops' own time  120 us (8%)
  matrix products  114 us (8%)
  between operations  16.5 us (1%)
    ppermute x96, starting transfers between devices, from_behind(): lax.ppermute(value, axis, [(source, source + steps) for source in range(l...  368 us
    ppermute x96, waiting for transfers between devices, from_behind(): lax.ppermute(value, axis, [(source, source + steps) for source in range(l...  288 us
    another operation x1, loops' own time, entering_2(): return lax.fori_loop(0, peers, hop, start)  120 us
    unnamed x1, blocking collectives  107 us
    exp x64, other arithmetic, link_states(): jnp.exp(late_decay)[:, None, None] * early_state * joined[0] + late_state  80.9 us
    dynamic_slice x64, local copies, waits for them, and re-layouts, hop(): part[k].astype(own.dtype)  78.8 us
    select_n x64, other arithmetic, hop(): return jax.tree.map(lambda a, b: jnp.where(reached, a, b), new, before)  70.9 us
    ppermute x32, local copies, waits for them, and re-layouts, from_behind(): lax.ppermute(value, axis, [(source, source + steps) for source in range(l...  57.3 us
  transfers between devices with their start and end apart: 97, of which 34 were waited for; matrix products, arithmetic and copies ran while one was open for 14% of the time, Pallas kernels for 0%

commit v1 on v0

v1 whole, which is shorter than its diff:
```python
import math

import jax
import jax.numpy as jnp
from jax import lax
from jax.experimental import pallas as pl
from jax.experimental.pallas import tpu as pltpu
from jax.sharding import Mesh
from jax.sharding import PartitionSpec as P

HEAD_TOTAL = 32
DH = 128
TOK = 128
WINDOW = 4096
HEADS = 8
META = 16
KV_ROWS = 2 * DH + META
ROWS = KV_ROWS + TOK
PLANE = 2 * HEADS * TOK
SCALE = 1.0 / math.sqrt(DH)
EXP2_SCALE = SCALE / math.log(2.0)
LOW = -1e30
F32 = jnp.float32
BF16 = jnp.bfloat16
CHUNK = 2 * TOK


def dot(a, b):
    return jnp.dot(a, b, preferred_element_type=F32)


def split3(x):
    high = x.astype(BF16)
    rest = x - high.astype(F32)
    mid = rest.astype(BF16)
    low = (rest - mid.astype(F32)).astype(BF16)
    return high, mid, low


def joined(rows, at):
    part = rows.astype(F32)
    return part[at : at + 1] + part[at + 1 : at + 2] + part[at + 2 : at + 3]


def column(row):
    return jnp.transpose(jnp.broadcast_to(row, (TOK, TOK)))


def split_dot(a, state):
    high = state.astype(BF16)
    low = (state - high.astype(F32)).astype(BF16)
    return dot(a, high) + dot(a, low)


def prepare_kernel(table_ref, index_ref, q_ref, k_ref, v_ref, speed_ref, drop_ref, doc_ref, out_ref):
    lane = lax.broadcasted_iota(jnp.int32, (1, HEADS), 1)
    rate = jnp.zeros((1, HEADS), F32)
    for h in range(HEADS):
        rate = jnp.where(lane == h, table_ref[index_ref[h]], rate)
    log_decay = -rate * speed_ref[...] - drop_ref[...]
    upto = (
        lax.broadcasted_iota(jnp.int32, (TOK, TOK), 0)
        <= lax.broadcasted_iota(jnp.int32, (TOK, TOK), 1)
    ).astype(F32)
    cum = lax.dot_general(
        log_decay,
        upto,
        (((0,), (0,)), ((), ())),
        precision=lax.Precision.HIGHEST,
        preferred_element_type=F32,
    )
    high, mid, low = split3(cum)
    row = lax.broadcasted_iota(jnp.int32, (META, TOK), 0)
    doc = jnp.broadcast_to(doc_ref[...].astype(F32), (META, TOK))
    for h in range(HEADS):
        cols = pl.ds(h * DH, DH)
        out_ref[h, 0:DH, :] = jnp.transpose(k_ref[:, cols])
        out_ref[h, DH : 2 * DH, :] = v_ref[:, cols]
        meta = jnp.where(row == 3, doc, 0.0)
        for n, part in enumerate((high, mid, low)):
            meta = jnp.where(row == n, jnp.broadcast_to(part[h : h + 1].astype(F32), (META, TOK)), meta)
        out_ref[h, 2 * DH : KV_ROWS, :] = meta.astype(BF16)
        out_ref[h, KV_ROWS:ROWS, :] = q_ref[:, cols]


def linear_kernel(info_ref, own_ref, other_ref, init_ref, partial_ref, weight_ref, state_ref):
    x, core = info_ref[0], info_ref[2]
    first = core == 0
    state = jnp.where(x == 0, init_ref[0], 0.0)
    carry = jnp.where(x == 0, jnp.zeros((1, TOK), F32), jnp.full((1, TOK), -1.0, F32))
    prefix = jnp.zeros((1, TOK), F32)
    places = lax.broadcasted_iota(jnp.int32, (TOK, TOK), 0)
    causal = places >= lax.broadcasted_iota(jnp.int32, (TOK, TOK), 1)

    def read(swap, i):
        mine, theirs = own_ref[i, 0:KV_ROWS, :], other_ref[i]
        got = jnp.where(swap, theirs, mine)
        rows = got[2 * DH :]
        cum = joined(rows, 0)
        doc = rows.astype(F32)[3:4]
        overall = jnp.broadcast_to(cum[:, TOK - 1 :], (1, TOK))
        last = jnp.broadcast_to(doc[:, TOK - 1 :], (1, TOK))
        return got[:DH], got[DH : 2 * DH], cum, doc, overall, last

    def advance(state, carry, prefix, block):
        keys, values, cum, doc, overall, last = block
        factor = jnp.where(doc == last, jnp.exp(overall - cum), 0.0)
        scaled = (keys.astype(F32) * factor).astype(BF16)
        keep = jnp.where(last == carry, jnp.exp(overall), 0.0)
        return dot(scaled, values) + keep * state, last, prefix + overall

    for i in range(HEADS):
        even = read(jnp.logical_not(first), i)
        odd = read(first, i)
        middle = advance(state, carry, prefix, even)
        at_state = jnp.where(first, state, middle[0])
        at_carry = jnp.where(first, carry, middle[1])
        at_prefix = jnp.where(first, prefix, middle[2])
        keys, values, cum, doc, _, _ = [jnp.where(first, a, b) for a, b in zip(even, odd)]
        queries = own_ref[i, KV_ROWS:ROWS, :]
        cum_col, doc_col = column(cum), column(doc)
        inside = causal & (doc_col == doc)
        fading = jnp.exp(jnp.where(inside, cum_col - cum, 0.0))
        weights = jnp.where(inside, fading * dot(queries, keys) * SCALE, 0.0).astype(BF16)
        grown = jnp.exp(cum_col) * SCALE
        outside = jnp.where(doc_col == at_carry, grown * split_dot(queries, at_state), 0.0)
        partial_ref[i] = dot(weights, values) + outside
        weight_ref[i] = jnp.exp(cum_col + at_prefix) * SCALE
        state, carry, prefix = advance(*middle, odd)
    state_ref[0:DH, :] = state
    row = lax.broadcasted_iota(jnp.int32, (8, TOK), 0)
    state_ref[DH : DH + 8, :] = jnp.where(row == 0, prefix, carry)


def enter_kernel(info_ref, own_ref, partial_ref, weight_ref, near_ref, far_ref, linear_ref, square_ref):
    x = info_ref[0]
    near_decay, near_doc = near_ref[DH : DH + 1, :], near_ref[DH + 1 : DH + 2, :]
    far_doc = far_ref[DH + 1 : DH + 2, :]
    keep = jnp.where((far_doc == near_doc) & (x >= 2), jnp.exp(near_decay), 0.0)
    state = near_ref[0:DH, :] + keep * far_ref[0:DH, :]
    ones = jnp.ones((8, DH), F32)
    for i in range(HEADS):
        doc_col = column(own_ref[i, 2 * DH : KV_ROWS, :].astype(F32)[3:4])
        live = (doc_col == near_doc) & (x >= 1)
        product = split_dot(own_ref[i, KV_ROWS:ROWS, :], state)
        linear = partial_ref[i] + jnp.where(live, weight_ref[i] * product, 0.0)
        linear_ref[i] = linear.astype(BF16)
        square = lax.dot_general(
            ones,
            linear * linear,
            (((1,), (1,)), ((), ())),
            precision=lax.Precision.HIGHEST,
            preferred_element_type=F32,
        )
        square_ref[i : i + 1, :] = square[0:1]


def doc_rows(ref, i):
    return ref[i, 2 * DH : 2 * DH + META, :].astype(F32)[3:4]


def below(refs, number):
    total = jnp.zeros((1, TOK), F32)
    for ref in refs:
        for i in range(HEADS):
            total = total + jnp.where(doc_rows(ref, i) < number, 1.0, 0.0)
    return jnp.sum(total)


def first_places(doc_col, counts):
    place = jnp.zeros(doc_col.shape, F32)
    for number, count in counts:
        place = jnp.where(doc_col == number, count, place)
    return place


def soft_part(queries, score_ref, read, begin, end, mask):
    rows = queries.shape[0]

    def fill(n, top):
        keys, _ = read(n)
        scores = mask(dot(queries, keys), n)
        score_ref[n] = scores
        return jnp.maximum(top, jnp.maximum(scores[:, :TOK], scores[:, TOK:]))

    top = lax.fori_loop(begin, end, fill, jnp.full((rows, TOK), LOW, F32))
    top = jnp.max(top, axis=1, keepdims=True)

    def add(n, carry):
        total, output = carry
        _, values = read(n)
        weights = jnp.exp2((score_ref[n] - top) * EXP2_SCALE)
        total = total + weights[:, :TOK] + weights[:, TOK:]
        return total, output + dot(weights.astype(BF16), values)

    zero = jnp.zeros((rows, TOK), F32)
    total, output = lax.fori_loop(begin, end, add, (zero, zero))
    return top, jnp.sum(total, axis=1, keepdims=True), output


def both(a_ref, b_ref, n):
    keys = jnp.concatenate([a_ref[n, 0:DH, :], b_ref[n, 0:DH, :]], axis=1)
    values = jnp.concatenate([a_ref[n, DH : 2 * DH, :], b_ref[n, DH : 2 * DH, :]], axis=0)
    return keys, values


def key_place(core, rows):
    lane = lax.broadcasted_iota(jnp.int32, (rows, CHUNK), 1)
    own = lane + core * TOK
    return jnp.where(lane < TOK, own, lane - core * TOK)


def own_window_kernel(info_ref, own_ref, other_ref, top_ref, total_ref, output_ref, score_ref):
    core = info_ref[2]
    counts = [(float(d), below((own_ref, other_ref), float(d))) for d in range(4)]
    rows = 2 * TOK
    places = key_place(core, rows)
    row = lax.broadcasted_iota(jnp.int32, (rows, 1), 0)
    for tile in range(HEADS // 2):
        i = 2 * tile
        doc_col = jnp.concatenate([column(doc_rows(own_ref, i)), column(doc_rows(own_ref, i + 1))], axis=0)
        low = first_places(doc_col, counts).astype(jnp.int32)[:, :1]
        queries = jnp.concatenate([own_ref[i, KV_ROWS:ROWS, :], own_ref[i + 1, KV_ROWS:ROWS, :]], axis=0)
        at = (i + row // TOK) * CHUNK + core * TOK + row % TOK
        low = jnp.maximum(low, at - (WINDOW - 1))

        def mask(scores, n):
            key = places + n * CHUNK
            return jnp.where((key >= low) & (key <= at), scores, LOW)

        begin = jnp.min(low) // CHUNK
        top, total, output = soft_part(
            queries, score_ref, lambda n: both(own_ref, other_ref, n), begin, i + 2, mask
        )
        top_ref[pl.ds(tile * rows, rows), :] = jnp.broadcast_to(top, (rows, TOK))
        total_ref[pl.ds(tile * rows, rows), :] = jnp.broadcast_to(total, (rows, TOK))
        output_ref[pl.ds(tile * rows, rows), :] = output


def past_window_kernel(
    info_ref, own_ref, near_ref, near_other_ref, far_ref, far_other_ref, top_ref, total_ref,
    output_ref, linear_ref, square_ref, out_ref, near_score_ref, far_score_ref,
):
    x, core = info_ref[0], info_ref[2]
    rows = 2 * TOK
    whole = float(PLANE)
    counts = []
    for d in range(4):
        far = jnp.where(x >= 2, below((far_ref, far_other_ref), float(d)), whole)
        near = jnp.where(x >= 1, below((near_ref, near_other_ref), float(d)), whole)
        counts.append((float(d), far + near))
    places = key_place(core, rows)
    row = lax.broadcasted_iota(jnp.int32, (rows, 1), 0)
    meta_row = lax.broadcasted_iota(jnp.int32, (META, TOK), 0)
    for tile in range(HEADS // 2):
        i = 2 * tile
        doc_col = jnp.concatenate([column(doc_rows(own_ref, i)), column(doc_rows(own_ref, i + 1))], axis=0)
        low = first_places(doc_col, counts).astype(jnp.int32)[:, :1]
        queries = jnp.concatenate([own_ref[i, KV_ROWS:ROWS, :], own_ref[i + 1, KV_ROWS:ROWS, :]], axis=0)
        at = (i + row // TOK) * CHUNK + core * TOK + row % TOK + 2 * PLANE
        low = jnp.maximum(low, at - (WINDOW - 1))
        start = jnp.min(low)

        def mask_far(scores, n):
            return jnp.where(places + n * CHUNK >= low, scores, LOW)

        def mask_near(scores, n):
            return jnp.where(places + (n * CHUNK + PLANE) >= low, scores, LOW)

        far_begin = jnp.clip(start // CHUNK, 0, HEADS)
        near_begin = jnp.clip((start - PLANE) // CHUNK, 0, HEADS)
        span = pl.ds(tile * rows, rows)
        parts = [(top_ref[span, :1], total_ref[span, :1], output_ref[span, :])]
        parts.append(
            soft_part(queries, near_score_ref, lambda n: both(near_ref, near_other_ref, n), near_begin, HEADS, mask_near)
        )
        parts.append(
            soft_part(queries, far_score_ref, lambda n: both(far_ref, far_other_ref, n), far_begin, HEADS, mask_far)
        )
        top = jnp.maximum(parts[0][0], jnp.maximum(parts[1][0], parts[2][0]))
        total = jnp.zeros((rows, 1), F32)
        output = jnp.zeros((rows, DH), F32)
        for part_top, part_total, part_output in parts:
            shrink = jnp.exp2((part_top - top) * EXP2_SCALE)
            total = total + part_total * shrink
            output = output + part_output * shrink
        result = (output / total).astype(BF16)
        out_ref[i, 0:TOK, :] = result[:TOK]
        out_ref[i + 1, 0:TOK, :] = result[TOK:]
    for i in range(HEADS):
        out_ref[i, TOK : 2 * TOK, :] = linear_ref[i]
        meta = jnp.zeros((META, TOK), F32)
        for n, part in enumerate(split3(square_ref[i : i + 1, :])):
            meta = jnp.where(meta_row == n, jnp.broadcast_to(part.astype(F32), (META, TOK)), meta)
        out_ref[i, 2 * TOK :, :] = meta.astype(BF16)


def finish_kernel(got_ref, gain_ref, out_ref):
    total = jnp.zeros((1, TOK), F32)
    for h in range(HEADS):
        total = total + joined(got_ref[h, 2 * TOK :, :], 0)
    inverse = column(lax.rsqrt(total / (HEAD_TOTAL * DH) + 1e-06))
    for h in range(HEADS):
        cols = pl.ds(h * DH, DH)
        linear = got_ref[h, TOK : 2 * TOK, :].astype(F32)
        window = got_ref[h, 0:TOK, :].astype(F32)
        out_ref[:, cols] = (gain_ref[:, cols] * linear * inverse + window).astype(BF16)


VMEM = pl.BlockSpec(memory_space=pltpu.VMEM)
SMEM = pl.BlockSpec(memory_space=pltpu.SMEM)


def call(kernel, name, specs, shapes, scratch=(), flops=0, moved=0):
    many = isinstance(shapes, (list, tuple))
    return pl.pallas_call(
        kernel,
        name=name,
        out_shape=shapes,
        in_specs=specs,
        out_specs=[VMEM] * len(shapes) if many else VMEM,
        scratch_shapes=list(scratch),
        compiler_params=pltpu.CompilerParams(vmem_limit_bytes=40 * 2**20),
        cost_estimate=pl.CostEstimate(flops=flops, bytes_accessed=moved, transcendentals=0),
    )


def body(queries, keys, values, init_state, lin_gain, rate_table, rate_index, speed, drop, doc_id):
    x, z, core = (lax.axis_index(a).astype(jnp.int32) for a in ("x", "z", "core"))
    info = jnp.stack([x, z, core])
    shape = jax.ShapeDtypeStruct
    packed = call(
        prepare_kernel, "prepare", [SMEM, SMEM] + [VMEM] * 6, shape((HEADS, ROWS, TOK), BF16), moved=2 << 20
    )(rate_table, rate_index, queries, keys, values, speed, drop, doc_id[None, :])
    own = lax.all_to_all(packed, "z", 0, 0, tiled=True)
    sent = own[:, :KV_ROWS]
    pair = [(0, 1), (1, 0)]
    other = lax.ppermute(sent, "core", pair)
    near = lax.ppermute(sent, "x", [(0, 1), (1, 2), (2, 3)])
    far = lax.ppermute(sent, "x", [(0, 2), (1, 3)])

    tokens = HEADS * TOK
    init = lax.dynamic_slice_in_dim(init_state, z, 1, 0)
    partial, weight, state = call(
        linear_kernel,
        "linear",
        [SMEM] + [VMEM] * 3,
        [shape((HEADS, TOK, DH), F32), shape((HEADS, TOK, DH), F32), shape((DH + 8, DH), F32)],
        moved=4 << 20,
    )(info, own, other, init)
    near_state = lax.ppermute(state, "x", [(0, 1), (1, 2), (2, 3)])
    far_state = lax.ppermute(state, "x", [(0, 2), (1, 3)])
    own_top, own_total, own_output = call(
        own_window_kernel,
        "own_window",
        [SMEM] + [VMEM] * 2,
        [shape((tokens, TOK), F32), shape((tokens, TOK), F32), shape((tokens, DH), F32)],
        scratch=[pltpu.VMEM((HEADS, 2 * TOK, CHUNK), F32)],
        moved=6 << 20,
    )(info, own, other)
    linear, square = call(
        enter_kernel,
        "enter",
        [SMEM] + [VMEM] * 5,
        [shape((HEADS, TOK, DH), BF16), shape((HEADS, TOK), F32)],
        moved=3 << 20,
    )(info, own, partial, weight, near_state, far_state)
    square = square + lax.ppermute(square, "head", [(i, i ^ 1) for i in range(4)])
    square = square + lax.ppermute(square, "head", [(i, i ^ 2) for i in range(4)])
    near_other = lax.ppermute(near, "core", pair)
    far_other = lax.ppermute(far, "core", pair)
    mixed = call(
        past_window_kernel,
        "past_window",
        [SMEM] + [VMEM] * 10,
        shape((HEADS, 2 * TOK + META, DH), BF16),
        scratch=[pltpu.VMEM((HEADS, 2 * TOK, CHUNK), F32)] * 2,
        moved=12 << 20,
    )(info, own, near, near_other, far, far_other, own_top, own_total, own_output, linear, square)
    back = lax.all_to_all(mixed, "z", 0, 0, tiled=True)
    return call(finish_kernel, "finish", [VMEM] * 2, shape((TOK, HEADS * DH), BF16), moved=1 << 20)(
        back, lin_gain[None, :]
    )


def solution(mesh):
    split = Mesh(mesh.devices.reshape(4, 8, 2, 4), ("x", "z", "core", "head"))
    ctx = ("x", "z", "core")
    placed = (
        P(ctx, "head"),
        P(ctx, "head"),
        P(ctx, "head"),
        P("head", None, None),
        P("head"),
        P(),
        P("head"),
        P(ctx, "head"),
        P(ctx, "head"),
        P(ctx),
    )
    return jax.shard_map(body, mesh=split, in_specs=placed, out_specs=P(ctx, "head"), check_vma=False)
```

time: 1420 us -> 135 us (0.10); the launches traced: 1400 us -> 132 us
  starting transfers between devices: 368 us -> 12.5 us
  waiting for transfers between devices: 288 us -> 30.6 us
  other arithmetic: 192 us -> 0.08 us
  local copies, waits for them, and re-layouts: 146 us -> 5.35 us
  loops' own time: 120 us -> 0 us
  matrix products: 114 us -> 0 us
  blocking collectives: 158 us -> 52 us
  Pallas kernels: 0 us -> 31.3 us
  between operations: 16.5 us -> 0.16 us
    ppermute x96 -> x9, starting transfers between devices: 368 us -> 12.5 us  [the longest x1 3.2 us: body(): lax.ppermute(square, 'head', [(i, i ^ 2) for i in range(4)])]
    ppermute x96 -> x9, waiting for transfers between devices: 288 us -> 30.6 us  [the longest x1 13.2 us: body(): near = lax.ppermute(sent, 'x', [(0, 1), (1, 2), (2, 3)])]
    another operation x1 -> x0, loops' own time: 120 us -> none  [entering_2(): return lax.fori_loop(0, peers, hop, start)]
    dot_general x69 -> x0, matrix products: 114 us -> none  [the longest x33 55.5 us: absorb_block(): jnp.einsum('hts,shd->htd', weights.astype(jnp.bfloat16), value_block.resh...]
    unnamed x1 -> x0, blocking collectives: 107 us -> none
    exp x64 -> x0, other arithmetic: 80.9 us -> none  [link_states(): jnp.exp(late_decay)[:, None, None] * early_state * joined[0] + late_state]
    dynamic_slice x64 -> x1, local copies, waits for them, and re-layouts: 78.8 us -> 0.01 us  [body(): init = lax.dynamic_slice_in_dim(init_state, z, 1, 0)]
    select_n x65 -> x0, other arithmetic: 70.9 us -> none  [the longest x64 70.9 us: hop(): return jax.tree.map(lambda a, b: jnp.where(reached, a, b), new, before)]
  transfers between devices with their start and end apart: 97 -> 9, of which waited for: 34 -> 5; matrix products, arithmetic and copies ran while one was open for 14% -> 0% of each run, Pallas kernels for 0% -> 10%
where the time goes in v1:
time: 135 us; the launch traced here: 132 us
  blocking collectives  52 us (39%)
  Pallas kernels  31.3 us (23%)
  waiting for transfers between devices  30.6 us (23%)
  starting transfers between devices  12.5 us (9%)
  local copies, waits for them, and re-layouts  5.35 us (4%)
    all_to_all x1, blocking collectives, body(): own = lax.all_to_all(packed, 'z', 0, 0, tiled=True)  32.1 us
    all_to_all x1, blocking collectives, body(): back = lax.all_to_all(mixed, 'z', 0, 0, tiled=True)  19.9 us
    pallas_call x1, Pallas kernels, body(): call(past_window_kernel, 'past_window', [SMEM] + [VMEM] * 10, shape((HEAD...  16.9 us
    ppermute x1, waiting for transfers between devices, body(): near = lax.ppermute(sent, 'x', [(0, 1), (1, 2), (2, 3)])  13.2 us
    ppermute x1, waiting for transfers between devices, body(): far = lax.ppermute(sent, 'x', [(0, 2), (1, 3)])  8.71 us
    pallas_call x1, Pallas kernels, body(): call(own_window_kernel, 'own_window', [SMEM] + [VMEM] * 2, [shape((tokens...  8.42 us
    unnamed x20, local copies, waits for them, and re-layouts  4.49 us
    ppermute x1, waiting for transfers between devices, body(): far_state = lax.ppermute(state, 'x', [(0, 2), (1, 3)])  3.43 us
  transfers between devices with their start and end apart: 9, of which 5 were waited for; matrix products, arithmetic and copies ran while one was open for 0% of the time, Pallas kernels for 10%

profile of v1, /device:TPU:4, one launch (start us, length us, event | category | flops | bytes accessed | tf_op | source)
XLA Modules:
  0.0 132.0 jit_solution(13547742041111668359)
XLA Ops:
  0.0 0.9 copy.11.speed_ref
  1.7 0.9 copy-done.1
  2.6 0.9 copy-done.2
  3.6 0.9 copy-done.3
  4.5 0.8 prepare.1
  5.3 32.1 %all_to_all.10.own_ref = bf16[8,400,128]{2,1,0:T(8,128)(2,1)S(1)} all-to-all(bf16[8,400,128]{2,1,0:T(8,128)(2,1)S(1)} %prepare.1), channel_id=1, replica_groups=mesh['x'=4,'z'=8,'core'=2,'head'=4] {'z'}, dimensions={0} | all-to-all | bytes 1638400 | tf_op jit(solution)/shard_map/all_to_all | solution.py:335
  37.4 0.9 slice.4
  38.2 3.1 %collective-permute-start = (bf16[8,272,128]{2,1,0:T(8,128)(2,1)}, bf16[8,272,128]{2,1,0:T(8,128)(2,1)S(1)}, u32[]{:S(2)}, u32[]{:S(2)}) collective-permute-start(bf16[8,272,128]{2,1,0:T(8,128)(2,1)} %slice.4), channel_id=1, source_target_pairs={{0,64},{64,128},{128,192},{1,65},{65,129},{129,193},{2,66},{66,130... | collective-permute-start | bytes 1671176 | tf_op jit(solution)/shard_map/ppermute | solution.py:339
  41.3 1.3 collective-permute-start.2
  42.7 13.2 %collective-permute-done.near_ref = bf16[8,272,128]{2,1,0:T(8,128)(2,1)S(1)} collective-permute-done((bf16[8,272,128]{2,1,0:T(8,128)(2,1)}, bf16[8,272,128]{2,1,0:T(8,128)(2,1)S(1)}, u32[]{:S(2)}, u32[]{:S(2)}) %collective-permute-start) | collective-permute-done | bytes 557088 | tf_op jit(solution)/shard_map/ppermute | solution.py:339
  55.9 8.7 %collective-permute-done.2.far_ref = bf16[8,272,128]{2,1,0:T(8,128)(2,1)S(1)} collective-permute-done((bf16[8,272,128]{2,1,0:T(8,128)(2,1)}, bf16[8,272,128]{2,1,0:T(8,128)(2,1)S(1)}, u32[]{:S(2)}, u32[]{:S(2)}) %collective-permute-start.2) | collective-permute-done | bytes 557088 | tf_op jit(solution)/shard_map/ppermute | solution.py:340
  64.7 2.2 %linear.1 = (f32[8,128,128]{2,1,0:T(8,128)S(1)}, f32[8,128,128]{2,1,0:T(8,128)S(1)}, f32[136,128]{1,0:T(8,128)S(1)}) custom-call(s32[3]{0:T(128)S(1)} %pad_add_fusion.info_ref, bf16[8,400,128]{2,1,0:T(8,128)(2,1)S(1)} %all_to_all.10.own_ref, bf16[8,272,128]{2,1,0:T(8,128)(2,1)S(1)} %collective-permute-done.4.other_ref, ...), custom_call_target="tpu_custom_call" | custom-call | bytes 4194304 | tf_op jit(solution)/shard_map/linear/pallas_call | solution.py:344
  67.0 1.9 %collective-permute-start.5 = (f32[136,128]{1,0:T(8,128)S(1)}, f32[136,128]{1,0:T(8,128)S(1)}, u32[]{:S(2)}, u32[]{:S(2)}) collective-permute-start(f32[136,128]{1,0:T(8,128)S(1)} %get-tuple-element.18), channel_id=1, source_target_pairs={{0,64},{64,128},{128,192},{1,65},{65,129},{129,193},{2,66},{66,130... | collective-permute-start | bytes 208904 | tf_op jit(solution)/shard_map/ppermute | solution.py:351
  68.9 1.3 collective-permute-start.6
  70.2 3.3 %collective-permute-done.5.near_ref = f32[136,128]{1,0:T(8,128)S(1)} collective-permute-done((f32[136,128]{1,0:T(8,128)S(1)}, f32[136,128]{1,0:T(8,128)S(1)}, u32[]{:S(2)}, u32[]{:S(2)}) %collective-permute-start.5) | collective-permute-done | bytes 69664 | tf_op jit(solution)/shard_map/ppermute | solution.py:351
  73.4 3.4 %collective-permute-done.6.far_ref = f32[136,128]{1,0:T(8,128)S(1)} collective-permute-done((f32[136,128]{1,0:T(8,128)S(1)}, f32[136,128]{1,0:T(8,128)S(1)}, u32[]{:S(2)}, u32[]{:S(2)}) %collective-permute-start.6) | collective-permute-done | bytes 69664 | tf_op jit(solution)/shard_map/ppermute | solution.py:352
  76.9 2.1 %enter.1 = (bf16[8,128,128]{2,1,0:T(8,128)(2,1)S(1)}, f32[8,128]{1,0:T(8,128)S(1)}) custom-call(s32[3]{0:T(128)S(1)} %pad_add_fusion.info_ref, bf16[8,400,128]{2,1,0:T(8,128)(2,1)S(1)} %all_to_all.10.own_ref, f32[8,128,128]{2,1,0:T(8,128)S(1)} %get-tuple-element.16.partial_ref, f32[8,128,128]{2,1,0:T(8,128)S(1)} %get-tuple-element.17.weight_ref, ...), custom_call_target="tpu_custom_call" | custom-call | bytes 3145728 | tf_op jit(solution)/shard_map/enter/pallas_call | solution.py:361
  79.0 1.6 %collective-permute-start.7 = (f32[8,128]{1,0:T(8,128)S(1)}, f32[8,128]{1,0:T(8,128)S(1)}, u32[]{:S(2)}, u32[]{:S(2)}) collective-permute-start(f32[8,128]{1,0:T(8,128)S(1)} %get-tuple-element.20), channel_id=1, source_target_pairs={{0,1},{1,0},{2,3},{3,2},{4,5},{5,4},{6,7},{7,6},{8,9},{9,8},{10,11... | collective-permute-start | bytes 12296 | tf_op jit(solution)/shard_map/ppermute | solution.py:368
  80.6 2.0 %collective-permute-done.7 = f32[8,128]{1,0:T(8,128)S(1)} collective-permute-done((f32[8,128]{1,0:T(8,128)S(1)}, f32[8,128]{1,0:T(8,128)S(1)}, u32[]{:S(2)}, u32[]{:S(2)}) %collective-permute-start.7) | collective-permute-done | bytes 4128 | tf_op jit(solution)/shard_map/ppermute | solution.py:368
  82.6 3.2 %collective-permute-start.8 = (f32[8,128]{1,0:T(8,128)S(1)}, f32[8,128]{1,0:T(8,128)S(1)}, u32[]{:S(2)}, u32[]{:S(2)}) collective-permute-start(f32[8,128]{1,0:T(8,128)S(1)} %add.10), channel_id=1, source_target_pairs={{0,2},{1,3},{2,0},{3,1},{4,6},{5,7},{6,4},{7,5},{8,10},{9,11},{10,... | collective-permute-start | bytes 12296 | tf_op jit(solution)/shard_map/ppermute | solution.py:369
  85.8 8.4 %own_window.1 = (f32[1024,128]{1,0:T(8,128)S(1)}, f32[1024,128]{1,0:T(8,128)S(1)}, f32[1024,128]{1,0:T(8,128)S(1)}) custom-call(s32[3]{0:T(128)S(1)} %pad_add_fusion.info_ref, bf16[8,400,128]{2,1,0:T(8,128)(2,1)S(1)} %all_to_all.10.own_ref, bf16[8,272,128]{2,1,0:T(8,128)(2,1)S(1)} %collective-permute-done.4.other_ref), custom_call_target="tpu_custom_call" | custom-call | bytes 6291456 | tf_op jit(solution)/shard_map/own_window/pallas_call | solution.py:353
  94.3 16.9 %past_window.1 = bf16[8,272,128]{2,1,0:T(8,128)(2,1)S(1)} custom-call(s32[3]{0:T(128)S(1)} %pad_add_fusion.info_ref, bf16[8,400,128]{2,1,0:T(8,128)(2,1)S(1)} %all_to_all.10.own_ref, bf16[8,272,128]{2,1,0:T(8,128)(2,1)S(1)} %collective-permute-done.near_ref, bf16[8,272,128]{2,1,0:T(8,128)(2,1)} %collective-permute-done.1.near_other_ref, ...), custom_call_target="tpu_custom_call" | custom-call | bytes 12582912 | tf_op jit(solution)/shard_map/past_window/pallas_call | solution.py:372
  111.2 19.9 %all_to_all.11.got_ref = bf16[8,272,128]{2,1,0:T(8,128)(2,1)S(1)} all-to-all(bf16[8,272,128]{2,1,0:T(8,128)(2,1)S(1)} %past_window.1), channel_id=1, replica_groups=mesh['x'=4,'z'=8,'core'=2,'head'=4] {'z'}, dimensions={0} | all-to-all | bytes 1114112 | tf_op jit(solution)/shard_map/all_to_all | solution.py:380
  131.1 0.9 finish.1
  (27 shorter events, 1.0 us)
Async XLA Ops:
  0.0 64.7 %copy-start = (f32[8,128,128]{2,1,0:T(8,128)S(1)}, f32[8,128,128]{2,1,0:T(8,128)}, u32[]{:S(2)}) copy-start(f32[8,128,128]{2,1,0:T(8,128)} %param.13) | copy-start | bytes 1572868
  0.0 0.9 copy-start.8
  1.0 0.7 copy-start.5
  1.0 0.7 copy-start.6
  1.0 0.7 copy-start.7
  1.7 0.9 copy-start.1
  2.6 0.9 copy-start.2
  3.6 0.9 copy-start.3
  38.2 17.7 %collective-permute-start = (bf16[8,272,128]{2,1,0:T(8,128)(2,1)}, bf16[8,272,128]{2,1,0:T(8,128)(2,1)S(1)}, u32[]{:S(2)}, u32[]{:S(2)}) collective-permute-start(bf16[8,272,128]{2,1,0:T(8,128)(2,1)} %slice.4), channel_id=1, source_target_pairs={{0,64},{64,128},{128,192},{1,65},{65,129},{129,193},{2,66},{66,130... | collective-permute-start | bytes 1671176 | tf_op jit(solution)/shard_map/ppermute | solution.py:339
  41.3 23.3 %collective-permute-start.2 = (bf16[8,272,128]{2,1,0:T(8,128)(2,1)}, bf16[8,272,128]{2,1,0:T(8,128)(2,1)S(1)}, u32[]{:S(2)}, u32[]{:S(2)}) collective-permute-start(bf16[8,272,128]{2,1,0:T(8,128)(2,1)} %slice.4), channel_id=1, source_target_pairs={{0,128},{64,192},{1,129},{65,193},{2,130},{66,194},{3,131},{67,195... | collective-permute-start | bytes 1671176 | tf_op jit(solution)/shard_map/ppermute | solution.py:340
  42.6 22.1 %collective-permute-start.4 = (bf16[8,272,128]{2,1,0:T(8,128)(2,1)}, bf16[8,272,128]{2,1,0:T(8,128)(2,1)S(1)}, u32[]{:S(2)}, u32[]{:S(2)}) collective-permute-start(bf16[8,272,128]{2,1,0:T(8,128)(2,1)} %slice.4), channel_id=1, source_target_pairs={{0,4},{4,0},{1,5},{5,1},{2,6},{6,2},{3,7},{7,3},{8,12},{12,8},{9,1... | collective-permute-start | bytes 1671176 | tf_op jit(solution)/shard_map/ppermute | solution.py:338
  55.9 38.4 %collective-permute-start.1 = (bf16[8,272,128]{2,1,0:T(8,128)(2,1)S(1)}, bf16[8,272,128]{2,1,0:T(8,128)(2,1)}, u32[]{:S(2)}, u32[]{:S(2)}) collective-permute-start(bf16[8,272,128]{2,1,0:T(8,128)(2,1)S(1)} %collective-permute-done.near_ref), channel_id=1, source_target_pairs={{0,4},{4,0},{1,5},{5,1},{2,6},{6,2},{3,7},{7,3},{8,12},{12,8},{9,1... | collective-permute-start | bytes 1671176 | tf_op jit(solution)/shard_map/ppermute | solution.py:370
  64.6 29.7 %collective-permute-start.3 = (bf16[8,272,128]{2,1,0:T(8,128)(2,1)S(1)}, bf16[8,272,128]{2,1,0:T(8,128)(2,1)}, u32[]{:S(2)}, u32[]{:S(2)}) collective-permute-start(bf16[8,272,128]{2,1,0:T(8,128)(2,1)S(1)} %collective-permute-done.2.far_ref), channel_id=1, source_target_pairs={{0,4},{4,0},{1,5},{5,1},{2,6},{6,2},{3,7},{7,3},{8,12},{12,8},{9,1... | collective-permute-start | bytes 1671176 | tf_op jit(solution)/shard_map/ppermute | solution.py:371
  67.0 6.5 %collective-permute-start.5 = (f32[136,128]{1,0:T(8,128)S(1)}, f32[136,128]{1,0:T(8,128)S(1)}, u32[]{:S(2)}, u32[]{:S(2)}) collective-permute-start(f32[136,128]{1,0:T(8,128)S(1)} %get-tuple-element.18), channel_id=1, source_target_pairs={{0,64},{64,128},{128,192},{1,65},{65,129},{129,193},{2,66},{66,130... | collective-permute-start | bytes 208904 | tf_op jit(solution)/shard_map/ppermute | solution.py:351
  68.9 8.0 %collective-permute-start.6 = (f32[136,128]{1,0:T(8,128)S(1)}, f32[136,128]{1,0:T(8,128)S(1)}, u32[]{:S(2)}, u32[]{:S(2)}) collective-permute-start(f32[136,128]{1,0:T(8,128)S(1)} %get-tuple-element.18), channel_id=1, source_target_pairs={{0,128},{64,192},{1,129},{65,193},{2,130},{66,194},{3,131},{67,195... | collective-permute-start | bytes 208904 | tf_op jit(solution)/shard_map/ppermute | solution.py:352
  79.0 3.6 %collective-permute-start.7 = (f32[8,128]{1,0:T(8,128)S(1)}, f32[8,128]{1,0:T(8,128)S(1)}, u32[]{:S(2)}, u32[]{:S(2)}) collective-permute-start(f32[8,128]{1,0:T(8,128)S(1)} %get-tuple-element.20), channel_id=1, source_target_pairs={{0,1},{1,0},{2,3},{3,2},{4,5},{5,4},{6,7},{7,6},{8,9},{9,8},{10,11... | collective-permute-start | bytes 12296 | tf_op jit(solution)/shard_map/ppermute | solution.py:368
  82.6 11.6 %collective-permute-start.8 = (f32[8,128]{1,0:T(8,128)S(1)}, f32[8,128]{1,0:T(8,128)S(1)}, u32[]{:S(2)}, u32[]{:S(2)}) collective-permute-start(f32[8,128]{1,0:T(8,128)S(1)} %add.10), channel_id=1, source_target_pairs={{0,2},{1,3},{2,0},{3,1},{4,6},{5,7},{6,4},{7,5},{8,10},{9,11},{10,... | collective-permute-start | bytes 12296 | tf_op jit(solution)/shard_map/ppermute | solution.py:369
  111.2 19.9 %copy-start.4 = (f32[1024]{0:T(1024)S(1)}, f32[1024]{0:T(1024)}, u32[]{:S(2)}) copy-start(f32[1024]{0:T(1024)} %param.14) | copy-start | bytes 12292

commit v2 on v1

v2 whole, which is shorter than its diff:
```python
import math

import jax
import jax.numpy as jnp
from jax import lax
from jax.experimental import pallas as pl
from jax.experimental.pallas import tpu as pltpu
from jax.sharding import Mesh
from jax.sharding import PartitionSpec as P

HEAD_TOTAL = 32
DH = 128
TOK = 128
WINDOW = 4096
HEADS = 8
META = 16
KV_ROWS = 2 * DH + META
ROWS = KV_ROWS + TOK
PLANE = 2 * HEADS * TOK
SCALE = 1.0 / math.sqrt(DH)
EXP2_SCALE = SCALE / math.log(2.0)
LOW = -1e30
F32 = jnp.float32
BF16 = jnp.bfloat16
CHUNK = 2 * TOK
TILES = HEADS // 2
META_AT = DH
VALUE_AT = DH + META


def dot(a, b):
    return jnp.dot(a, b, preferred_element_type=F32)


def split3(x):
    high = x.astype(BF16)
    rest = x - high.astype(F32)
    mid = rest.astype(BF16)
    low = (rest - mid.astype(F32)).astype(BF16)
    return high, mid, low


def joined(rows, at):
    part = rows.astype(F32)
    return part[at : at + 1] + part[at + 1 : at + 2] + part[at + 2 : at + 3]


def column(row):
    return jnp.transpose(jnp.broadcast_to(row, (TOK, TOK)))


def split_dot(a, state):
    high = state.astype(BF16)
    low = (state - high.astype(F32)).astype(BF16)
    return dot(a, high) + dot(a, low)


def prepare_kernel(
    table_ref, index_ref, q_hbm, k_hbm, v_hbm, speed_ref, drop_ref, doc_ref, out_ref, q_ref, k_ref, v_ref, sems
):
    copies = [
        pltpu.make_async_copy(src, dst, sems.at[n])
        for n, (src, dst) in enumerate(((k_hbm, k_ref), (v_hbm, v_ref), (q_hbm, q_ref)))
    ]
    for copy in copies:
        copy.start()
    head = lax.broadcasted_iota(jnp.int32, (HEADS, TOK), 0)
    rate = jnp.zeros((HEADS, TOK), F32)
    for h in range(HEADS):
        rate = jnp.where(head == h, table_ref[index_ref[h]], rate)
    log_decay = -rate * speed_ref[...] - drop_ref[...]
    upto = (
        lax.broadcasted_iota(jnp.int32, (TOK, TOK), 0)
        <= lax.broadcasted_iota(jnp.int32, (TOK, TOK), 1)
    ).astype(F32)
    cum = jnp.dot(log_decay, upto, precision=lax.Precision.HIGHEST, preferred_element_type=F32)
    parts = [part.astype(F32) for part in split3(cum)]
    row = lax.broadcasted_iota(jnp.int32, (META, TOK), 0)
    doc = jnp.broadcast_to(doc_ref[...].astype(F32), (META, TOK))
    bias = jnp.where(doc == (row - 4).astype(F32), 0.0, LOW)
    shared = jnp.where(row == 3, doc, jnp.where((row >= 4) & (row < 8), bias, 0.0))
    for h in range(HEADS):
        meta = shared
        for n, part in enumerate(parts):
            meta = jnp.where(row == n, jnp.broadcast_to(part[h : h + 1], (META, TOK)), meta)
        out_ref[h, META_AT:VALUE_AT, :] = meta.astype(BF16)
    copies[0].wait()
    for h in range(HEADS):
        out_ref[h, 0:DH, :] = jnp.transpose(k_ref[:, pl.ds(h * DH, DH)])
    copies[1].wait()
    copies[2].wait()
    for h in range(HEADS):
        cols = pl.ds(h * DH, DH)
        out_ref[h, VALUE_AT:KV_ROWS, :] = v_ref[:, cols]
        out_ref[h, KV_ROWS:ROWS, :] = q_ref[:, cols]


def meta_rows(ref, i):
    return ref[i, META_AT:VALUE_AT, :].astype(F32)


def linear_kernel(info_ref, own_ref, other_ref, init_ref, partial_ref, weight_ref, state_ref, mark_ref):
    x, core = info_ref[0], info_ref[2]
    first = core == 0
    state = jnp.where(x == 0, init_ref[0], 0.0)
    carry = jnp.where(x == 0, jnp.zeros((1, TOK), F32), jnp.full((1, TOK), -1.0, F32))
    prefix = jnp.zeros((1, TOK), F32)
    places = lax.broadcasted_iota(jnp.int32, (TOK, TOK), 0)
    lanes = lax.broadcasted_iota(jnp.int32, (TOK, TOK), 1)
    causal = places >= lanes
    marked = (lanes >= 4) & (lanes < 8)
    number = (lanes - 4).astype(F32)
    start_doc = None

    def read(swap, i):
        mine, theirs = own_ref[i, 0:KV_ROWS, :], other_ref[i]
        got = jnp.where(swap, theirs, mine)
        rows = got[META_AT:VALUE_AT].astype(F32)
        cum, doc = rows[0:1] + rows[1:2] + rows[2:3], rows[3:4]
        overall = jnp.broadcast_to(cum[:, TOK - 1 :], (1, TOK))
        last = jnp.broadcast_to(doc[:, TOK - 1 :], (1, TOK))
        return got[:DH], got[VALUE_AT:], cum, doc, overall, last

    def advance(state, carry, prefix, block):
        keys, values, cum, doc, overall, last = block
        factor = jnp.where(doc == last, jnp.exp(overall - cum), 0.0)
        scaled = (keys.astype(F32) * factor).astype(BF16)
        keep = jnp.where(last == carry, jnp.exp(overall), 0.0)
        return dot(scaled, values) + keep * state, last, prefix + overall

    for i in range(HEADS):
        even = read(jnp.logical_not(first), i)
        odd = read(first, i)
        if start_doc is None:
            start_doc = jnp.broadcast_to(even[3][:, :1], (1, TOK))
        middle = advance(state, carry, prefix, even)
        at_state = jnp.where(first, state, middle[0])
        at_carry = jnp.where(first, carry, middle[1])
        at_prefix = jnp.where(first, prefix, middle[2])
        keys, values, cum, doc, _, _ = [jnp.where(first, a, b) for a, b in zip(even, odd)]
        queries = own_ref[i, KV_ROWS:ROWS, :]
        cum_col, doc_col = column(cum), column(doc)
        inside = causal & (doc_col == doc)
        fading = jnp.exp(jnp.where(inside, cum_col - cum, 0.0))
        weights = jnp.where(inside, fading * dot(queries, keys) * SCALE, 0.0).astype(BF16)
        grown = jnp.exp(cum_col) * SCALE
        outside = jnp.where(doc_col == at_carry, grown * split_dot(queries, at_state), 0.0)
        partial_ref[i] = dot(weights, values) + outside
        weight_ref[i] = jnp.where(doc_col == start_doc, jnp.exp(cum_col + at_prefix) * SCALE, 0.0)
        mark_ref[i] = jnp.where(marked & (doc_col == number), 1.0, 0.0).astype(BF16)
        state, carry, prefix = advance(*middle, odd)
    state_ref[0:DH, :] = state
    row = lax.broadcasted_iota(jnp.int32, (8, TOK), 0)
    state_ref[DH : DH + 8, :] = jnp.where(row == 0, prefix, jnp.where(row == 1, carry, start_doc))


def enter_kernel(
    info_ref, own_ref, partial_ref, weight_ref, state_ref, near_ref, far_ref, linear_ref, square_ref, need_ref
):
    x = info_ref[0]
    near_decay, near_doc = near_ref[DH : DH + 1, :], near_ref[DH + 1 : DH + 2, :]
    far_doc, start_doc = far_ref[DH + 1 : DH + 2, :], state_ref[DH + 2 : DH + 3, :]
    keep = jnp.where((far_doc == near_doc) & (x >= 2), jnp.exp(near_decay), 0.0)
    state = near_ref[0:DH, :] + keep * far_ref[0:DH, :]
    state = jnp.where((start_doc == near_doc) & (x >= 1), state, 0.0)
    ones = jnp.ones((8, DH), F32)
    for i in range(HEADS):
        linear = partial_ref[i] + weight_ref[i] * split_dot(own_ref[i, KV_ROWS:ROWS, :], state)
        linear_ref[i] = linear.astype(BF16)
        square = lax.dot_general(
            ones,
            linear * linear,
            (((1,), (1,)), ((), ())),
            precision=lax.Precision.HIGHEST,
            preferred_element_type=F32,
        )
        square_ref[i : i + 1, :] = square[0:1]
    for tile in range(TILES):
        tile_doc = jnp.broadcast_to(meta_rows(own_ref, 2 * tile)[3:4, :1], (1, TOK))
        need_ref[2 * tile] = jnp.where(x >= 1, jnp.max(jnp.where(tile_doc == near_doc, 1, 0)), 0)
        need_ref[2 * tile + 1] = jnp.where(x >= 2, jnp.max(jnp.where(tile_doc == far_doc, 1, 0)), 0)


def marked_queries(own_ref, mark_ref, tile):
    i = 2 * tile
    queries = jnp.concatenate([own_ref[i, KV_ROWS:ROWS, :], own_ref[i + 1, KV_ROWS:ROWS, :]], axis=0)
    marks = jnp.concatenate([mark_ref[i], mark_ref[i + 1]], axis=0)[:, :META]
    return jnp.concatenate([queries, marks], axis=1)


def absorb(queries, ref, pieces, diagonal, old):
    scores = []
    top = None
    for m in pieces:
        keys = jnp.concatenate([ref[2 * m, 0:VALUE_AT, :], ref[2 * m + 1, 0:VALUE_AT, :]], axis=1)
        score = dot(queries, keys)
        if m == diagonal[0]:
            score = jnp.where(diagonal[1], score, LOW)
        scores.append(score)
        most = jnp.maximum(score[:, :TOK], score[:, TOK:])
        top = most if top is None else jnp.maximum(top, most)
    top = jnp.max(top, axis=1, keepdims=True)
    if old is not None:
        top = jnp.maximum(top, old[0])
    base = top * EXP2_SCALE
    sums, output = None, None
    for m, score in zip(pieces, scores):
        weights = jnp.exp2(score * EXP2_SCALE - base)
        part = weights[:, :TOK] + weights[:, TOK:]
        sums = part if sums is None else sums + part
        values = jnp.concatenate([ref[2 * m, VALUE_AT:KV_ROWS, :], ref[2 * m + 1, VALUE_AT:KV_ROWS, :]], axis=0)
        product = dot(weights.astype(BF16), values)
        output = product if output is None else output + product
    total = jnp.sum(sums, axis=1, keepdims=True)
    if old is not None:
        shrink = jnp.exp2(old[0] * EXP2_SCALE - base)
        total = total + old[1] * shrink
        output = output + old[2] * shrink
    return top, total, output


def tile_places(core, own):
    rows = lax.broadcasted_iota(jnp.int32, (CHUNK, CHUNK), 0)
    lanes = lax.broadcasted_iota(jnp.int32, (CHUNK, CHUNK), 1)
    key_core = core if own else 1 - core
    at = jnp.where(rows < TOK, rows, rows + TOK) + core * TOK
    key = jnp.where(lanes < TOK, lanes, lanes + TOK) + key_core * TOK
    return at, key


def span_of(tile):
    return pl.ds(tile * CHUNK, CHUNK)


def load_part(refs, tile):
    top_ref, total_ref, output_ref = refs
    span = span_of(tile)
    return top_ref[span, :1], total_ref[span, :1], output_ref[span, :]


def store_part(refs, tile, part):
    span = span_of(tile)
    for ref, value in zip(refs, part):
        ref[span, :] = jnp.broadcast_to(value, (CHUNK, TOK))


def own_window_kernel(info_ref, own_ref, other_ref, mark_ref, *refs):
    core = info_ref[2]
    masks = []
    for own in (True, False):
        at, key = tile_places(core, own)
        masks.append(key <= at)
    for tile in range(TILES):
        queries = marked_queries(own_ref, mark_ref, tile)
        part = absorb(queries, own_ref, range(tile + 1), (tile, masks[0]), None)
        part = absorb(queries, other_ref, range(tile + 1), (tile, masks[1]), part)
        store_part(refs, tile, part)


def past_blocks(core, own, own_ref, mark_ref, need_ref, near_ref, far_ref, refs):
    at, key = tile_places(core, own)
    mask = key > at
    for tile in range(TILES):

        @pl.when(need_ref[2 * tile] == 1)
        def _(tile=tile):
            queries = marked_queries(own_ref, mark_ref, tile)
            store_part(refs, tile, absorb(queries, near_ref, range(TILES), (None, None), load_part(refs, tile)))

        @pl.when(need_ref[2 * tile + 1] == 1)
        def _(tile=tile):
            queries = marked_queries(own_ref, mark_ref, tile)
            store_part(refs, tile, absorb(queries, far_ref, range(tile, TILES), (tile, mask), load_part(refs, tile)))


def past_own_kernel(info_ref, need_ref, own_ref, mark_ref, near_ref, far_ref, a_ref, b_ref, c_ref, *refs):
    for before, after in zip((a_ref, b_ref, c_ref), refs):
        after[...] = before[...]
    past_blocks(info_ref[2], True, own_ref, mark_ref, need_ref, near_ref, far_ref, refs)


def past_other_kernel(
    info_ref, need_ref, own_ref, mark_ref, near_ref, far_ref, a_ref, b_ref, c_ref, linear_ref, square_ref, out_ref, *refs
):
    for before, after in zip((a_ref, b_ref, c_ref), refs):
        after[...] = before[...]
    row = lax.broadcasted_iota(jnp.int32, (META, TOK), 0)
    for i in range(HEADS):
        out_ref[i, TOK : 2 * TOK, :] = linear_ref[i]
        meta = jnp.zeros((META, TOK), F32)
        for n, part in enumerate(split3(square_ref[i : i + 1, :])):
            meta = jnp.where(row == n, jnp.broadcast_to(part.astype(F32), (META, TOK)), meta)
        out_ref[i, 2 * TOK :, :] = meta.astype(BF16)
    past_blocks(info_ref[2], False, own_ref, mark_ref, need_ref, near_ref, far_ref, refs)
    _, total_ref, output_ref = refs
    for i in range(HEADS):
        span = pl.ds(i * TOK, TOK)
        out_ref[i, 0:TOK, :] = (output_ref[span, :] / total_ref[span, :]).astype(BF16)


def finish_kernel(got_ref, gain_ref, out_ref):
    total = jnp.zeros((1, TOK), F32)
    for h in range(HEADS):
        total = total + joined(got_ref[h, 2 * TOK :, :], 0)
    inverse = column(lax.rsqrt(total / (HEAD_TOTAL * DH) + 1e-06))
    for h in range(HEADS):
        cols = pl.ds(h * DH, DH)
        linear = got_ref[h, TOK : 2 * TOK, :].astype(F32)
        window = got_ref[h, 0:TOK, :].astype(F32)
        out_ref[:, cols] = (gain_ref[:, cols] * linear * inverse + window).astype(BF16)


VMEM = pl.BlockSpec(memory_space=pltpu.VMEM)
SMEM = pl.BlockSpec(memory_space=pltpu.SMEM)
HBM = pl.BlockSpec(memory_space=pltpu.HBM)


def call(kernel, name, specs, shapes, scratch=(), flops=0, moved=0, outs=None):
    many = isinstance(shapes, (list, tuple))
    return pl.pallas_call(
        kernel,
        name=name,
        out_shape=shapes,
        in_specs=specs,
        out_specs=outs or ([VMEM] * len(shapes) if many else VMEM),
        scratch_shapes=list(scratch),
        compiler_params=pltpu.CompilerParams(vmem_limit_bytes=32 * 2**20),
        cost_estimate=pl.CostEstimate(flops=flops, bytes_accessed=moved, transcendentals=0),
    )


def body(queries, keys, values, init_state, lin_gain, rate_table, rate_index, speed, drop, doc_id):
    x, z, core = (lax.axis_index(a).astype(jnp.int32) for a in ("x", "z", "core"))
    info = jnp.stack([x, z, core])
    shape = jax.ShapeDtypeStruct
    packed = call(
        prepare_kernel,
        "prepare",
        [SMEM, SMEM, HBM, HBM, HBM, VMEM, VMEM, VMEM],
        shape((HEADS, ROWS, TOK), BF16),
        scratch=[pltpu.VMEM((TOK, HEADS * DH), BF16)] * 3 + [pltpu.SemaphoreType.DMA((3,))],
        moved=2 << 20,
    )(rate_table, rate_index, queries, keys, values, speed.T, drop.T, doc_id[None, :])
    own = lax.all_to_all(packed, "z", 0, 0, tiled=True)
    sent = own[:, :KV_ROWS]
    pair = [(0, 1), (1, 0)]
    near = lax.ppermute(sent, "x", [(0, 1), (1, 2), (2, 3)])
    far = lax.ppermute(sent, "x", [(0, 2), (1, 3)])
    other = lax.ppermute(sent, "core", pair)

    tokens = HEADS * TOK
    part_shapes = [shape((tokens, TOK), F32), shape((tokens, TOK), F32), shape((tokens, DH), F32)]
    init = lax.dynamic_slice_in_dim(init_state, z, 1, 0)
    partial, weight, state, mark = call(
        linear_kernel,
        "linear",
        [SMEM] + [VMEM] * 3,
        [
            shape((HEADS, TOK, DH), F32),
            shape((HEADS, TOK, DH), F32),
            shape((DH + 8, DH), F32),
            shape((HEADS, TOK, TOK), BF16),
        ],
        flops=2_000_000_000,
        moved=4 << 20,
    )(info, own, other, init)
    near_state = lax.ppermute(state, "x", [(0, 1), (1, 2), (2, 3)])
    far_state = lax.ppermute(state, "x", [(0, 2), (1, 3)])
    own_part = call(
        own_window_kernel, "own_window", [SMEM] + [VMEM] * 3, part_shapes, flops=5_000_000_000, moved=6 << 20
    )(info, own, other, mark)
    linear, square, need = call(
        enter_kernel,
        "enter",
        [SMEM] + [VMEM] * 6,
        [shape((HEADS, TOK, DH), BF16), shape((HEADS, TOK), F32), shape((2 * TILES,), jnp.int32)],
        outs=[VMEM, VMEM, SMEM],
        flops=1_000_000_000,
        moved=3 << 20,
    )(info, own, partial, weight, state, near_state, far_state)
    square = square + lax.ppermute(square, "head", [(i, i ^ 1) for i in range(4)])
    square = square + lax.ppermute(square, "head", [(i, i ^ 2) for i in range(4)])
    near, far, square, own_part = lax.optimization_barrier((near, far, square, own_part))
    near_other = lax.ppermute(near, "core", pair)
    far_other = lax.ppermute(far, "core", pair)
    own_part = call(
        past_own_kernel,
        "past_own",
        [SMEM] * 2 + [VMEM] * 7,
        part_shapes,
        flops=4_000_000_000,
        moved=8 << 20,
    )(info, need, own, mark, near, far, *own_part)
    mixed = call(
        past_other_kernel,
        "past_other",
        [SMEM] * 2 + [VMEM] * 9,
        shape((HEADS, 2 * TOK + META, DH), BF16),
        scratch=[pltpu.VMEM((tokens, TOK), F32)] * 3,
        flops=4_000_000_000,
        moved=8 << 20,
    )(info, need, own, mark, near_other, far_other, *own_part, linear, square)
    back = lax.all_to_all(mixed, "z", 0, 0, tiled=True)
    return call(finish_kernel, "finish", [VMEM] * 2, shape((TOK, HEADS * DH), BF16), moved=1 << 20)(
        back, lin_gain[None, :]
    )


def solution(mesh):
    split = Mesh(mesh.devices.reshape(4, 8, 2, 4), ("x", "z", "core", "head"))
    ctx = ("x", "z", "core")
    placed = (
        P(ctx, "head"),
        P(ctx, "head"),
        P(ctx, "head"),
        P("head", None, None),
        P("head"),
        P(),
        P("head"),
        P(ctx, "head"),
        P(ctx, "head"),
        P(ctx),
    )
    return jax.shard_map(body, mesh=split, in_specs=placed, out_specs=P(ctx, "head"), check_vma=False)
```

time: 135 us -> 109 us (0.81); the launches traced: 132 us -> 108 us
  waiting for transfers between devices: 30.6 us -> 17.1 us
  Pallas kernels: 31.3 us -> 20.5 us
    pallas_call x4 -> x5, Pallas kernels: 28.2 us -> 17.4 us  [the longest x1 5.04 us: body(): call(past_own_kernel, 'past_own', [SMEM] * 2 + [VMEM] * 7, part_shapes, f...]
    ppermute x1, waiting for transfers between devices: 8.71 us -> 0.89 us  [body(): far = lax.ppermute(sent, 'x', [(0, 2), (1, 3)])]
    ppermute x1, waiting for transfers between devices: 3.43 us -> 0.12 us  [body(): far_state = lax.ppermute(state, 'x', [(0, 2), (1, 3)])]
    ppermute x1, waiting for transfers between devices: 13.2 us -> 10.8 us  [body(): near = lax.ppermute(sent, 'x', [(0, 1), (1, 2), (2, 3)])]
    ppermute x1, waiting for transfers between devices: 0.01 us -> 1.84 us  [body(): other = lax.ppermute(sent, 'core', pair)]
    ppermute x1, waiting for transfers between devices: 3.26 us -> 1.44 us  [body(): near_state = lax.ppermute(state, 'x', [(0, 1), (1, 2), (2, 3)])]
  transfers between devices with their start and end apart: 9 -> 9, of which waited for: 5 -> 6; matrix products, arithmetic and copies ran while one was open for 0% -> 0% of each run, Pallas kernels for 10% -> 10%
where the time goes in v2:
time: 109 us; the launch traced here: 108 us
  blocking collectives  53.1 us (49%)
  Pallas kernels  20.5 us (19%)
  waiting for transfers between devices  17.1 us (16%)
  starting transfers between devices  13.1 us (12%)
  local copies, waits for them, and re-layouts  4.33 us (4%)
    all_to_all x1, blocking collectives, body(): own = lax.all_to_all(packed, 'z', 0, 0, tiled=True)  32.1 us
    all_to_all x1, blocking collectives, body(): back = lax.all_to_all(mixed, 'z', 0, 0, tiled=True)  21.1 us
    ppermute x1, waiting for transfers between devices, body(): near = lax.ppermute(sent, 'x', [(0, 1), (1, 2), (2, 3)])  10.8 us
    pallas_call x1, Pallas kernels, body(): call(past_own_kernel, 'past_own', [SMEM] * 2 + [VMEM] * 7, part_shapes, f...  5.04 us
    pallas_call x1, Pallas kernels, body(): call(past_other_kernel, 'past_other', [SMEM] * 2 + [VMEM] * 9, shape((HEA...  5 us
    unnamed x20, local copies, waits for them, and re-layouts  4.28 us
    pallas_call x1, Pallas kernels, body(): call(own_window_kernel, 'own_window', [SMEM] + [VMEM] * 3, part_shapes, f...  3.73 us
    ppermute x1, starting transfers between devices, body(): lax.ppermute(square, 'head', [(i, i ^ 2) for i in range(4)])  3.2 us
  transfers between devices with their start and end apart: 9, of which 6 were waited for; matrix products, arithmetic and copies ran while one was open for 0% of the time, Pallas kernels for 10%

profile of v2, /device:TPU:4, one launch (start us, length us, event | category | flops | bytes accessed | tf_op | source)
XLA Modules:
  0.0 108.4 jit_solution(1976684269898313852)
XLA Ops:
  0.0 0.7 copy-done.4
  0.8 0.9 copy-done.1
  1.7 0.9 copy-done.2
  2.7 0.9 copy-done.3
  4.3 1.0 prepare.1
  5.3 32.1 %all_to_all.10.own_ref = bf16[8,400,128]{2,1,0:T(8,128)(2,1)S(1)} all-to-all(bf16[8,400,128]{2,1,0:T(8,128)(2,1)S(1)} %prepare.1), channel_id=1, replica_groups=mesh['x'=4,'z'=8,'core'=2,'head'=4] {'z'}, dimensions={0} | all-to-all | bytes 1638400 | tf_op jit(solution)/shard_map/all_to_all | solution.py:344
  37.7 1.8 %collective-permute-done.other_ref = bf16[8,272,128]{2,1,0:T(8,128)(2,1)S(1)} collective-permute-done((bf16[8,272,128]{2,1,0:T(8,128)(2,1)S(1)}, bf16[8,272,128]{2,1,0:T(8,128)(2,1)S(1)}, u32[]{:S(2)}, u32[]{:S(2)}) %collective-permute-start) | collective-permute-done | bytes 557088 | tf_op jit(solution)/shard_map/ppermute | solution.py:349
  39.5 2.2 %linear.1 = (f32[8,128,128]{2,1,0:T(8,128)S(1)}, f32[8,128,128]{2,1,0:T(8,128)S(1)}, f32[136,128]{1,0:T(8,128)S(1)}, bf16[8,128,128]{2,1,0:T(8,128)(2,1)S(1)}) custom-call(s32[3]{0:T(128)S(1)} %pad_add_fusion.info_ref, bf16[8,400,128]{2,1,0:T(8,128)(2,1)S(1)} %all_to_all.10.own_ref, bf16[8,272,128]{2,1,0:T(8,128)(2,1)S(1)} %collective-permute-done.other_ref, ...), custom_call_target="tpu_custom_call" | custom-call | flops 2000000000 | bytes 4194304 | tf_op jit(solution)/shard_map/linear/pallas_call | solution.py:354
  41.7 1.3 %collective-permute-start.2 = (f32[136,128]{1,0:T(8,128)S(1)}, f32[136,128]{1,0:T(8,128)S(1)}, u32[]{:S(2)}, u32[]{:S(2)}) collective-permute-start(f32[136,128]{1,0:T(8,128)S(1)} %get-tuple-element.26.state_ref), channel_id=1, source_target_pairs={{0,128},{64,192},{1,129},{65,193},{2,130},{66,194},{3,131},{67,195... | collective-permute-start | bytes 208904 | tf_op jit(solution)/shard_map/ppermute | solution.py:368
  43.0 3.1 %collective-permute-start.1 = (f32[136,128]{1,0:T(8,128)S(1)}, f32[136,128]{1,0:T(8,128)S(1)}, u32[]{:S(2)}, u32[]{:S(2)}) collective-permute-start(f32[136,128]{1,0:T(8,128)S(1)} %get-tuple-element.26.state_ref), channel_id=1, source_target_pairs={{0,64},{64,128},{128,192},{1,65},{65,129},{129,193},{2,66},{66,130... | collective-permute-start | bytes 208904 | tf_op jit(solution)/shard_map/ppermute | solution.py:367
  46.2 1.3 %collective-permute-start.4 = (bf16[8,272,128]{2,1,0:T(8,128)(2,1)S(1)}, bf16[8,272,128]{2,1,0:T(8,128)(2,1)S(1)}, u32[]{:S(2)}, u32[]{:S(2)}) collective-permute-start(bf16[8,272,128]{2,1,0:T(8,128)(2,1)S(1)} %slice.4), channel_id=1, source_target_pairs={{0,128},{64,192},{1,129},{65,193},{2,130},{66,194},{3,131},{67,195... | collective-permute-start | bytes 1671176 | tf_op jit(solution)/shard_map/ppermute | solution.py:348
  47.5 1.9 %collective-permute-start.3 = (bf16[8,272,128]{2,1,0:T(8,128)(2,1)S(1)}, bf16[8,272,128]{2,1,0:T(8,128)(2,1)S(1)}, u32[]{:S(2)}, u32[]{:S(2)}) collective-permute-start(bf16[8,272,128]{2,1,0:T(8,128)(2,1)S(1)} %slice.4), channel_id=1, source_target_pairs={{0,64},{64,128},{128,192},{1,65},{65,129},{129,193},{2,66},{66,130... | collective-permute-start | bytes 1671176 | tf_op jit(solution)/shard_map/ppermute | solution.py:347
  49.5 1.4 %collective-permute-done.1.near_ref = f32[136,128]{1,0:T(8,128)S(1)} collective-permute-done((f32[136,128]{1,0:T(8,128)S(1)}, f32[136,128]{1,0:T(8,128)S(1)}, u32[]{:S(2)}, u32[]{:S(2)}) %collective-permute-start.1) | collective-permute-done | bytes 69664 | tf_op jit(solution)/shard_map/ppermute | solution.py:367
  50.9 2.6 %enter.1 = (bf16[8,128,128]{2,1,0:T(8,128)(2,1)S(1)}, f32[8,128]{1,0:T(8,128)S(1)}, s32[8]{0:T(128)S(1)}) custom-call(s32[3]{0:T(128)S(1)} %pad_add_fusion.info_ref, bf16[8,400,128]{2,1,0:T(8,128)(2,1)S(1)} %all_to_all.10.own_ref, f32[8,128,128]{2,1,0:T(8,128)S(1)} %get-tuple-element.24.partial_ref, f32[8,128,128]{2,1,0:T(8,128)S(1)} %get-tuple-element.25.weight_ref, ...), custom_call_target="tpu_custom_call" | custom-call | flops 1000000000 | bytes 3145728 | tf_op jit(solution)/shard_map/enter/pallas_call | solution.py:372
  53.6 1.7 %collective-permute-start.5 = (f32[8,128]{1,0:T(8,128)S(1)}, f32[8,128]{1,0:T(8,128)S(1)}, u32[]{:S(2)}, u32[]{:S(2)}) collective-permute-start(f32[8,128]{1,0:T(8,128)S(1)} %get-tuple-element.29), channel_id=1, source_target_pairs={{0,1},{1,0},{2,3},{3,2},{4,5},{5,4},{6,7},{7,6},{8,9},{9,8},{10,11... | collective-permute-start | bytes 12296 | tf_op jit(solution)/shard_map/ppermute | solution.py:381
  55.2 2.0 %collective-permute-done.5 = f32[8,128]{1,0:T(8,128)S(1)} collective-permute-done((f32[8,128]{1,0:T(8,128)S(1)}, f32[8,128]{1,0:T(8,128)S(1)}, u32[]{:S(2)}, u32[]{:S(2)}) %collective-permute-start.5) | collective-permute-done | bytes 4128 | tf_op jit(solution)/shard_map/ppermute | solution.py:381
  57.3 3.2 %collective-permute-start.6 = (f32[8,128]{1,0:T(8,128)S(1)}, f32[8,128]{1,0:T(8,128)S(1)}, u32[]{:S(2)}, u32[]{:S(2)}) collective-permute-start(f32[8,128]{1,0:T(8,128)S(1)} %add.10), channel_id=1, source_target_pairs={{0,2},{1,3},{2,0},{3,1},{4,6},{5,7},{6,4},{7,5},{8,10},{9,11},{10,... | collective-permute-start | bytes 12296 | tf_op jit(solution)/shard_map/ppermute | solution.py:382
  60.4 3.7 %own_window.1 = (f32[1024,128]{1,0:T(8,128)S(1)}, f32[1024,128]{1,0:T(8,128)S(1)}, f32[1024,128]{1,0:T(8,128)S(1)}) custom-call(s32[3]{0:T(128)S(1)} %pad_add_fusion.info_ref, bf16[8,400,128]{2,1,0:T(8,128)(2,1)S(1)} %all_to_all.10.own_ref, bf16[8,272,128]{2,1,0:T(8,128)(2,1)S(1)} %collective-permute-done.other_ref, ...), custom_call_target="tpu_custom_call" | custom-call | flops 5000000000 | bytes 6291456 | tf_op jit(solution)/shard_map/own_window/pallas_call | solution.py:369
  64.2 0.9 collective-permute-done.4.far_ref
  65.1 10.8 %collective-permute-done.3.near_ref = bf16[8,272,128]{2,1,0:T(8,128)(2,1)S(1)} collective-permute-done((bf16[8,272,128]{2,1,0:T(8,128)(2,1)S(1)}, bf16[8,272,128]{2,1,0:T(8,128)(2,1)S(1)}, u32[]{:S(2)}, u32[]{:S(2)}) %collective-permute-start.3) | collective-permute-done | bytes 557088 | tf_op jit(solution)/shard_map/ppermute | solution.py:347
  76.4 5.0 %past_own.1 = (f32[1024,128]{1,0:T(8,128)S(1)}, f32[1024,128]{1,0:T(8,128)S(1)}, f32[1024,128]{1,0:T(8,128)S(1)}) custom-call(s32[3]{0:T(128)S(1)} %pad_add_fusion.info_ref, s32[8]{0:T(128)S(1)} %get-tuple-element.27.need_ref, bf16[8,400,128]{2,1,0:T(8,128)(2,1)S(1)} %all_to_all.10.own_ref, bf16[8,128,128]{2,1,0:T(8,128)(2,1)S(1)} %get-tuple-element.28.mark_ref, ...), custom_call_target="tpu_custom_call" | custom-call | flops 4000000000 | bytes 8388608 | tf_op jit(solution)/shard_map/past_own/pallas_call | solution.py:386
  81.5 5.0 %past_other.1 = bf16[8,272,128]{2,1,0:T(8,128)(2,1)S(1)} custom-call(s32[3]{0:T(128)S(1)} %pad_add_fusion.info_ref, s32[8]{0:T(128)S(1)} %get-tuple-element.27.need_ref, bf16[8,400,128]{2,1,0:T(8,128)(2,1)S(1)} %all_to_all.10.own_ref, bf16[8,128,128]{2,1,0:T(8,128)(2,1)S(1)} %get-tuple-element.28.mark_ref, ...), custom_call_target="tpu_custom_call" | custom-call | flops 4000000000 | bytes 8388608 | tf_op jit(solution)/shard_map/past_other/pallas_call | solution.py:394
  86.5 21.1 %all_to_all.11.got_ref = bf16[8,272,128]{2,1,0:T(8,128)(2,1)S(1)} all-to-all(bf16[8,272,128]{2,1,0:T(8,128)(2,1)S(1)} %past_other.1), channel_id=1, replica_groups=mesh['x'=4,'z'=8,'core'=2,'head'=4] {'z'}, dimensions={0} | all-to-all | bytes 1114112 | tf_op jit(solution)/shard_map/all_to_all | solution.py:403
  107.5 0.9 finish.1
  (28 shorter events, 1.6 us)
Async XLA Ops:
  0.0 37.6 %copy-start = (f32[8,128,128]{2,1,0:T(8,128)S(1)}, f32[8,128,128]{2,1,0:T(8,128)}, u32[]{:S(2)}) copy-start(f32[8,128,128]{2,1,0:T(8,128)} %param.13) | copy-start | bytes 1572868
  0.0 0.7 copy-start.4
  0.0 0.7 copy-start.7
  0.0 0.7 copy-start.8
  0.0 0.7 copy-start.9
  0.8 0.9 copy-start.1
  1.7 0.9 copy-start.2
  2.7 0.9 copy-start.3
  3.6 0.7 copy-start.5
  37.5 2.0 %collective-permute-start = (bf16[8,272,128]{2,1,0:T(8,128)(2,1)S(1)}, bf16[8,272,128]{2,1,0:T(8,128)(2,1)S(1)}, u32[]{:S(2)}, u32[]{:S(2)}) collective-permute-start(bf16[8,272,128]{2,1,0:T(8,128)(2,1)S(1)} %slice.4), channel_id=1, source_target_pairs={{0,4},{4,0},{1,5},{5,1},{2,6},{6,2},{3,7},{7,3},{8,12},{12,8},{9,1... | collective-permute-start | bytes 1671176 | tf_op jit(solution)/shard_map/ppermute | solution.py:349
  41.7 7.8 %collective-permute-start.2 = (f32[136,128]{1,0:T(8,128)S(1)}, f32[136,128]{1,0:T(8,128)S(1)}, u32[]{:S(2)}, u32[]{:S(2)}) collective-permute-start(f32[136,128]{1,0:T(8,128)S(1)} %get-tuple-element.26.state_ref), channel_id=1, source_target_pairs={{0,128},{64,192},{1,129},{65,193},{2,130},{66,194},{3,131},{67,195... | collective-permute-start | bytes 208904 | tf_op jit(solution)/shard_map/ppermute | solution.py:368
  43.0 7.9 %collective-permute-start.1 = (f32[136,128]{1,0:T(8,128)S(1)}, f32[136,128]{1,0:T(8,128)S(1)}, u32[]{:S(2)}, u32[]{:S(2)}) collective-permute-start(f32[136,128]{1,0:T(8,128)S(1)} %get-tuple-element.26.state_ref), channel_id=1, source_target_pairs={{0,64},{64,128},{128,192},{1,65},{65,129},{129,193},{2,66},{66,130... | collective-permute-start | bytes 208904 | tf_op jit(solution)/shard_map/ppermute | solution.py:367
  46.2 18.9 %collective-permute-start.4 = (bf16[8,272,128]{2,1,0:T(8,128)(2,1)S(1)}, bf16[8,272,128]{2,1,0:T(8,128)(2,1)S(1)}, u32[]{:S(2)}, u32[]{:S(2)}) collective-permute-start(bf16[8,272,128]{2,1,0:T(8,128)(2,1)S(1)} %slice.4), channel_id=1, source_target_pairs={{0,128},{64,192},{1,129},{65,193},{2,130},{66,194},{3,131},{67,195... | collective-permute-start | bytes 1671176 | tf_op jit(solution)/shard_map/ppermute | solution.py:348
  47.5 28.4 %collective-permute-start.3 = (bf16[8,272,128]{2,1,0:T(8,128)(2,1)S(1)}, bf16[8,272,128]{2,1,0:T(8,128)(2,1)S(1)}, u32[]{:S(2)}, u32[]{:S(2)}) collective-permute-start(bf16[8,272,128]{2,1,0:T(8,128)(2,1)S(1)} %slice.4), channel_id=1, source_target_pairs={{0,64},{64,128},{128,192},{1,65},{65,129},{129,193},{2,66},{66,130... | collective-permute-start | bytes 1671176 | tf_op jit(solution)/shard_map/ppermute | solution.py:347
  53.6 3.7 %collective-permute-start.5 = (f32[8,128]{1,0:T(8,128)S(1)}, f32[8,128]{1,0:T(8,128)S(1)}, u32[]{:S(2)}, u32[]{:S(2)}) collective-permute-start(f32[8,128]{1,0:T(8,128)S(1)} %get-tuple-element.29), channel_id=1, source_target_pairs={{0,1},{1,0},{2,3},{3,2},{4,5},{5,4},{6,7},{7,6},{8,9},{9,8},{10,11... | collective-permute-start | bytes 12296 | tf_op jit(solution)/shard_map/ppermute | solution.py:381
  57.3 6.9 %collective-permute-start.6 = (f32[8,128]{1,0:T(8,128)S(1)}, f32[8,128]{1,0:T(8,128)S(1)}, u32[]{:S(2)}, u32[]{:S(2)}) collective-permute-start(f32[8,128]{1,0:T(8,128)S(1)} %add.10), channel_id=1, source_target_pairs={{0,2},{1,3},{2,0},{3,1},{4,6},{5,7},{6,4},{7,5},{8,10},{9,11},{10,... | collective-permute-start | bytes 12296 | tf_op jit(solution)/shard_map/ppermute | solution.py:382
  75.9 5.6 %collective-permute-start.7 = (bf16[8,272,128]{2,1,0:T(8,128)(2,1)S(1)}, bf16[8,272,128]{2,1,0:T(8,128)(2,1)S(1)}, u32[]{:S(2)}, u32[]{:S(2)}) collective-permute-start(bf16[8,272,128]{2,1,0:T(8,128)(2,1)S(1)} %collective-permute-done.3.near_ref), channel_id=1, source_target_pairs={{0,4},{4,0},{1,5},{5,1},{2,6},{6,2},{3,7},{7,3},{8,12},{12,8},{9,1... | collective-permute-start | bytes 1671176 | tf_op jit(solution)/shard_map/ppermute | solution.py:384
  75.9 5.5 %collective-permute-start.8 = (bf16[8,272,128]{2,1,0:T(8,128)(2,1)S(1)}, bf16[8,272,128]{2,1,0:T(8,128)(2,1)S(1)}, u32[]{:S(2)}, u32[]{:S(2)}) collective-permute-start(bf16[8,272,128]{2,1,0:T(8,128)(2,1)S(1)} %collective-permute-done.4.far_ref), channel_id=1, source_target_pairs={{0,4},{4,0},{1,5},{5,1},{2,6},{6,2},{3,7},{7,3},{8,12},{12,8},{9,1... | collective-permute-start | bytes 1671176 | tf_op jit(solution)/shard_map/ppermute | solution.py:385
  86.5 21.1 %copy-start.6 = (f32[1024]{0:T(1024)S(1)}, f32[1024]{0:T(1024)}, u32[]{:S(2)}) copy-start(f32[1024]{0:T(1024)} %param.14) | copy-start | bytes 12292

commit v3 on v2

--- a/solution.py
+++ b/solution.py
@@ -163,18 +163,17 @@
     keep = jnp.where((far_doc == near_doc) & (x >= 2), jnp.exp(near_decay), 0.0)
     state = near_ref[0:DH, :] + keep * far_ref[0:DH, :]
     state = jnp.where((start_doc == near_doc) & (x >= 1), state, 0.0)
-    ones = jnp.ones((8, DH), F32)
+    high = state.astype(BF16)
+    low = (state - high.astype(F32)).astype(BF16)
+    queries = jnp.concatenate([own_ref[i, KV_ROWS:ROWS, :] for i in range(HEADS)], axis=0)
+    product = dot(queries, jnp.concatenate([high, low], axis=1))
+    product = product[:, :DH] + product[:, DH:]
+    eye = lax.broadcasted_iota(jnp.int32, (TOK, DH), 0) == lax.broadcasted_iota(jnp.int32, (TOK, DH), 1)
     for i in range(HEADS):
-        linear = partial_ref[i] + weight_ref[i] * split_dot(own_ref[i, KV_ROWS:ROWS, :], state)
+        linear = partial_ref[i] + weight_ref[i] * product[i * TOK : (i + 1) * TOK]
         linear_ref[i] = linear.astype(BF16)
-        square = lax.dot_general(
-            ones,
-            linear * linear,
-            (((1,), (1,)), ((), ())),
-            precision=lax.Precision.HIGHEST,
-            preferred_element_type=F32,
-        )
-        square_ref[i : i + 1, :] = square[0:1]
+        square = jnp.sum(linear * linear, axis=1, keepdims=True)
+        square_ref[i : i + 1, :] = jnp.sum(jnp.where(eye, square, 0.0), axis=0, keepdims=True)
     for tile in range(TILES):
         tile_doc = jnp.broadcast_to(meta_rows(own_ref, 2 * tile)[3:4, :1], (1, TOK))
         need_ref[2 * tile] = jnp.where(x >= 1, jnp.max(jnp.where(tile_doc == near_doc, 1, 0)), 0)
@@ -257,33 +256,45 @@
         store_part(refs, tile, part)
 
 
-def past_blocks(core, own, own_ref, mark_ref, need_ref, near_ref, far_ref, refs):
+def near_kernel(need_ref, own_ref, mark_ref, near_ref, other_ref, a_ref, b_ref, c_ref, *refs):
+    olds = (a_ref, b_ref, c_ref)
+    for tile in range(TILES):
+        needed = need_ref[2 * tile] == 1
+
+        @pl.when(needed)
+        def _(tile=tile):
+            queries = marked_queries(own_ref, mark_ref, tile)
+            part = absorb(queries, near_ref, range(TILES), (None, None), load_part(olds, tile))
+            store_part(refs, tile, absorb(queries, other_ref, range(TILES), (None, None), part))
+
+        @pl.when(jnp.logical_not(needed))
+        def _(tile=tile):
+            store_part(refs, tile, load_part(olds, tile))
+
+
+def far_blocks(core, own, own_ref, mark_ref, need_ref, far_ref, olds, refs):
     at, key = tile_places(core, own)
     mask = key > at
     for tile in range(TILES):
-
-        @pl.when(need_ref[2 * tile] == 1)
+        needed = need_ref[2 * tile + 1] == 1
+
+        @pl.when(needed)
         def _(tile=tile):
             queries = marked_queries(own_ref, mark_ref, tile)
-            store_part(refs, tile, absorb(queries, near_ref, range(TILES), (None, None), load_part(refs, tile)))
-
-        @pl.when(need_ref[2 * tile + 1] == 1)
+            store_part(refs, tile, absorb(queries, far_ref, range(tile, TILES), (tile, mask), load_part(olds, tile)))
+
+        @pl.when(jnp.logical_not(needed))
         def _(tile=tile):
-            queries = marked_queries(own_ref, mark_ref, tile)
-            store_part(refs, tile, absorb(queries, far_ref, range(tile, TILES), (tile, mask), load_part(refs, tile)))
-
-
-def past_own_kernel(info_ref, need_ref, own_ref, mark_ref, near_ref, far_ref, a_ref, b_ref, c_ref, *refs):
-    for before, after in zip((a_ref, b_ref, c_ref), refs):
-        after[...] = before[...]
-    past_blocks(info_ref[2], True, own_ref, mark_ref, need_ref, near_ref, far_ref, refs)
-
-
-def past_other_kernel(
-    info_ref, need_ref, own_ref, mark_ref, near_ref, far_ref, a_ref, b_ref, c_ref, linear_ref, square_ref, out_ref, *refs
+            store_part(refs, tile, load_part(olds, tile))
+
+
+def far_own_kernel(info_ref, need_ref, own_ref, mark_ref, far_ref, a_ref, b_ref, c_ref, *refs):
+    far_blocks(info_ref[2], True, own_ref, mark_ref, need_ref, far_ref, (a_ref, b_ref, c_ref), refs)
+
+
+def far_other_kernel(
+    info_ref, need_ref, own_ref, mark_ref, far_ref, a_ref, b_ref, c_ref, linear_ref, square_ref, out_ref, *refs
 ):
-    for before, after in zip((a_ref, b_ref, c_ref), refs):
-        after[...] = before[...]
     row = lax.broadcasted_iota(jnp.int32, (META, TOK), 0)
     for i in range(HEADS):
         out_ref[i, TOK : 2 * TOK, :] = linear_ref[i]
@@ -291,7 +302,7 @@
         for n, part in enumerate(split3(square_ref[i : i + 1, :])):
             meta = jnp.where(row == n, jnp.broadcast_to(part.astype(F32), (META, TOK)), meta)
         out_ref[i, 2 * TOK :, :] = meta.astype(BF16)
-    past_blocks(info_ref[2], False, own_ref, mark_ref, need_ref, near_ref, far_ref, refs)
+    far_blocks(info_ref[2], False, own_ref, mark_ref, need_ref, far_ref, (a_ref, b_ref, c_ref), refs)
     _, total_ref, output_ref = refs
     for i in range(HEADS):
         span = pl.ds(i * TOK, TOK)
@@ -315,7 +326,10 @@
 HBM = pl.BlockSpec(memory_space=pltpu.HBM)
 
 
-def call(kernel, name, specs, shapes, scratch=(), flops=0, moved=0, outs=None):
+LIMIT = {"prepare": 58}
+
+
+def call(kernel, name, specs, shapes, scratch=(), outs=None):
     many = isinstance(shapes, (list, tuple))
     return pl.pallas_call(
         kernel,
@@ -324,8 +338,8 @@
         in_specs=specs,
         out_specs=outs or ([VMEM] * len(shapes) if many else VMEM),
         scratch_shapes=list(scratch),
-        compiler_params=pltpu.CompilerParams(vmem_limit_bytes=32 * 2**20),
-        cost_estimate=pl.CostEstimate(flops=flops, bytes_accessed=moved, transcendentals=0),
+        compiler_params=pltpu.CompilerParams(vmem_limit_bytes=LIMIT.get(name, 16) * 2**20),
+        cost_estimate=pl.CostEstimate(flops=0, bytes_accessed=0, transcendentals=0),
     )
 
 
@@ -339,7 +353,6 @@
         [SMEM, SMEM, HBM, HBM, HBM, VMEM, VMEM, VMEM],
         shape((HEADS, ROWS, TOK), BF16),
         scratch=[pltpu.VMEM((TOK, HEADS * DH), BF16)] * 3 + [pltpu.SemaphoreType.DMA((3,))],
-        moved=2 << 20,
     )(rate_table, rate_index, queries, keys, values, speed.T, drop.T, doc_id[None, :])
     own = lax.all_to_all(packed, "z", 0, 0, tiled=True)
     sent = own[:, :KV_ROWS]
@@ -361,47 +374,39 @@
             shape((DH + 8, DH), F32),
             shape((HEADS, TOK, TOK), BF16),
         ],
-        flops=2_000_000_000,
-        moved=4 << 20,
     )(info, own, other, init)
     near_state = lax.ppermute(state, "x", [(0, 1), (1, 2), (2, 3)])
     far_state = lax.ppermute(state, "x", [(0, 2), (1, 3)])
     own_part = call(
-        own_window_kernel, "own_window", [SMEM] + [VMEM] * 3, part_shapes, flops=5_000_000_000, moved=6 << 20
+        own_window_kernel, "own_window", [SMEM] + [VMEM] * 3, part_shapes
     )(info, own, other, mark)
+    near_state, far_state, own_part = lax.optimization_barrier((near_state, far_state, own_part))
     linear, square, need = call(
         enter_kernel,
         "enter",
         [SMEM] + [VMEM] * 6,
         [shape((HEADS, TOK, DH), BF16), shape((HEADS, TOK), F32), shape((2 * TILES,), jnp.int32)],
         outs=[VMEM, VMEM, SMEM],
-        flops=1_000_000_000,
-        moved=3 << 20,
     )(info, own, partial, weight, state, near_state, far_state)
     square = square + lax.ppermute(square, "head", [(i, i ^ 1) for i in range(4)])
+    near, need, own_part, square = lax.optimization_barrier((near, need, own_part, square))
     square = square + lax.ppermute(square, "head", [(i, i ^ 2) for i in range(4)])
-    near, far, square, own_part = lax.optimization_barrier((near, far, square, own_part))
     near_other = lax.ppermute(near, "core", pair)
+    part = call(near_kernel, "near_window", [SMEM] + [VMEM] * 7, part_shapes)(
+        need, own, mark, near, near_other, *own_part
+    )
+    far, part, square = lax.optimization_barrier((far, part, square))
     far_other = lax.ppermute(far, "core", pair)
-    own_part = call(
-        past_own_kernel,
-        "past_own",
-        [SMEM] * 2 + [VMEM] * 7,
-        part_shapes,
-        flops=4_000_000_000,
-        moved=8 << 20,
-    )(info, need, own, mark, near, far, *own_part)
+    part = call(far_own_kernel, "far_own", [SMEM] * 2 + [VMEM] * 6, part_shapes)(info, need, own, mark, far, *part)
     mixed = call(
-        past_other_kernel,
-        "past_other",
-        [SMEM] * 2 + [VMEM] * 9,
+        far_other_kernel,
+        "far_other",
+        [SMEM] * 2 + [VMEM] * 8,
         shape((HEADS, 2 * TOK + META, DH), BF16),
         scratch=[pltpu.VMEM((tokens, TOK), F32)] * 3,
-        flops=4_000_000_000,
-        moved=8 << 20,
-    )(info, need, own, mark, near_other, far_other, *own_part, linear, square)
+    )(info, need, own, mark, far_other, *part, linear, square)
     back = lax.all_to_all(mixed, "z", 0, 0, tiled=True)
-    return call(finish_kernel, "finish", [VMEM] * 2, shape((TOK, HEADS * DH), BF16), moved=1 << 20)(
+    return call(finish_kernel, "finish", [VMEM] * 2, shape((TOK, HEADS * DH), BF16))(
         back, lin_gain[None, :]
     )
 

time: 109 us -> 107 us (0.982)
  local copies, waits for them, and re-layouts: 4.33 us -> 0.05 us
  Pallas kernels: 20.5 us -> 21.8 us
  waiting for transfers between devices: 17.1 us -> 18.3 us
    ppermute x1, waiting for transfers between devices: 10.8 us -> 0.01 us  [body(): near = lax.ppermute(sent, 'x', [(0, 1), (1, 2), (2, 3)])]
    ppermute x1, waiting for transfers between devices: 0.12 us -> 6.35 us  [body(): far_state = lax.ppermute(state, 'x', [(0, 2), (1, 3)])]
    ppermute x1, waiting for transfers between devices: 0.89 us -> 6.83 us  [body(): far = lax.ppermute(sent, 'x', [(0, 2), (1, 3)])]
    unnamed x20 -> x4, local copies, waits for them, and re-layouts: 4.28 us -> 0.01 us
    pallas_call x1, Pallas kernels: 1.03 us -> 2.95 us  [body(): call(prepare_kernel, 'prepare', [SMEM, SMEM, HBM, HBM, HBM, VMEM, VMEM, V...]
    ppermute x1, waiting for transfers between devices: 0.01 us -> 1.92 us  [body(): lax.ppermute(square, 'head', [(i, i ^ 2) for i in range(4)])]
    ppermute x1, waiting for transfers between devices: 1.84 us -> 0.01 us  [body(): other = lax.ppermute(sent, 'core', pair)]
    ppermute x1, starting transfers between devices: 1.92 us -> 3.11 us  [body(): near = lax.ppermute(sent, 'x', [(0, 1), (1, 2), (2, 3)])]
  transfers between devices with their start and end apart: 9 -> 9, of which waited for: 6 -> 5; matrix products, arithmetic and copies ran while one was open for 0% -> 0% of each run, Pallas kernels for 10% -> 14%
where the time goes in v3:
time: 107 us
  blocking collectives  53.8 us (50%)
  Pallas kernels  21.8 us (20%)
  waiting for transfers between devices  18.3 us (17%)
  starting transfers between devices  12.6 us (12%)
    all_to_all x1, blocking collectives, body(): own = lax.all_to_all(packed, 'z', 0, 0, tiled=True)  32.3 us
    all_to_all x1, blocking collectives, body(): back = lax.all_to_all(mixed, 'z', 0, 0, tiled=True)  21.5 us
    ppermute x1, waiting for transfers between devices, body(): far = lax.ppermute(sent, 'x', [(0, 2), (1, 3)])  6.83 us
    ppermute x1, waiting for transfers between devices, body(): far_state = lax.ppermute(state, 'x', [(0, 2), (1, 3)])  6.35 us
    pallas_call x1, Pallas kernels, body(): call(near_kernel, 'near_window', [SMEM] + [VMEM] * 7, part_shapes)  5.08 us
    pallas_call x1, Pallas kernels, body(): call(own_window_kernel, 'own_window', [SMEM] + [VMEM] * 3, part_shapes)  3.74 us
    ppermute x1, starting transfers between devices, body(): lax.ppermute(square, 'head', [(i, i ^ 2) for i in range(4)])  3.28 us
    ppermute x1, starting transfers between devices, body(): near = lax.ppermute(sent, 'x', [(0, 1), (1, 2), (2, 3)])  3.11 us
  transfers between devices with their start and end apart: 9, of which 5 were waited for; matrix products, arithmetic and copies ran while one was open for 0% of the time, Pallas kernels for 14%

profile of v3, /device:TPU:4, one launch (start us, length us, event | category | flops | bytes accessed | tf_op | source)
XLA Modules:
  0.0 106.8 jit_solution(13396658375268783421)
XLA Ops:
  0.0 2.9 %prepare.1 = bf16[8,400,128]{2,1,0:T(8,128)(2,1)} custom-call(f32[16]{0:T(128)} %table_ref.1, s32[8]{0:T(128)} %index_ref.1, bf16[128,1024]{1,0:T(8,128)(2,1)} %q_hbm.1, bf16[128,1024]{1,0:T(8,128)(2,1)} %k_hbm.1, bf16[128,1024]{1,0:T(8,128)(2,1)} %v_hbm.1, f32[8,128]{1,0:T(8,128)} %bitcast.8, f32[8,128]{1,0:T(8,128)} %bitcast.9, s32[1,128]{1,0:T(1,128)} %bitcast.10), custom_call_target="tpu_custom_call" | custom-call | tf_op jit(solution)/shard_map/prepare/pallas_call | solution.py:350
  3.0 32.3 %all_to_all.10.own_ref = bf16[8,400,128]{2,1,0:T(8,128)(2,1)S(1)} all-to-all(bf16[8,400,128]{2,1,0:T(8,128)(2,1)} %prepare.1), channel_id=1, replica_groups=mesh['x'=4,'z'=8,'core'=2,'head'=4] {'z'}, dimensions={0} | all-to-all | bytes 1638400 | tf_op jit(solution)/shard_map/all_to_all | solution.py:357
  35.3 0.1 collective-permute-start.1
  35.4 3.1 %collective-permute-start = (bf16[8,272,128]{2,1,0:T(8,128)(2,1)S(1)}, bf16[8,272,128]{2,1,0:T(8,128)(2,1)S(1)}, u32[]{:S(2)}, u32[]{:S(2)}) collective-permute-start(bf16[8,272,128]{2,1,0:T(8,128)(2,1)S(1)} %slice.4), channel_id=1, source_target_pairs={{0,64},{64,128},{128,192},{1,65},{65,129},{129,193},{2,66},{66,130... | collective-permute-start | bytes 1671176 | tf_op jit(solution)/shard_map/ppermute | solution.py:360
  38.5 0.1 pad_add_fusion.info_ref
  38.6 2.2 %linear.1 = (f32[8,128,128]{2,1,0:T(8,128)S(1)}, f32[8,128,128]{2,1,0:T(8,128)S(1)}, f32[136,128]{1,0:T(8,128)S(1)}, bf16[8,128,128]{2,1,0:T(8,128)(2,1)S(1)}) custom-call(s32[3]{0:T(128)S(1)} %pad_add_fusion.info_ref, bf16[8,400,128]{2,1,0:T(8,128)(2,1)S(1)} %all_to_all.10.own_ref, bf16[8,272,128]{2,1,0:T(8,128)(2,1)S(1)} %collective-permute-done.1.other_ref, ...), custom_call_target="tpu_custom_call" | custom-call | tf_op jit(solution)/shard_map/linear/pallas_call | solution.py:367
  40.8 1.3 %collective-permute-start.3 = (f32[136,128]{1,0:T(8,128)S(1)}, f32[136,128]{1,0:T(8,128)S(1)}, u32[]{:S(2)}, u32[]{:S(2)}) collective-permute-start(f32[136,128]{1,0:T(8,128)S(1)} %get-tuple-element.39.state_ref), channel_id=1, source_target_pairs={{0,128},{64,192},{1,129},{65,193},{2,130},{66,194},{3,131},{67,195... | collective-permute-start | bytes 208904 | tf_op jit(solution)/shard_map/ppermute | solution.py:379
  42.1 1.9 %collective-permute-start.2 = (f32[136,128]{1,0:T(8,128)S(1)}, f32[136,128]{1,0:T(8,128)S(1)}, u32[]{:S(2)}, u32[]{:S(2)}) collective-permute-start(f32[136,128]{1,0:T(8,128)S(1)} %get-tuple-element.39.state_ref), channel_id=1, source_target_pairs={{0,64},{64,128},{128,192},{1,65},{65,129},{129,193},{2,66},{66,130... | collective-permute-start | bytes 208904 | tf_op jit(solution)/shard_map/ppermute | solution.py:378
  44.1 3.7 %own_window.1 = (f32[1024,128]{1,0:T(8,128)S(1)}, f32[1024,128]{1,0:T(8,128)S(1)}, f32[1024,128]{1,0:T(8,128)S(1)}) custom-call(s32[3]{0:T(128)S(1)} %pad_add_fusion.info_ref, bf16[8,400,128]{2,1,0:T(8,128)(2,1)S(1)} %all_to_all.10.own_ref, bf16[8,272,128]{2,1,0:T(8,128)(2,1)S(1)} %collective-permute-done.1.other_ref, ...), custom_call_target="tpu_custom_call" | custom-call | tf_op jit(solution)/shard_map/own_window/pallas_call | solution.py:380
  47.8 6.3 %collective-permute-done.3.far_ref = f32[136,128]{1,0:T(8,128)S(1)} collective-permute-done((f32[136,128]{1,0:T(8,128)S(1)}, f32[136,128]{1,0:T(8,128)S(1)}, u32[]{:S(2)}, u32[]{:S(2)}) %collective-permute-start.3) | collective-permute-done | bytes 69664 | tf_op jit(solution)/shard_map/ppermute | solution.py:379
  54.2 1.1 %collective-permute-done.2.near_ref = f32[136,128]{1,0:T(8,128)S(1)} collective-permute-done((f32[136,128]{1,0:T(8,128)S(1)}, f32[136,128]{1,0:T(8,128)S(1)}, u32[]{:S(2)}, u32[]{:S(2)}) %collective-permute-start.2) | collective-permute-done | bytes 69664 | tf_op jit(solution)/shard_map/ppermute | solution.py:378
  55.3 1.4 %enter.1 = (bf16[8,128,128]{2,1,0:T(8,128)(2,1)S(1)}, f32[8,128]{1,0:T(8,128)S(1)}, s32[8]{0:T(128)S(1)}) custom-call(s32[3]{0:T(128)S(1)} %pad_add_fusion.info_ref, bf16[8,400,128]{2,1,0:T(8,128)(2,1)S(1)} %all_to_all.10.own_ref, f32[8,128,128]{2,1,0:T(8,128)S(1)} %get-tuple-element.37.partial_ref, f32[8,128,128]{2,1,0:T(8,128)S(1)} %get-tuple-element.38.weight_ref, ...), custom_call_target="tpu_custom_call" | custom-call | tf_op jit(solution)/shard_map/enter/pallas_call | solution.py:384
  56.7 1.7 %collective-permute-start.4 = (f32[8,128]{1,0:T(8,128)S(1)}, f32[8,128]{1,0:T(8,128)S(1)}, u32[]{:S(2)}, u32[]{:S(2)}) collective-permute-start(f32[8,128]{1,0:T(8,128)S(1)} %get-tuple-element.50), channel_id=1, source_target_pairs={{0,1},{1,0},{2,3},{3,2},{4,5},{5,4},{6,7},{7,6},{8,9},{9,8},{10,11... | collective-permute-start | bytes 12296 | tf_op jit(solution)/shard_map/ppermute | solution.py:391
  58.4 2.0 %collective-permute-done.4 = f32[8,128]{1,0:T(8,128)S(1)} collective-permute-done((f32[8,128]{1,0:T(8,128)S(1)}, f32[8,128]{1,0:T(8,128)S(1)}, u32[]{:S(2)}, u32[]{:S(2)}) %collective-permute-start.4) | collective-permute-done | bytes 4128 | tf_op jit(solution)/shard_map/ppermute | solution.py:391
  60.4 1.3 %collective-permute-start.5 = (bf16[8,272,128]{2,1,0:T(8,128)(2,1)S(1)}, bf16[8,272,128]{2,1,0:T(8,128)(2,1)S(1)}, u32[]{:S(2)}, u32[]{:S(2)}) collective-permute-start(bf16[8,272,128]{2,1,0:T(8,128)(2,1)S(1)} %slice.4), channel_id=1, source_target_pairs={{0,128},{64,192},{1,129},{65,193},{2,130},{66,194},{3,131},{67,195... | collective-permute-start | bytes 1671176 | tf_op jit(solution)/shard_map/ppermute | solution.py:361
  61.7 3.3 %collective-permute-start.7 = (f32[8,128]{1,0:T(8,128)S(1)}, f32[8,128]{1,0:T(8,128)S(1)}, u32[]{:S(2)}, u32[]{:S(2)}) collective-permute-start(f32[8,128]{1,0:T(8,128)S(1)} %add.10), channel_id=1, source_target_pairs={{0,2},{1,3},{2,0},{3,1},{4,6},{5,7},{6,4},{7,5},{8,10},{9,11},{10,... | collective-permute-start | bytes 12296 | tf_op jit(solution)/shard_map/ppermute | solution.py:393
  65.0 1.9 %collective-permute-done.7 = f32[8,128]{1,0:T(8,128)S(1)} collective-permute-done((f32[8,128]{1,0:T(8,128)S(1)}, f32[8,128]{1,0:T(8,128)S(1)}, u32[]{:S(2)}, u32[]{:S(2)}) %collective-permute-start.7) | collective-permute-done | bytes 4128 | tf_op jit(solution)/shard_map/ppermute | solution.py:393
  66.9 5.1 %near_window.1 = (f32[1024,128]{1,0:T(8,128)S(1)}, f32[1024,128]{1,0:T(8,128)S(1)}, f32[1024,128]{1,0:T(8,128)S(1)}) custom-call(s32[8]{0:T(128)S(1)} %get-tuple-element.51.need_ref, bf16[8,400,128]{2,1,0:T(8,128)(2,1)S(1)} %all_to_all.10.own_ref, bf16[8,128,128]{2,1,0:T(8,128)(2,1)S(1)} %get-tuple-element.40.mark_ref, ...), custom_call_target="tpu_custom_call" | custom-call | tf_op jit(solution)/shard_map/near_window/pallas_call | solution.py:395
  72.0 6.8 %collective-permute-done.5.far_ref = bf16[8,272,128]{2,1,0:T(8,128)(2,1)S(1)} collective-permute-done((bf16[8,272,128]{2,1,0:T(8,128)(2,1)S(1)}, bf16[8,272,128]{2,1,0:T(8,128)(2,1)S(1)}, u32[]{:S(2)}, u32[]{:S(2)}) %collective-permute-start.5) | collective-permute-done | bytes 557088 | tf_op jit(solution)/shard_map/ppermute | solution.py:361
  78.9 2.7 %far_own.1 = (f32[1024,128]{1,0:T(8,128)S(1)}, f32[1024,128]{1,0:T(8,128)S(1)}, f32[1024,128]{1,0:T(8,128)S(1)}) custom-call(s32[3]{0:T(128)S(1)} %pad_add_fusion.info_ref, s32[8]{0:T(128)S(1)} %get-tuple-element.51.need_ref, bf16[8,400,128]{2,1,0:T(8,128)(2,1)S(1)} %all_to_all.10.own_ref, bf16[8,128,128]{2,1,0:T(8,128)(2,1)S(1)} %get-tuple-element.40.mark_ref, ...), custom_call_target="tpu_custom_call" | custom-call | tf_op jit(solution)/shard_map/far_own/pallas_call | solution.py:400
  81.6 2.8 %far_other.1 = bf16[8,272,128]{2,1,0:T(8,128)(2,1)S(1)} custom-call(s32[3]{0:T(128)S(1)} %pad_add_fusion.info_ref, s32[8]{0:T(128)S(1)} %get-tuple-element.51.need_ref, bf16[8,400,128]{2,1,0:T(8,128)(2,1)S(1)} %all_to_all.10.own_ref, bf16[8,128,128]{2,1,0:T(8,128)(2,1)S(1)} %get-tuple-element.40.mark_ref, ...), custom_call_target="tpu_custom_call" | custom-call | tf_op jit(solution)/shard_map/far_other/pallas_call | solution.py:401
  84.4 0.0 copy-start.1
  84.4 21.5 %all_to_all.11.got_ref = bf16[8,272,128]{2,1,0:T(8,128)(2,1)S(1)} all-to-all(bf16[8,272,128]{2,1,0:T(8,128)(2,1)S(1)} %far_other.1), channel_id=1, replica_groups=mesh['x'=4,'z'=8,'core'=2,'head'=4] {'z'}, dimensions={0} | all-to-all | bytes 1114112 | tf_op jit(solution)/shard_map/all_to_all | solution.py:408
  105.9 0.9 finish.1
  (13 shorter events, 0.1 us)
Async XLA Ops:
  0.0 38.6 %copy-start = (f32[8,128,128]{2,1,0:T(8,128)S(1)}, f32[8,128,128]{2,1,0:T(8,128)}, u32[]{:S(2)}) copy-start(f32[8,128,128]{2,1,0:T(8,128)} %param.13) | copy-start | bytes 1572868
  35.3 3.3 %collective-permute-start.1 = (bf16[8,272,128]{2,1,0:T(8,128)(2,1)S(1)}, bf16[8,272,128]{2,1,0:T(8,128)(2,1)S(1)}, u32[]{:S(2)}, u32[]{:S(2)}) collective-permute-start(bf16[8,272,128]{2,1,0:T(8,128)(2,1)S(1)} %slice.4), channel_id=1, source_target_pairs={{0,4},{4,0},{1,5},{5,1},{2,6},{6,2},{3,7},{7,3},{8,12},{12,8},{9,1... | collective-permute-start | bytes 1671176 | tf_op jit(solution)/shard_map/ppermute | solution.py:362
  35.4 25.0 %collective-permute-start = (bf16[8,272,128]{2,1,0:T(8,128)(2,1)S(1)}, bf16[8,272,128]{2,1,0:T(8,128)(2,1)S(1)}, u32[]{:S(2)}, u32[]{:S(2)}) collective-permute-start(bf16[8,272,128]{2,1,0:T(8,128)(2,1)S(1)} %slice.4), channel_id=1, source_target_pairs={{0,64},{64,128},{128,192},{1,65},{65,129},{129,193},{2,66},{66,130... | collective-permute-start | bytes 1671176 | tf_op jit(solution)/shard_map/ppermute | solution.py:360
  40.8 13.3 %collective-permute-start.3 = (f32[136,128]{1,0:T(8,128)S(1)}, f32[136,128]{1,0:T(8,128)S(1)}, u32[]{:S(2)}, u32[]{:S(2)}) collective-permute-start(f32[136,128]{1,0:T(8,128)S(1)} %get-tuple-element.39.state_ref), channel_id=1, source_target_pairs={{0,128},{64,192},{1,129},{65,193},{2,130},{66,194},{3,131},{67,195... | collective-permute-start | bytes 208904 | tf_op jit(solution)/shard_map/ppermute | solution.py:379
  42.1 13.1 %collective-permute-start.2 = (f32[136,128]{1,0:T(8,128)S(1)}, f32[136,128]{1,0:T(8,128)S(1)}, u32[]{:S(2)}, u32[]{:S(2)}) collective-permute-start(f32[136,128]{1,0:T(8,128)S(1)} %get-tuple-element.39.state_ref), channel_id=1, source_target_pairs={{0,64},{64,128},{128,192},{1,65},{65,129},{129,193},{2,66},{66,130... | collective-permute-start | bytes 208904 | tf_op jit(solution)/shard_map/ppermute | solution.py:378
  56.7 3.7 %collective-permute-start.4 = (f32[8,128]{1,0:T(8,128)S(1)}, f32[8,128]{1,0:T(8,128)S(1)}, u32[]{:S(2)}, u32[]{:S(2)}) collective-permute-start(f32[8,128]{1,0:T(8,128)S(1)} %get-tuple-element.50), channel_id=1, source_target_pairs={{0,1},{1,0},{2,3},{3,2},{4,5},{5,4},{6,7},{7,6},{8,9},{9,8},{10,11... | collective-permute-start | bytes 12296 | tf_op jit(solution)/shard_map/ppermute | solution.py:391
  60.4 6.5 %collective-permute-start.6 = (bf16[8,272,128]{2,1,0:T(8,128)(2,1)S(1)}, bf16[8,272,128]{2,1,0:T(8,128)(2,1)S(1)}, u32[]{:S(2)}, u32[]{:S(2)}) collective-permute-start(bf16[8,272,128]{2,1,0:T(8,128)(2,1)S(1)} %collective-permute-done.near_ref), channel_id=1, source_target_pairs={{0,4},{4,0},{1,5},{5,1},{2,6},{6,2},{3,7},{7,3},{8,12},{12,8},{9,1... | collective-permute-start | bytes 1671176 | tf_op jit(solution)/shard_map/ppermute | solution.py:394
  60.4 18.4 %collective-permute-start.5 = (bf16[8,272,128]{2,1,0:T(8,128)(2,1)S(1)}, bf16[8,272,128]{2,1,0:T(8,128)(2,1)S(1)}, u32[]{:S(2)}, u32[]{:S(2)}) collective-permute-start(bf16[8,272,128]{2,1,0:T(8,128)(2,1)S(1)} %slice.4), channel_id=1, source_target_pairs={{0,128},{64,192},{1,129},{65,193},{2,130},{66,194},{3,131},{67,195... | collective-permute-start | bytes 1671176 | tf_op jit(solution)/shard_map/ppermute | solution.py:361
  61.7 5.2 %collective-permute-start.7 = (f32[8,128]{1,0:T(8,128)S(1)}, f32[8,128]{1,0:T(8,128)S(1)}, u32[]{:S(2)}, u32[]{:S(2)}) collective-permute-start(f32[8,128]{1,0:T(8,128)S(1)} %add.10), channel_id=1, source_target_pairs={{0,2},{1,3},{2,0},{3,1},{4,6},{5,7},{6,4},{7,5},{8,10},{9,11},{10,... | collective-permute-start | bytes 12296 | tf_op jit(solution)/shard_map/ppermute | solution.py:393
  78.9 2.7 %collective-permute-start.8 = (bf16[8,272,128]{2,1,0:T(8,128)(2,1)S(1)}, bf16[8,272,128]{2,1,0:T(8,128)(2,1)S(1)}, u32[]{:S(2)}, u32[]{:S(2)}) collective-permute-start(bf16[8,272,128]{2,1,0:T(8,128)(2,1)S(1)} %collective-permute-done.5.far_ref), channel_id=1, source_target_pairs={{0,4},{4,0},{1,5},{5,1},{2,6},{6,2},{3,7},{7,3},{8,12},{12,8},{9,1... | collective-permute-start | bytes 1671176 | tf_op jit(solution)/shard_map/ppermute | solution.py:399
  84.4 21.5 %copy-start.1 = (f32[1024]{0:T(1024)S(1)}, f32[1024]{0:T(1024)}, u32[]{:S(2)}) copy-start(f32[1024]{0:T(1024)} %param.14) | copy-start | bytes 12292

commit v4 on v3

--- a/solution.py
+++ b/solution.py
@@ -256,7 +256,7 @@
         store_part(refs, tile, part)
 
 
-def near_kernel(need_ref, own_ref, mark_ref, near_ref, other_ref, a_ref, b_ref, c_ref, *refs):
+def near_kernel(need_ref, own_ref, mark_ref, near_ref, other_ref, more_ref, a_ref, b_ref, c_ref, *refs):
     olds = (a_ref, b_ref, c_ref)
     for tile in range(TILES):
         needed = need_ref[2 * tile] == 1
@@ -265,7 +265,8 @@
         def _(tile=tile):
             queries = marked_queries(own_ref, mark_ref, tile)
             part = absorb(queries, near_ref, range(TILES), (None, None), load_part(olds, tile))
-            store_part(refs, tile, absorb(queries, other_ref, range(TILES), (None, None), part))
+            part = absorb(queries, other_ref, range(TILES // 2), (None, None), part)
+            store_part(refs, tile, absorb(queries, more_ref, range(TILES // 2), (None, None), part))
 
         @pl.when(jnp.logical_not(needed))
         def _(tile=tile):
@@ -358,7 +359,6 @@
     sent = own[:, :KV_ROWS]
     pair = [(0, 1), (1, 0)]
     near = lax.ppermute(sent, "x", [(0, 1), (1, 2), (2, 3)])
-    far = lax.ppermute(sent, "x", [(0, 2), (1, 3)])
     other = lax.ppermute(sent, "core", pair)
 
     tokens = HEADS * TOK
@@ -380,6 +380,8 @@
     own_part = call(
         own_window_kernel, "own_window", [SMEM] + [VMEM] * 3, part_shapes
     )(info, own, other, mark)
+    sent, own_part = lax.optimization_barrier((sent, own_part))
+    far = lax.ppermute(sent, "x", [(0, 2), (1, 3)])
     near_state, far_state, own_part = lax.optimization_barrier((near_state, far_state, own_part))
     linear, square, need = call(
         enter_kernel,
@@ -391,9 +393,9 @@
     square = square + lax.ppermute(square, "head", [(i, i ^ 1) for i in range(4)])
     near, need, own_part, square = lax.optimization_barrier((near, need, own_part, square))
     square = square + lax.ppermute(square, "head", [(i, i ^ 2) for i in range(4)])
-    near_other = lax.ppermute(near, "core", pair)
-    part = call(near_kernel, "near_window", [SMEM] + [VMEM] * 7, part_shapes)(
-        need, own, mark, near, near_other, *own_part
+    near_other = [lax.ppermute(near[at : at + TILES], "core", pair) for at in (0, TILES)]
+    part = call(near_kernel, "near_window", [SMEM] + [VMEM] * 8, part_shapes)(
+        need, own, mark, near, *near_other, *own_part
     )
     far, part, square = lax.optimization_barrier((far, part, square))
     far_other = lax.ppermute(far, "core", pair)

time: 107 us -> 102 us (0.953)
  waiting for transfers between devices: 18.3 us -> 10.5 us
  Pallas kernels: 21.8 us -> 24.8 us
    ppermute x1, waiting for transfers between devices: 6.83 us -> 0.01 us  [body(): far = lax.ppermute(sent, 'x', [(0, 2), (1, 3)])]
    pallas_call x1, Pallas kernels: 5.08 us -> 7.36 us  [body(): call(near_kernel, 'near_window', [SMEM] + [VMEM] * 8, part_shapes)]
    ppermute x1, waiting for transfers between devices: 6.35 us -> 5.05 us  [body(): far_state = lax.ppermute(state, 'x', [(0, 2), (1, 3)])]
  transfers between devices with their start and end apart: 9 -> 10, of which waited for: 5 -> 4; matrix products, arithmetic and copies ran while one was open for 0% -> 0% of each run, Pallas kernels for 14% -> 17%
where the time goes in v4:
time: 102 us; the launch traced here: 103 us
  blocking collectives  53.8 us (53%)
  Pallas kernels  24.8 us (24%)
  starting transfers between devices  13.2 us (13%)
  waiting for transfers between devices  10.5 us (10%)
    all_to_all x1, blocking collectives, body(): own = lax.all_to_all(packed, 'z', 0, 0, tiled=True)  32.3 us
    all_to_all x1, blocking collectives, body(): back = lax.all_to_all(mixed, 'z', 0, 0, tiled=True)  21.5 us
    pallas_call x1, Pallas kernels, body(): call(near_kernel, 'near_window', [SMEM] + [VMEM] * 8, part_shapes)  7.36 us
    ppermute x1, waiting for transfers between devices, body(): far_state = lax.ppermute(state, 'x', [(0, 2), (1, 3)])  5.05 us
    pallas_call x1, Pallas kernels, body(): call(own_window_kernel, 'own_window', [SMEM] + [VMEM] * 3, part_shapes)  3.74 us
    pallas_call x1, Pallas kernels, body(): call(far_other_kernel, 'far_other', [SMEM] * 2 + [VMEM] * 8, shape((HEADS...  3.19 us
    ppermute x1, starting transfers between devices, body(): lax.ppermute(square, 'head', [(i, i ^ 2) for i in range(4)])  3.19 us
    ppermute x1, starting transfers between devices, body(): near = lax.ppermute(sent, 'x', [(0, 1), (1, 2), (2, 3)])  3.11 us
  transfers between devices with their start and end apart: 10, of which 4 were waited for; matrix products, arithmetic and copies ran while one was open for 0% of the time, Pallas kernels for 17%

profile of v4, /device:TPU:4, one launch (start us, length us, event | category | flops | bytes accessed | tf_op | source)
XLA Modules:
  0.0 102.8 jit_solution(4702009775659081471)
XLA Ops:
  0.0 2.9 %prepare.1 = bf16[8,400,128]{2,1,0:T(8,128)(2,1)} custom-call(f32[16]{0:T(128)} %table_ref.1, s32[8]{0:T(128)} %index_ref.1, bf16[128,1024]{1,0:T(8,128)(2,1)} %q_hbm.1, bf16[128,1024]{1,0:T(8,128)(2,1)} %k_hbm.1, bf16[128,1024]{1,0:T(8,128)(2,1)} %v_hbm.1, f32[8,128]{1,0:T(8,128)} %bitcast.8, f32[8,128]{1,0:T(8,128)} %bitcast.9, s32[1,128]{1,0:T(1,128)} %bitcast.10), custom_call_target="tpu_custom_call" | custom-call | tf_op jit(solution)/shard_map/prepare/pallas_call | solution.py:351
  2.9 32.3 %all_to_all.10.own_ref = bf16[8,400,128]{2,1,0:T(8,128)(2,1)S(1)} all-to-all(bf16[8,400,128]{2,1,0:T(8,128)(2,1)} %prepare.1), channel_id=1, replica_groups=mesh['x'=4,'z'=8,'core'=2,'head'=4] {'z'}, dimensions={0} | all-to-all | bytes 1638400 | tf_op jit(solution)/shard_map/all_to_all | solution.py:358
  35.3 0.1 collective-permute-start.1
  35.4 3.1 %collective-permute-start = (bf16[8,272,128]{2,1,0:T(8,128)(2,1)S(1)}, bf16[8,272,128]{2,1,0:T(8,128)(2,1)S(1)}, u32[]{:S(2)}, u32[]{:S(2)}) collective-permute-start(bf16[8,272,128]{2,1,0:T(8,128)(2,1)S(1)} %slice.12), channel_id=1, source_target_pairs={{0,64},{64,128},{128,192},{1,65},{65,129},{129,193},{2,66},{66,130... | collective-permute-start | bytes 1671176 | tf_op jit(solution)/shard_map/ppermute | solution.py:361
  38.6 2.2 %linear.1 = (f32[8,128,128]{2,1,0:T(8,128)S(1)}, f32[8,128,128]{2,1,0:T(8,128)S(1)}, f32[136,128]{1,0:T(8,128)S(1)}, bf16[8,128,128]{2,1,0:T(8,128)(2,1)S(1)}) custom-call(s32[3]{0:T(128)S(1)} %pad_add_fusion.info_ref, bf16[8,400,128]{2,1,0:T(8,128)(2,1)S(1)} %all_to_all.10.own_ref, bf16[8,272,128]{2,1,0:T(8,128)(2,1)S(1)} %collective-permute-done.1.other_ref, ...), custom_call_target="tpu_custom_call" | custom-call | tf_op jit(solution)/shard_map/linear/pallas_call | solution.py:367
  40.8 1.3 %collective-permute-start.3 = (f32[136,128]{1,0:T(8,128)S(1)}, f32[136,128]{1,0:T(8,128)S(1)}, u32[]{:S(2)}, u32[]{:S(2)}) collective-permute-start(f32[136,128]{1,0:T(8,128)S(1)} %get-tuple-element.43.state_ref), channel_id=1, source_target_pairs={{0,128},{64,192},{1,129},{65,193},{2,130},{66,194},{3,131},{67,195... | collective-permute-start | bytes 208904 | tf_op jit(solution)/shard_map/ppermute | solution.py:379
  42.1 1.9 %collective-permute-start.2 = (f32[136,128]{1,0:T(8,128)S(1)}, f32[136,128]{1,0:T(8,128)S(1)}, u32[]{:S(2)}, u32[]{:S(2)}) collective-permute-start(f32[136,128]{1,0:T(8,128)S(1)} %get-tuple-element.43.state_ref), channel_id=1, source_target_pairs={{0,64},{64,128},{128,192},{1,65},{65,129},{129,193},{2,66},{66,130... | collective-permute-start | bytes 208904 | tf_op jit(solution)/shard_map/ppermute | solution.py:378
  44.1 3.7 %own_window.1 = (f32[1024,128]{1,0:T(8,128)S(1)}, f32[1024,128]{1,0:T(8,128)S(1)}, f32[1024,128]{1,0:T(8,128)S(1)}) custom-call(s32[3]{0:T(128)S(1)} %pad_add_fusion.info_ref, bf16[8,400,128]{2,1,0:T(8,128)(2,1)S(1)} %all_to_all.10.own_ref, bf16[8,272,128]{2,1,0:T(8,128)(2,1)S(1)} %collective-permute-done.1.other_ref, ...), custom_call_target="tpu_custom_call" | custom-call | tf_op jit(solution)/shard_map/own_window/pallas_call | solution.py:380
  47.8 1.3 %collective-permute-start.5 = (bf16[8,272,128]{2,1,0:T(8,128)(2,1)S(1)}, bf16[8,272,128]{2,1,0:T(8,128)(2,1)S(1)}, u32[]{:S(2)}, u32[]{:S(2)}) collective-permute-start(bf16[8,272,128]{2,1,0:T(8,128)(2,1)S(1)} %slice.12), channel_id=1, source_target_pairs={{0,128},{64,192},{1,129},{65,193},{2,130},{66,194},{3,131},{67,195... | collective-permute-start | bytes 1671176 | tf_op jit(solution)/shard_map/ppermute | solution.py:384
  49.1 5.0 %collective-permute-done.3.far_ref = f32[136,128]{1,0:T(8,128)S(1)} collective-permute-done((f32[136,128]{1,0:T(8,128)S(1)}, f32[136,128]{1,0:T(8,128)S(1)}, u32[]{:S(2)}, u32[]{:S(2)}) %collective-permute-start.3) | collective-permute-done | bytes 69664 | tf_op jit(solution)/shard_map/ppermute | solution.py:379
  54.2 1.5 %collective-permute-done.2.near_ref = f32[136,128]{1,0:T(8,128)S(1)} collective-permute-done((f32[136,128]{1,0:T(8,128)S(1)}, f32[136,128]{1,0:T(8,128)S(1)}, u32[]{:S(2)}, u32[]{:S(2)}) %collective-permute-start.2) | collective-permute-done | bytes 69664 | tf_op jit(solution)/shard_map/ppermute | solution.py:378
  55.7 1.4 %enter.1 = (bf16[8,128,128]{2,1,0:T(8,128)(2,1)S(1)}, f32[8,128]{1,0:T(8,128)S(1)}, s32[8]{0:T(128)S(1)}) custom-call(s32[3]{0:T(128)S(1)} %pad_add_fusion.info_ref, bf16[8,400,128]{2,1,0:T(8,128)(2,1)S(1)} %all_to_all.10.own_ref, f32[8,128,128]{2,1,0:T(8,128)S(1)} %get-tuple-element.41.partial_ref, f32[8,128,128]{2,1,0:T(8,128)S(1)} %get-tuple-element.42.weight_ref, ...), custom_call_target="tpu_custom_call" | custom-call | tf_op jit(solution)/shard_map/enter/pallas_call | solution.py:386
  57.1 1.7 %collective-permute-start.4 = (f32[8,128]{1,0:T(8,128)S(1)}, f32[8,128]{1,0:T(8,128)S(1)}, u32[]{:S(2)}, u32[]{:S(2)}) collective-permute-start(f32[8,128]{1,0:T(8,128)S(1)} %get-tuple-element.57), channel_id=1, source_target_pairs={{0,1},{1,0},{2,3},{3,2},{4,5},{5,4},{6,7},{7,6},{8,9},{9,8},{10,11... | collective-permute-start | bytes 12296 | tf_op jit(solution)/shard_map/ppermute | solution.py:393
  58.8 2.0 %collective-permute-done.4 = f32[8,128]{1,0:T(8,128)S(1)} collective-permute-done((f32[8,128]{1,0:T(8,128)S(1)}, f32[8,128]{1,0:T(8,128)S(1)}, u32[]{:S(2)}, u32[]{:S(2)}) %collective-permute-start.4) | collective-permute-done | bytes 4128 | tf_op jit(solution)/shard_map/ppermute | solution.py:393
  60.9 0.1 collective-permute-start.7
  61.0 0.5 collective-permute-start.6
  61.5 3.2 %collective-permute-start.8 = (f32[8,128]{1,0:T(8,128)S(1)}, f32[8,128]{1,0:T(8,128)S(1)}, u32[]{:S(2)}, u32[]{:S(2)}) collective-permute-start(f32[8,128]{1,0:T(8,128)S(1)} %add.10), channel_id=1, source_target_pairs={{0,2},{1,3},{2,0},{3,1},{4,6},{5,7},{6,4},{7,5},{8,10},{9,11},{10,... | collective-permute-start | bytes 12296 | tf_op jit(solution)/shard_map/ppermute | solution.py:395
  64.7 1.9 %collective-permute-done.8 = f32[8,128]{1,0:T(8,128)S(1)} collective-permute-done((f32[8,128]{1,0:T(8,128)S(1)}, f32[8,128]{1,0:T(8,128)S(1)}, u32[]{:S(2)}, u32[]{:S(2)}) %collective-permute-start.8) | collective-permute-done | bytes 4128 | tf_op jit(solution)/shard_map/ppermute | solution.py:395
  66.6 7.4 %near_window.1 = (f32[1024,128]{1,0:T(8,128)S(1)}, f32[1024,128]{1,0:T(8,128)S(1)}, f32[1024,128]{1,0:T(8,128)S(1)}) custom-call(s32[8]{0:T(128)S(1)} %get-tuple-element.58.need_ref, bf16[8,400,128]{2,1,0:T(8,128)(2,1)S(1)} %all_to_all.10.own_ref, bf16[8,128,128]{2,1,0:T(8,128)(2,1)S(1)} %get-tuple-element.44.mark_ref, ...), custom_call_target="tpu_custom_call" | custom-call | tf_op jit(solution)/shard_map/near_window/pallas_call | solution.py:397
  74.0 0.1 collective-permute-start.9
  74.1 3.1 %far_own.1 = (f32[1024,128]{1,0:T(8,128)S(1)}, f32[1024,128]{1,0:T(8,128)S(1)}, f32[1024,128]{1,0:T(8,128)S(1)}) custom-call(s32[3]{0:T(128)S(1)} %pad_add_fusion.info_ref, s32[8]{0:T(128)S(1)} %get-tuple-element.58.need_ref, bf16[8,400,128]{2,1,0:T(8,128)(2,1)S(1)} %all_to_all.10.own_ref, bf16[8,128,128]{2,1,0:T(8,128)(2,1)S(1)} %get-tuple-element.44.mark_ref, ...), custom_call_target="tpu_custom_call" | custom-call | tf_op jit(solution)/shard_map/far_own/pallas_call | solution.py:402
  77.2 3.2 %far_other.1 = bf16[8,272,128]{2,1,0:T(8,128)(2,1)S(1)} custom-call(s32[3]{0:T(128)S(1)} %pad_add_fusion.info_ref, s32[8]{0:T(128)S(1)} %get-tuple-element.58.need_ref, bf16[8,400,128]{2,1,0:T(8,128)(2,1)S(1)} %all_to_all.10.own_ref, bf16[8,128,128]{2,1,0:T(8,128)(2,1)S(1)} %get-tuple-element.44.mark_ref, ...), custom_call_target="tpu_custom_call" | custom-call | tf_op jit(solution)/shard_map/far_other/pallas_call | solution.py:403
  80.4 21.5 %all_to_all.11.got_ref = bf16[8,272,128]{2,1,0:T(8,128)(2,1)S(1)} all-to-all(bf16[8,272,128]{2,1,0:T(8,128)(2,1)S(1)} %far_other.1), channel_id=1, replica_groups=mesh['x'=4,'z'=8,'core'=2,'head'=4] {'z'}, dimensions={0} | all-to-all | bytes 1114112 | tf_op jit(solution)/shard_map/all_to_all | solution.py:410
  101.9 0.9 finish.1
  (16 shorter events, 0.2 us)
Async XLA Ops:
  0.0 38.6 %copy-start = (f32[8,128,128]{2,1,0:T(8,128)S(1)}, f32[8,128,128]{2,1,0:T(8,128)}, u32[]{:S(2)}) copy-start(f32[8,128,128]{2,1,0:T(8,128)} %param.13) | copy-start | bytes 1572868
  35.3 3.3 %collective-permute-start.1 = (bf16[8,272,128]{2,1,0:T(8,128)(2,1)S(1)}, bf16[8,272,128]{2,1,0:T(8,128)(2,1)S(1)}, u32[]{:S(2)}, u32[]{:S(2)}) collective-permute-start(bf16[8,272,128]{2,1,0:T(8,128)(2,1)S(1)} %slice.12), channel_id=1, source_target_pairs={{0,4},{4,0},{1,5},{5,1},{2,6},{6,2},{3,7},{7,3},{8,12},{12,8},{9,1... | collective-permute-start | bytes 1671176 | tf_op jit(solution)/shard_map/ppermute | solution.py:362
  35.4 25.5 %collective-permute-start = (bf16[8,272,128]{2,1,0:T(8,128)(2,1)S(1)}, bf16[8,272,128]{2,1,0:T(8,128)(2,1)S(1)}, u32[]{:S(2)}, u32[]{:S(2)}) collective-permute-start(bf16[8,272,128]{2,1,0:T(8,128)(2,1)S(1)} %slice.12), channel_id=1, source_target_pairs={{0,64},{64,128},{128,192},{1,65},{65,129},{129,193},{2,66},{66,130... | collective-permute-start | bytes 1671176 | tf_op jit(solution)/shard_map/ppermute | solution.py:361
  40.8 13.3 %collective-permute-start.3 = (f32[136,128]{1,0:T(8,128)S(1)}, f32[136,128]{1,0:T(8,128)S(1)}, u32[]{:S(2)}, u32[]{:S(2)}) collective-permute-start(f32[136,128]{1,0:T(8,128)S(1)} %get-tuple-element.43.state_ref), channel_id=1, source_target_pairs={{0,128},{64,192},{1,129},{65,193},{2,130},{66,194},{3,131},{67,195... | collective-permute-start | bytes 208904 | tf_op jit(solution)/shard_map/ppermute | solution.py:379
  42.1 13.5 %collective-permute-start.2 = (f32[136,128]{1,0:T(8,128)S(1)}, f32[136,128]{1,0:T(8,128)S(1)}, u32[]{:S(2)}, u32[]{:S(2)}) collective-permute-start(f32[136,128]{1,0:T(8,128)S(1)} %get-tuple-element.43.state_ref), channel_id=1, source_target_pairs={{0,64},{64,128},{128,192},{1,65},{65,129},{129,193},{2,66},{66,130... | collective-permute-start | bytes 208904 | tf_op jit(solution)/shard_map/ppermute | solution.py:378
  47.8 26.2 %collective-permute-start.5 = (bf16[8,272,128]{2,1,0:T(8,128)(2,1)S(1)}, bf16[8,272,128]{2,1,0:T(8,128)(2,1)S(1)}, u32[]{:S(2)}, u32[]{:S(2)}) collective-permute-start(bf16[8,272,128]{2,1,0:T(8,128)(2,1)S(1)} %slice.12), channel_id=1, source_target_pairs={{0,128},{64,192},{1,129},{65,193},{2,130},{66,194},{3,131},{67,195... | collective-permute-start | bytes 1671176 | tf_op jit(solution)/shard_map/ppermute | solution.py:384
  57.1 3.7 %collective-permute-start.4 = (f32[8,128]{1,0:T(8,128)S(1)}, f32[8,128]{1,0:T(8,128)S(1)}, u32[]{:S(2)}, u32[]{:S(2)}) collective-permute-start(f32[8,128]{1,0:T(8,128)S(1)} %get-tuple-element.57), channel_id=1, source_target_pairs={{0,1},{1,0},{2,3},{3,2},{4,5},{5,4},{6,7},{7,6},{8,9},{9,8},{10,11... | collective-permute-start | bytes 12296 | tf_op jit(solution)/shard_map/ppermute | solution.py:393
  60.9 5.7 %collective-permute-start.7 = (bf16[4,272,128]{2,1,0:T(8,128)(2,1)S(1)}, bf16[4,272,128]{2,1,0:T(8,128)(2,1)S(1)}, u32[]{:S(2)}, u32[]{:S(2)}) collective-permute-start(bf16[4,272,128]{2,1,0:T(8,128)(2,1)S(1)} %get-tuple-element.77), channel_id=1, source_target_pairs={{0,4},{4,0},{1,5},{5,1},{2,6},{6,2},{3,7},{7,3},{8,12},{12,8},{9,1... | collective-permute-start | bytes 835592 | tf_op jit(solution)/shard_map/ppermute | solution.py:396
  61.0 5.6 %collective-permute-start.6 = (bf16[4,272,128]{2,1,0:T(8,128)(2,1)S(1)}, bf16[4,272,128]{2,1,0:T(8,128)(2,1)S(1)}, u32[]{:S(2)}, u32[]{:S(2)}) collective-permute-start(bf16[4,272,128]{2,1,0:T(8,128)(2,1)S(1)} %get-tuple-element.78), channel_id=1, source_target_pairs={{0,4},{4,0},{1,5},{5,1},{2,6},{6,2},{3,7},{7,3},{8,12},{12,8},{9,1... | collective-permute-start | bytes 835592 | tf_op jit(solution)/shard_map/ppermute | solution.py:396
  61.5 5.1 %collective-permute-start.8 = (f32[8,128]{1,0:T(8,128)S(1)}, f32[8,128]{1,0:T(8,128)S(1)}, u32[]{:S(2)}, u32[]{:S(2)}) collective-permute-start(f32[8,128]{1,0:T(8,128)S(1)} %add.10), channel_id=1, source_target_pairs={{0,2},{1,3},{2,0},{3,1},{4,6},{5,7},{6,4},{7,5},{8,10},{9,11},{10,... | collective-permute-start | bytes 12296 | tf_op jit(solution)/shard_map/ppermute | solution.py:395
  74.0 3.2 %collective-permute-start.9 = (bf16[8,272,128]{2,1,0:T(8,128)(2,1)S(1)}, bf16[8,272,128]{2,1,0:T(8,128)(2,1)S(1)}, u32[]{:S(2)}, u32[]{:S(2)}) collective-permute-start(bf16[8,272,128]{2,1,0:T(8,128)(2,1)S(1)} %collective-permute-done.5.far_ref), channel_id=1, source_target_pairs={{0,4},{4,0},{1,5},{5,1},{2,6},{6,2},{3,7},{7,3},{8,12},{12,8},{9,1... | collective-permute-start | bytes 1671176 | tf_op jit(solution)/shard_map/ppermute | solution.py:401
  80.4 21.5 %copy-start.1 = (f32[1024]{0:T(1024)S(1)}, f32[1024]{0:T(1024)}, u32[]{:S(2)}) copy-start(f32[1024]{0:T(1024)} %param.14) | copy-start | bytes 12292

commit v5 on v4

--- a/solution.py
+++ b/solution.py
@@ -391,13 +391,13 @@
         outs=[VMEM, VMEM, SMEM],
     )(info, own, partial, weight, state, near_state, far_state)
     square = square + lax.ppermute(square, "head", [(i, i ^ 1) for i in range(4)])
-    near, need, own_part, square = lax.optimization_barrier((near, need, own_part, square))
-    square = square + lax.ppermute(square, "head", [(i, i ^ 2) for i in range(4)])
+    near, own_part = lax.optimization_barrier((near, own_part))
     near_other = [lax.ppermute(near[at : at + TILES], "core", pair) for at in (0, TILES)]
     part = call(near_kernel, "near_window", [SMEM] + [VMEM] * 8, part_shapes)(
         need, own, mark, near, *near_other, *own_part
     )
     far, part, square = lax.optimization_barrier((far, part, square))
+    square = square + lax.ppermute(square, "head", [(i, i ^ 2) for i in range(4)])
     far_other = lax.ppermute(far, "core", pair)
     part = call(far_own_kernel, "far_own", [SMEM] * 2 + [VMEM] * 6, part_shapes)(info, need, own, mark, far, *part)
     mixed = call(

time: 102 us -> 99.4 us (0.975)
  waiting for transfers between devices: 10.5 us -> 8.63 us
  blocking collectives: 53.8 us -> 52.7 us
    ppermute x1, waiting for transfers between devices: 1.92 us -> 0.01 us  [body(): lax.ppermute(square, 'head', [(i, i ^ 2) for i in range(4)])]
    all_to_all x1, blocking collectives: 21.5 us -> 20.4 us  [body(): back = lax.all_to_all(mixed, 'z', 0, 0, tiled=True)]
  transfers between devices with their start and end apart: 10 -> 10, of which waited for: 4 -> 3; matrix products, arithmetic and copies ran while one was open for 0% -> 0% of each run, Pallas kernels for 17% -> 18%
where the time goes in v5:
time: 99.4 us; the launch traced here: 99.8 us
  blocking collectives  52.7 us (53%)
  Pallas kernels  24.8 us (25%)
  starting transfers between devices  13.3 us (13%)
  waiting for transfers between devices  8.63 us (9%)
    all_to_all x1, blocking collectives, body(): own = lax.all_to_all(packed, 'z', 0, 0, tiled=True)  32.3 us
    all_to_all x1, blocking collectives, body(): back = lax.all_to_all(mixed, 'z', 0, 0, tiled=True)  20.4 us
    pallas_call x1, Pallas kernels, body(): call(near_kernel, 'near_window', [SMEM] + [VMEM] * 8, part_shapes)  7.34 us
    ppermute x1, waiting for transfers between devices, body(): far_state = lax.ppermute(state, 'x', [(0, 2), (1, 3)])  5.05 us
    pallas_call x1, Pallas kernels, body(): call(own_window_kernel, 'own_window', [SMEM] + [VMEM] * 3, part_shapes)  3.74 us
    ppermute x1, starting transfers between devices, body(): lax.ppermute(square, 'head', [(i, i ^ 2) for i in range(4)])  3.27 us
    pallas_call x1, Pallas kernels, body(): call(far_other_kernel, 'far_other', [SMEM] * 2 + [VMEM] * 8, shape((HEADS...  3.2 us
    ppermute x1, starting transfers between devices, body(): near = lax.ppermute(sent, 'x', [(0, 1), (1, 2), (2, 3)])  3.11 us
  transfers between devices with their start and end apart: 10, of which 3 were waited for; matrix products, arithmetic and copies ran while one was open for 0% of the time, Pallas kernels for 18%

profile of v5, /device:TPU:4, one launch (start us, length us, event | category | flops | bytes accessed | tf_op | source)
XLA Modules:
  0.0 99.8 jit_solution(8088804934279422315)
XLA Ops:
  0.0 2.9 %prepare.1 = bf16[8,400,128]{2,1,0:T(8,128)(2,1)} custom-call(f32[16]{0:T(128)} %table_ref.1, s32[8]{0:T(128)} %index_ref.1, bf16[128,1024]{1,0:T(8,128)(2,1)} %q_hbm.1, bf16[128,1024]{1,0:T(8,128)(2,1)} %k_hbm.1, bf16[128,1024]{1,0:T(8,128)(2,1)} %v_hbm.1, f32[8,128]{1,0:T(8,128)} %bitcast.8, f32[8,128]{1,0:T(8,128)} %bitcast.9, s32[1,128]{1,0:T(1,128)} %bitcast.10), custom_call_target="tpu_custom_call" | custom-call | tf_op jit(solution)/shard_map/prepare/pallas_call | solution.py:351
  2.9 32.3 %all_to_all.10.own_ref = bf16[8,400,128]{2,1,0:T(8,128)(2,1)S(1)} all-to-all(bf16[8,400,128]{2,1,0:T(8,128)(2,1)} %prepare.1), channel_id=1, replica_groups=mesh['x'=4,'z'=8,'core'=2,'head'=4] {'z'}, dimensions={0} | all-to-all | bytes 1638400 | tf_op jit(solution)/shard_map/all_to_all | solution.py:358
  35.3 0.1 collective-permute-start
  35.4 3.1 %collective-permute-start.4 = (bf16[8,272,128]{2,1,0:T(8,128)(2,1)S(1)}, bf16[8,272,128]{2,1,0:T(8,128)(2,1)S(1)}, u32[]{:S(2)}, u32[]{:S(2)}) collective-permute-start(bf16[8,272,128]{2,1,0:T(8,128)(2,1)S(1)} %slice.12), channel_id=1, source_target_pairs={{0,64},{64,128},{128,192},{1,65},{65,129},{129,193},{2,66},{66,130... | collective-permute-start | bytes 1671176 | tf_op jit(solution)/shard_map/ppermute | solution.py:361
  38.5 0.1 pad_add_fusion.info_ref
  38.6 2.2 %linear.1 = (f32[8,128,128]{2,1,0:T(8,128)S(1)}, f32[8,128,128]{2,1,0:T(8,128)S(1)}, f32[136,128]{1,0:T(8,128)S(1)}, bf16[8,128,128]{2,1,0:T(8,128)(2,1)S(1)}) custom-call(s32[3]{0:T(128)S(1)} %pad_add_fusion.info_ref, bf16[8,400,128]{2,1,0:T(8,128)(2,1)S(1)} %all_to_all.10.own_ref, bf16[8,272,128]{2,1,0:T(8,128)(2,1)S(1)} %collective-permute-done.other_ref, ...), custom_call_target="tpu_custom_call" | custom-call | tf_op jit(solution)/shard_map/linear/pallas_call | solution.py:367
  40.8 1.3 %collective-permute-start.2 = (f32[136,128]{1,0:T(8,128)S(1)}, f32[136,128]{1,0:T(8,128)S(1)}, u32[]{:S(2)}, u32[]{:S(2)}) collective-permute-start(f32[136,128]{1,0:T(8,128)S(1)} %get-tuple-element.41.state_ref), channel_id=1, source_target_pairs={{0,128},{64,192},{1,129},{65,193},{2,130},{66,194},{3,131},{67,195... | collective-permute-start | bytes 208904 | tf_op jit(solution)/shard_map/ppermute | solution.py:379
  42.1 1.9 %collective-permute-start.1 = (f32[136,128]{1,0:T(8,128)S(1)}, f32[136,128]{1,0:T(8,128)S(1)}, u32[]{:S(2)}, u32[]{:S(2)}) collective-permute-start(f32[136,128]{1,0:T(8,128)S(1)} %get-tuple-element.41.state_ref), channel_id=1, source_target_pairs={{0,64},{64,128},{128,192},{1,65},{65,129},{129,193},{2,66},{66,130... | collective-permute-start | bytes 208904 | tf_op jit(solution)/shard_map/ppermute | solution.py:378
  44.1 3.7 %own_window.1 = (f32[1024,128]{1,0:T(8,128)S(1)}, f32[1024,128]{1,0:T(8,128)S(1)}, f32[1024,128]{1,0:T(8,128)S(1)}) custom-call(s32[3]{0:T(128)S(1)} %pad_add_fusion.info_ref, bf16[8,400,128]{2,1,0:T(8,128)(2,1)S(1)} %all_to_all.10.own_ref, bf16[8,272,128]{2,1,0:T(8,128)(2,1)S(1)} %collective-permute-done.other_ref, ...), custom_call_target="tpu_custom_call" | custom-call | tf_op jit(solution)/shard_map/own_window/pallas_call | solution.py:380
  47.8 1.3 %collective-permute-start.3 = (bf16[8,272,128]{2,1,0:T(8,128)(2,1)S(1)}, bf16[8,272,128]{2,1,0:T(8,128)(2,1)S(1)}, u32[]{:S(2)}, u32[]{:S(2)}) collective-permute-start(bf16[8,272,128]{2,1,0:T(8,128)(2,1)S(1)} %slice.12), channel_id=1, source_target_pairs={{0,128},{64,192},{1,129},{65,193},{2,130},{66,194},{3,131},{67,195... | collective-permute-start | bytes 1671176 | tf_op jit(solution)/shard_map/ppermute | solution.py:384
  49.1 5.0 %collective-permute-done.2.far_ref = f32[136,128]{1,0:T(8,128)S(1)} collective-permute-done((f32[136,128]{1,0:T(8,128)S(1)}, f32[136,128]{1,0:T(8,128)S(1)}, u32[]{:S(2)}, u32[]{:S(2)}) %collective-permute-start.2) | collective-permute-done | bytes 69664 | tf_op jit(solution)/shard_map/ppermute | solution.py:379
  54.2 1.5 %collective-permute-done.1.near_ref = f32[136,128]{1,0:T(8,128)S(1)} collective-permute-done((f32[136,128]{1,0:T(8,128)S(1)}, f32[136,128]{1,0:T(8,128)S(1)}, u32[]{:S(2)}, u32[]{:S(2)}) %collective-permute-start.1) | collective-permute-done | bytes 69664 | tf_op jit(solution)/shard_map/ppermute | solution.py:378
  55.7 0.1 collective-permute-start.6
  55.8 0.5 collective-permute-start.5
  56.3 1.4 %enter.1 = (bf16[8,128,128]{2,1,0:T(8,128)(2,1)S(1)}, f32[8,128]{1,0:T(8,128)S(1)}, s32[8]{0:T(128)S(1)}) custom-call(s32[3]{0:T(128)S(1)} %pad_add_fusion.info_ref, bf16[8,400,128]{2,1,0:T(8,128)(2,1)S(1)} %all_to_all.10.own_ref, f32[8,128,128]{2,1,0:T(8,128)S(1)} %get-tuple-element.39.partial_ref, f32[8,128,128]{2,1,0:T(8,128)S(1)} %get-tuple-element.40.weight_ref, ...), custom_call_target="tpu_custom_call" | custom-call | tf_op jit(solution)/shard_map/enter/pallas_call | solution.py:386
  57.8 1.7 %collective-permute-start.7 = (f32[8,128]{1,0:T(8,128)S(1)}, f32[8,128]{1,0:T(8,128)S(1)}, u32[]{:S(2)}, u32[]{:S(2)}) collective-permute-start(f32[8,128]{1,0:T(8,128)S(1)} %get-tuple-element.63), channel_id=1, source_target_pairs={{0,1},{1,0},{2,3},{3,2},{4,5},{5,4},{6,7},{7,6},{8,9},{9,8},{10,11... | collective-permute-start | bytes 12296 | tf_op jit(solution)/shard_map/ppermute | solution.py:393
  59.4 2.0 %collective-permute-done.7 = f32[8,128]{1,0:T(8,128)S(1)} collective-permute-done((f32[8,128]{1,0:T(8,128)S(1)}, f32[8,128]{1,0:T(8,128)S(1)}, u32[]{:S(2)}, u32[]{:S(2)}) %collective-permute-start.7) | collective-permute-done | bytes 4128 | tf_op jit(solution)/shard_map/ppermute | solution.py:393
  61.5 7.3 %near_window.1 = (f32[1024,128]{1,0:T(8,128)S(1)}, f32[1024,128]{1,0:T(8,128)S(1)}, f32[1024,128]{1,0:T(8,128)S(1)}) custom-call(s32[8]{0:T(128)S(1)} %get-tuple-element.51.need_ref, bf16[8,400,128]{2,1,0:T(8,128)(2,1)S(1)} %all_to_all.10.own_ref, bf16[8,128,128]{2,1,0:T(8,128)(2,1)S(1)} %get-tuple-element.42.mark_ref, ...), custom_call_target="tpu_custom_call" | custom-call | tf_op jit(solution)/shard_map/near_window/pallas_call | solution.py:396
  68.8 0.1 collective-permute-start.8
  68.9 3.3 %collective-permute-start.9 = (f32[8,128]{1,0:T(8,128)S(1)}, f32[8,128]{1,0:T(8,128)S(1)}, u32[]{:S(2)}, u32[]{:S(2)}) collective-permute-start(f32[8,128]{1,0:T(8,128)S(1)} %add.10), channel_id=1, source_target_pairs={{0,2},{1,3},{2,0},{3,1},{4,6},{5,7},{6,4},{7,5},{8,10},{9,11},{10,... | collective-permute-start | bytes 12296 | tf_op jit(solution)/shard_map/ppermute | solution.py:400
  72.2 3.1 %far_own.1 = (f32[1024,128]{1,0:T(8,128)S(1)}, f32[1024,128]{1,0:T(8,128)S(1)}, f32[1024,128]{1,0:T(8,128)S(1)}) custom-call(s32[3]{0:T(128)S(1)} %pad_add_fusion.info_ref, s32[8]{0:T(128)S(1)} %get-tuple-element.51.need_ref, bf16[8,400,128]{2,1,0:T(8,128)(2,1)S(1)} %all_to_all.10.own_ref, bf16[8,128,128]{2,1,0:T(8,128)(2,1)S(1)} %get-tuple-element.42.mark_ref, ...), custom_call_target="tpu_custom_call" | custom-call | tf_op jit(solution)/shard_map/far_own/pallas_call | solution.py:402
  75.3 3.2 %far_other.1 = bf16[8,272,128]{2,1,0:T(8,128)(2,1)S(1)} custom-call(s32[3]{0:T(128)S(1)} %pad_add_fusion.info_ref, s32[8]{0:T(128)S(1)} %get-tuple-element.51.need_ref, bf16[8,400,128]{2,1,0:T(8,128)(2,1)S(1)} %all_to_all.10.own_ref, bf16[8,128,128]{2,1,0:T(8,128)(2,1)S(1)} %get-tuple-element.42.mark_ref, ...), custom_call_target="tpu_custom_call" | custom-call | tf_op jit(solution)/shard_map/far_other/pallas_call | solution.py:403
  78.6 20.4 %all_to_all.11.got_ref = bf16[8,272,128]{2,1,0:T(8,128)(2,1)S(1)} all-to-all(bf16[8,272,128]{2,1,0:T(8,128)(2,1)S(1)} %far_other.1), channel_id=1, replica_groups=mesh['x'=4,'z'=8,'core'=2,'head'=4] {'z'}, dimensions={0} | all-to-all | bytes 1114112 | tf_op jit(solution)/shard_map/all_to_all | solution.py:410
  99.0 0.9 finish.1
  (16 shorter events, 0.1 us)
Async XLA Ops:
  0.0 38.6 %copy-start = (f32[8,128,128]{2,1,0:T(8,128)S(1)}, f32[8,128,128]{2,1,0:T(8,128)}, u32[]{:S(2)}) copy-start(f32[8,128,128]{2,1,0:T(8,128)} %param.13) | copy-start | bytes 1572868
  35.3 3.3 %collective-permute-start = (bf16[8,272,128]{2,1,0:T(8,128)(2,1)S(1)}, bf16[8,272,128]{2,1,0:T(8,128)(2,1)S(1)}, u32[]{:S(2)}, u32[]{:S(2)}) collective-permute-start(bf16[8,272,128]{2,1,0:T(8,128)(2,1)S(1)} %slice.12), channel_id=1, source_target_pairs={{0,4},{4,0},{1,5},{5,1},{2,6},{6,2},{3,7},{7,3},{8,12},{12,8},{9,1... | collective-permute-start | bytes 1671176 | tf_op jit(solution)/shard_map/ppermute | solution.py:362
  35.4 20.3 %collective-permute-start.4 = (bf16[8,272,128]{2,1,0:T(8,128)(2,1)S(1)}, bf16[8,272,128]{2,1,0:T(8,128)(2,1)S(1)}, u32[]{:S(2)}, u32[]{:S(2)}) collective-permute-start(bf16[8,272,128]{2,1,0:T(8,128)(2,1)S(1)} %slice.12), channel_id=1, source_target_pairs={{0,64},{64,128},{128,192},{1,65},{65,129},{129,193},{2,66},{66,130... | collective-permute-start | bytes 1671176 | tf_op jit(solution)/shard_map/ppermute | solution.py:361
  40.8 13.3 %collective-permute-start.2 = (f32[136,128]{1,0:T(8,128)S(1)}, f32[136,128]{1,0:T(8,128)S(1)}, u32[]{:S(2)}, u32[]{:S(2)}) collective-permute-start(f32[136,128]{1,0:T(8,128)S(1)} %get-tuple-element.41.state_ref), channel_id=1, source_target_pairs={{0,128},{64,192},{1,129},{65,193},{2,130},{66,194},{3,131},{67,195... | collective-permute-start | bytes 208904 | tf_op jit(solution)/shard_map/ppermute | solution.py:379
  42.1 13.5 %collective-permute-start.1 = (f32[136,128]{1,0:T(8,128)S(1)}, f32[136,128]{1,0:T(8,128)S(1)}, u32[]{:S(2)}, u32[]{:S(2)}) collective-permute-start(f32[136,128]{1,0:T(8,128)S(1)} %get-tuple-element.41.state_ref), channel_id=1, source_target_pairs={{0,64},{64,128},{128,192},{1,65},{65,129},{129,193},{2,66},{66,130... | collective-permute-start | bytes 208904 | tf_op jit(solution)/shard_map/ppermute | solution.py:378
  47.8 21.0 %collective-permute-start.3 = (bf16[8,272,128]{2,1,0:T(8,128)(2,1)S(1)}, bf16[8,272,128]{2,1,0:T(8,128)(2,1)S(1)}, u32[]{:S(2)}, u32[]{:S(2)}) collective-permute-start(bf16[8,272,128]{2,1,0:T(8,128)(2,1)S(1)} %slice.12), channel_id=1, source_target_pairs={{0,128},{64,192},{1,129},{65,193},{2,130},{66,194},{3,131},{67,195... | collective-permute-start | bytes 1671176 | tf_op jit(solution)/shard_map/ppermute | solution.py:384
  55.7 5.7 %collective-permute-start.6 = (bf16[4,272,128]{2,1,0:T(8,128)(2,1)S(1)}, bf16[4,272,128]{2,1,0:T(8,128)(2,1)S(1)}, u32[]{:S(2)}, u32[]{:S(2)}) collective-permute-start(bf16[4,272,128]{2,1,0:T(8,128)(2,1)S(1)} %get-tuple-element.73), channel_id=1, source_target_pairs={{0,4},{4,0},{1,5},{5,1},{2,6},{6,2},{3,7},{7,3},{8,12},{12,8},{9,1... | collective-permute-start | bytes 835592 | tf_op jit(solution)/shard_map/ppermute | solution.py:395
  55.8 5.6 %collective-permute-start.5 = (bf16[4,272,128]{2,1,0:T(8,128)(2,1)S(1)}, bf16[4,272,128]{2,1,0:T(8,128)(2,1)S(1)}, u32[]{:S(2)}, u32[]{:S(2)}) collective-permute-start(bf16[4,272,128]{2,1,0:T(8,128)(2,1)S(1)} %get-tuple-element.74), channel_id=1, source_target_pairs={{0,4},{4,0},{1,5},{5,1},{2,6},{6,2},{3,7},{7,3},{8,12},{12,8},{9,1... | collective-permute-start | bytes 835592 | tf_op jit(solution)/shard_map/ppermute | solution.py:395
  57.8 3.7 %collective-permute-start.7 = (f32[8,128]{1,0:T(8,128)S(1)}, f32[8,128]{1,0:T(8,128)S(1)}, u32[]{:S(2)}, u32[]{:S(2)}) collective-permute-start(f32[8,128]{1,0:T(8,128)S(1)} %get-tuple-element.63), channel_id=1, source_target_pairs={{0,1},{1,0},{2,3},{3,2},{4,5},{5,4},{6,7},{7,6},{8,9},{9,8},{10,11... | collective-permute-start | bytes 12296 | tf_op jit(solution)/shard_map/ppermute | solution.py:393
  68.8 6.5 %collective-permute-start.8 = (bf16[8,272,128]{2,1,0:T(8,128)(2,1)S(1)}, bf16[8,272,128]{2,1,0:T(8,128)(2,1)S(1)}, u32[]{:S(2)}, u32[]{:S(2)}) collective-permute-start(bf16[8,272,128]{2,1,0:T(8,128)(2,1)S(1)} %collective-permute-done.3.far_ref), channel_id=1, source_target_pairs={{0,4},{4,0},{1,5},{5,1},{2,6},{6,2},{3,7},{7,3},{8,12},{12,8},{9,1... | collective-permute-start | bytes 1671176 | tf_op jit(solution)/shard_map/ppermute | solution.py:401
  68.9 6.4 %collective-permute-start.9 = (f32[8,128]{1,0:T(8,128)S(1)}, f32[8,128]{1,0:T(8,128)S(1)}, u32[]{:S(2)}, u32[]{:S(2)}) collective-permute-start(f32[8,128]{1,0:T(8,128)S(1)} %add.10), channel_id=1, source_target_pairs={{0,2},{1,3},{2,0},{3,1},{4,6},{5,7},{6,4},{7,5},{8,10},{9,11},{10,... | collective-permute-start | bytes 12296 | tf_op jit(solution)/shard_map/ppermute | solution.py:400
  78.5 20.4 %copy-start.1 = (f32[1024]{0:T(1024)S(1)}, f32[1024]{0:T(1024)}, u32[]{:S(2)}) copy-start(f32[1024]{0:T(1024)} %param.14) | copy-start | bytes 12292

commit v6 on v5

--- a/solution.py
+++ b/solution.py
@@ -187,14 +187,14 @@
     return jnp.concatenate([queries, marks], axis=1)
 
 
-def absorb(queries, ref, pieces, diagonal, old):
+def absorb(queries, pieces, old):
     scores = []
     top = None
-    for m in pieces:
+    for ref, m, mask in pieces:
         keys = jnp.concatenate([ref[2 * m, 0:VALUE_AT, :], ref[2 * m + 1, 0:VALUE_AT, :]], axis=1)
         score = dot(queries, keys)
-        if m == diagonal[0]:
-            score = jnp.where(diagonal[1], score, LOW)
+        if mask is not None:
+            score = jnp.where(mask, score, LOW)
         scores.append(score)
         most = jnp.maximum(score[:, :TOK], score[:, TOK:])
         top = most if top is None else jnp.maximum(top, most)
@@ -203,7 +203,7 @@
         top = jnp.maximum(top, old[0])
     base = top * EXP2_SCALE
     sums, output = None, None
-    for m, score in zip(pieces, scores):
+    for (ref, m, _), score in zip(pieces, scores):
         weights = jnp.exp2(score * EXP2_SCALE - base)
         part = weights[:, :TOK] + weights[:, TOK:]
         sums = part if sums is None else sums + part
@@ -251,9 +251,12 @@
         masks.append(key <= at)
     for tile in range(TILES):
         queries = marked_queries(own_ref, mark_ref, tile)
-        part = absorb(queries, own_ref, range(tile + 1), (tile, masks[0]), None)
-        part = absorb(queries, other_ref, range(tile + 1), (tile, masks[1]), part)
-        store_part(refs, tile, part)
+        pieces = [
+            (ref, m, mask if m == tile else None)
+            for ref, mask in zip((own_ref, other_ref), masks)
+            for m in range(tile + 1)
+        ]
+        store_part(refs, tile, absorb(queries, pieces, None))
 
 
 def near_kernel(need_ref, own_ref, mark_ref, near_ref, other_ref, more_ref, a_ref, b_ref, c_ref, *refs):
@@ -264,9 +267,9 @@
         @pl.when(needed)
         def _(tile=tile):
             queries = marked_queries(own_ref, mark_ref, tile)
-            part = absorb(queries, near_ref, range(TILES), (None, None), load_part(olds, tile))
-            part = absorb(queries, other_ref, range(TILES // 2), (None, None), part)
-            store_part(refs, tile, absorb(queries, more_ref, range(TILES // 2), (None, None), part))
+            pieces = [(near_ref, m, None) for m in range(TILES)]
+            pieces += [(ref, m, None) for ref in (other_ref, more_ref) for m in range(TILES // 2)]
+            store_part(refs, tile, absorb(queries, pieces, load_part(olds, tile)))
 
         @pl.when(jnp.logical_not(needed))
         def _(tile=tile):
@@ -282,7 +285,8 @@
         @pl.when(needed)
         def _(tile=tile):
             queries = marked_queries(own_ref, mark_ref, tile)
-            store_part(refs, tile, absorb(queries, far_ref, range(tile, TILES), (tile, mask), load_part(olds, tile)))
+            pieces = [(far_ref, m, mask if m == tile else None) for m in range(tile, TILES)]
+            store_part(refs, tile, absorb(queries, pieces, load_part(olds, tile)))
 
         @pl.when(jnp.logical_not(needed))
         def _(tile=tile):
@@ -397,7 +401,7 @@
         need, own, mark, near, *near_other, *own_part
     )
     far, part, square = lax.optimization_barrier((far, part, square))
-    square = square + lax.ppermute(square, "head", [(i, i ^ 2) for i in range(4)])
+    square = square + lax.ppermute(square, "head", [(i, 3 - i) for i in range(4)])
     far_other = lax.ppermute(far, "core", pair)
     part = call(far_own_kernel, "far_own", [SMEM] * 2 + [VMEM] * 6, part_shapes)(info, need, own, mark, far, *part)
     mixed = call(

time: 99.4 us -> 98.6 us (level); the launches traced: 99.8 us -> 97.9 us
  Pallas kernels: 24.8 us -> 20.4 us
  waiting for transfers between devices: 8.63 us -> 10.7 us
    pallas_call x1, Pallas kernels: 7.34 us -> 4.28 us  [body(): call(near_kernel, 'near_window', [SMEM] + [VMEM] * 8, part_shapes)]
    ppermute x1, waiting for transfers between devices: 0.01 us -> 1.44 us  [body(): far = lax.ppermute(sent, 'x', [(0, 2), (1, 3)])]
  transfers between devices with their start and end apart: 10 -> 10, of which waited for: 3 -> 4; matrix products, arithmetic and copies ran while one was open for 0% -> 0% of each run, Pallas kernels for 18% -> 14%
where the time goes in v6:
time: 98.6 us; the launch traced here: 97.9 us
  blocking collectives  53.5 us (54%)
  Pallas kernels  20.4 us (21%)
  starting transfers between devices  13 us (13%)
  waiting for transfers between devices  10.7 us (11%)
    all_to_all x1, blocking collectives, body(): own = lax.all_to_all(packed, 'z', 0, 0, tiled=True)  32.3 us
    all_to_all x1, blocking collectives, body(): back = lax.all_to_all(mixed, 'z', 0, 0, tiled=True)  21.2 us
    ppermute x1, waiting for transfers between devices, body(): far_state = lax.ppermute(state, 'x', [(0, 2), (1, 3)])  5.67 us
    pallas_call x1, Pallas kernels, body(): call(near_kernel, 'near_window', [SMEM] + [VMEM] * 8, part_shapes)  4.28 us
    pallas_call x1, Pallas kernels, body(): call(own_window_kernel, 'own_window', [SMEM] + [VMEM] * 3, part_shapes)  3.11 us
    ppermute x1, starting transfers between devices, body(): near = lax.ppermute(sent, 'x', [(0, 1), (1, 2), (2, 3)])  3.11 us
    ppermute x1, starting transfers between devices, body(): lax.ppermute(square, 'head', [(i, 3 - i) for i in range(4)])  3.01 us
    pallas_call x1, Pallas kernels, body(): call(prepare_kernel, 'prepare', [SMEM, SMEM, HBM, HBM, HBM, VMEM, VMEM, V...  2.94 us
  transfers between devices with their start and end apart: 10, of which 4 were waited for; matrix products, arithmetic and copies ran while one was open for 0% of the time, Pallas kernels for 14%

profile of v6, /device:TPU:4, one launch (start us, length us, event | category | flops | bytes accessed | tf_op | source)
XLA Modules:
  0.0 97.9 jit_solution(10460712547635292744)
XLA Ops:
  0.0 2.9 %prepare.1 = bf16[8,400,128]{2,1,0:T(8,128)(2,1)} custom-call(f32[16]{0:T(128)} %table_ref.1, s32[8]{0:T(128)} %index_ref.1, bf16[128,1024]{1,0:T(8,128)(2,1)} %q_hbm.1, bf16[128,1024]{1,0:T(8,128)(2,1)} %k_hbm.1, bf16[128,1024]{1,0:T(8,128)(2,1)} %v_hbm.1, f32[8,128]{1,0:T(8,128)} %bitcast.8, f32[8,128]{1,0:T(8,128)} %bitcast.9, s32[1,128]{1,0:T(1,128)} %bitcast.10), custom_call_target="tpu_custom_call" | custom-call | tf_op jit(solution)/shard_map/prepare/pallas_call | solution.py:355
  2.9 32.3 %all_to_all.10.own_ref = bf16[8,400,128]{2,1,0:T(8,128)(2,1)S(1)} all-to-all(bf16[8,400,128]{2,1,0:T(8,128)(2,1)} %prepare.1), channel_id=1, replica_groups=mesh['x'=4,'z'=8,'core'=2,'head'=4] {'z'}, dimensions={0} | all-to-all | bytes 1638400 | tf_op jit(solution)/shard_map/all_to_all | solution.py:362
  35.3 0.1 collective-permute-start
  35.4 3.1 %collective-permute-start.4 = (bf16[8,272,128]{2,1,0:T(8,128)(2,1)S(1)}, bf16[8,272,128]{2,1,0:T(8,128)(2,1)S(1)}, u32[]{:S(2)}, u32[]{:S(2)}) collective-permute-start(bf16[8,272,128]{2,1,0:T(8,128)(2,1)S(1)} %slice.12), channel_id=1, source_target_pairs={{0,64},{64,128},{128,192},{1,65},{65,129},{129,193},{2,66},{66,130... | collective-permute-start | bytes 1671176 | tf_op jit(solution)/shard_map/ppermute | solution.py:365
  38.5 0.1 pad_add_fusion.info_ref
  38.6 2.2 %linear.1 = (f32[8,128,128]{2,1,0:T(8,128)S(1)}, f32[8,128,128]{2,1,0:T(8,128)S(1)}, f32[136,128]{1,0:T(8,128)S(1)}, bf16[8,128,128]{2,1,0:T(8,128)(2,1)S(1)}) custom-call(s32[3]{0:T(128)S(1)} %pad_add_fusion.info_ref, bf16[8,400,128]{2,1,0:T(8,128)(2,1)S(1)} %all_to_all.10.own_ref, bf16[8,272,128]{2,1,0:T(8,128)(2,1)S(1)} %collective-permute-done.other_ref, ...), custom_call_target="tpu_custom_call" | custom-call | tf_op jit(solution)/shard_map/linear/pallas_call | solution.py:371
  40.8 1.3 %collective-permute-start.2 = (f32[136,128]{1,0:T(8,128)S(1)}, f32[136,128]{1,0:T(8,128)S(1)}, u32[]{:S(2)}, u32[]{:S(2)}) collective-permute-start(f32[136,128]{1,0:T(8,128)S(1)} %get-tuple-element.41.state_ref), channel_id=1, source_target_pairs={{0,128},{64,192},{1,129},{65,193},{2,130},{66,194},{3,131},{67,195... | collective-permute-start | bytes 208904 | tf_op jit(solution)/shard_map/ppermute | solution.py:383
  42.1 1.9 %collective-permute-start.1 = (f32[136,128]{1,0:T(8,128)S(1)}, f32[136,128]{1,0:T(8,128)S(1)}, u32[]{:S(2)}, u32[]{:S(2)}) collective-permute-start(f32[136,128]{1,0:T(8,128)S(1)} %get-tuple-element.41.state_ref), channel_id=1, source_target_pairs={{0,64},{64,128},{128,192},{1,65},{65,129},{129,193},{2,66},{66,130... | collective-permute-start | bytes 208904 | tf_op jit(solution)/shard_map/ppermute | solution.py:382
  44.1 3.1 %own_window.1 = (f32[1024,128]{1,0:T(8,128)S(1)}, f32[1024,128]{1,0:T(8,128)S(1)}, f32[1024,128]{1,0:T(8,128)S(1)}) custom-call(s32[3]{0:T(128)S(1)} %pad_add_fusion.info_ref, bf16[8,400,128]{2,1,0:T(8,128)(2,1)S(1)} %all_to_all.10.own_ref, bf16[8,272,128]{2,1,0:T(8,128)(2,1)S(1)} %collective-permute-done.other_ref, ...), custom_call_target="tpu_custom_call" | custom-call | tf_op jit(solution)/shard_map/own_window/pallas_call | solution.py:384
  47.2 1.3 %collective-permute-start.3 = (bf16[8,272,128]{2,1,0:T(8,128)(2,1)S(1)}, bf16[8,272,128]{2,1,0:T(8,128)(2,1)S(1)}, u32[]{:S(2)}, u32[]{:S(2)}) collective-permute-start(bf16[8,272,128]{2,1,0:T(8,128)(2,1)S(1)} %slice.12), channel_id=1, source_target_pairs={{0,128},{64,192},{1,129},{65,193},{2,130},{66,194},{3,131},{67,195... | collective-permute-start | bytes 1671176 | tf_op jit(solution)/shard_map/ppermute | solution.py:388
  48.5 5.7 %collective-permute-done.2.far_ref = f32[136,128]{1,0:T(8,128)S(1)} collective-permute-done((f32[136,128]{1,0:T(8,128)S(1)}, f32[136,128]{1,0:T(8,128)S(1)}, u32[]{:S(2)}, u32[]{:S(2)}) %collective-permute-start.2) | collective-permute-done | bytes 69664 | tf_op jit(solution)/shard_map/ppermute | solution.py:383
  54.2 1.5 %collective-permute-done.1.near_ref = f32[136,128]{1,0:T(8,128)S(1)} collective-permute-done((f32[136,128]{1,0:T(8,128)S(1)}, f32[136,128]{1,0:T(8,128)S(1)}, u32[]{:S(2)}, u32[]{:S(2)}) %collective-permute-start.1) | collective-permute-done | bytes 69664 | tf_op jit(solution)/shard_map/ppermute | solution.py:382
  55.7 0.1 collective-permute-start.6
  55.8 0.5 collective-permute-start.5
  56.3 1.4 %enter.1 = (bf16[8,128,128]{2,1,0:T(8,128)(2,1)S(1)}, f32[8,128]{1,0:T(8,128)S(1)}, s32[8]{0:T(128)S(1)}) custom-call(s32[3]{0:T(128)S(1)} %pad_add_fusion.info_ref, bf16[8,400,128]{2,1,0:T(8,128)(2,1)S(1)} %all_to_all.10.own_ref, f32[8,128,128]{2,1,0:T(8,128)S(1)} %get-tuple-element.39.partial_ref, f32[8,128,128]{2,1,0:T(8,128)S(1)} %get-tuple-element.40.weight_ref, ...), custom_call_target="tpu_custom_call" | custom-call | tf_op jit(solution)/shard_map/enter/pallas_call | solution.py:390
  57.8 1.7 %collective-permute-start.7 = (f32[8,128]{1,0:T(8,128)S(1)}, f32[8,128]{1,0:T(8,128)S(1)}, u32[]{:S(2)}, u32[]{:S(2)}) collective-permute-start(f32[8,128]{1,0:T(8,128)S(1)} %get-tuple-element.63), channel_id=1, source_target_pairs={{0,1},{1,0},{2,3},{3,2},{4,5},{5,4},{6,7},{7,6},{8,9},{9,8},{10,11... | collective-permute-start | bytes 12296 | tf_op jit(solution)/shard_map/ppermute | solution.py:397
  59.4 2.0 %collective-permute-done.7 = f32[8,128]{1,0:T(8,128)S(1)} collective-permute-done((f32[8,128]{1,0:T(8,128)S(1)}, f32[8,128]{1,0:T(8,128)S(1)}, u32[]{:S(2)}, u32[]{:S(2)}) %collective-permute-start.7) | collective-permute-done | bytes 4128 | tf_op jit(solution)/shard_map/ppermute | solution.py:397
  61.5 4.3 %near_window.1 = (f32[1024,128]{1,0:T(8,128)S(1)}, f32[1024,128]{1,0:T(8,128)S(1)}, f32[1024,128]{1,0:T(8,128)S(1)}) custom-call(s32[8]{0:T(128)S(1)} %get-tuple-element.51.need_ref, bf16[8,400,128]{2,1,0:T(8,128)(2,1)S(1)} %all_to_all.10.own_ref, bf16[8,128,128]{2,1,0:T(8,128)(2,1)S(1)} %get-tuple-element.42.mark_ref, ...), custom_call_target="tpu_custom_call" | custom-call | tf_op jit(solution)/shard_map/near_window/pallas_call | solution.py:400
  65.8 1.4 %collective-permute-done.3.far_ref = bf16[8,272,128]{2,1,0:T(8,128)(2,1)S(1)} collective-permute-done((bf16[8,272,128]{2,1,0:T(8,128)(2,1)S(1)}, bf16[8,272,128]{2,1,0:T(8,128)(2,1)S(1)}, u32[]{:S(2)}, u32[]{:S(2)}) %collective-permute-start.3) | collective-permute-done | bytes 557088 | tf_op jit(solution)/shard_map/ppermute | solution.py:388
  67.2 3.0 %collective-permute-start.9 = (f32[8,128]{1,0:T(8,128)S(1)}, f32[8,128]{1,0:T(8,128)S(1)}, u32[]{:S(2)}, u32[]{:S(2)}) collective-permute-start(f32[8,128]{1,0:T(8,128)S(1)} %add.10), channel_id=1, source_target_pairs={{0,3},{1,2},{2,1},{3,0},{4,7},{5,6},{6,5},{7,4},{8,11},{9,10},{10,... | collective-permute-start | bytes 12296 | tf_op jit(solution)/shard_map/ppermute | solution.py:404
  70.2 2.7 %far_own.1 = (f32[1024,128]{1,0:T(8,128)S(1)}, f32[1024,128]{1,0:T(8,128)S(1)}, f32[1024,128]{1,0:T(8,128)S(1)}) custom-call(s32[3]{0:T(128)S(1)} %pad_add_fusion.info_ref, s32[8]{0:T(128)S(1)} %get-tuple-element.51.need_ref, bf16[8,400,128]{2,1,0:T(8,128)(2,1)S(1)} %all_to_all.10.own_ref, bf16[8,128,128]{2,1,0:T(8,128)(2,1)S(1)} %get-tuple-element.42.mark_ref, ...), custom_call_target="tpu_custom_call" | custom-call | tf_op jit(solution)/shard_map/far_own/pallas_call | solution.py:406
  73.0 2.8 %far_other.1 = bf16[8,272,128]{2,1,0:T(8,128)(2,1)S(1)} custom-call(s32[3]{0:T(128)S(1)} %pad_add_fusion.info_ref, s32[8]{0:T(128)S(1)} %get-tuple-element.51.need_ref, bf16[8,400,128]{2,1,0:T(8,128)(2,1)S(1)} %all_to_all.10.own_ref, bf16[8,128,128]{2,1,0:T(8,128)(2,1)S(1)} %get-tuple-element.42.mark_ref, ...), custom_call_target="tpu_custom_call" | custom-call | tf_op jit(solution)/shard_map/far_other/pallas_call | solution.py:407
  75.8 21.2 %all_to_all.11.got_ref = bf16[8,272,128]{2,1,0:T(8,128)(2,1)S(1)} all-to-all(bf16[8,272,128]{2,1,0:T(8,128)(2,1)S(1)} %far_other.1), channel_id=1, replica_groups=mesh['x'=4,'z'=8,'core'=2,'head'=4] {'z'}, dimensions={0} | all-to-all | bytes 1114112 | tf_op jit(solution)/shard_map/all_to_all | solution.py:414
  97.0 0.9 finish.1
  (16 shorter events, 0.1 us)
Async XLA Ops:
  0.0 38.6 %copy-start = (f32[8,128,128]{2,1,0:T(8,128)S(1)}, f32[8,128,128]{2,1,0:T(8,128)}, u32[]{:S(2)}) copy-start(f32[8,128,128]{2,1,0:T(8,128)} %param.13) | copy-start | bytes 1572868
  35.3 3.3 %collective-permute-start = (bf16[8,272,128]{2,1,0:T(8,128)(2,1)S(1)}, bf16[8,272,128]{2,1,0:T(8,128)(2,1)S(1)}, u32[]{:S(2)}, u32[]{:S(2)}) collective-permute-start(bf16[8,272,128]{2,1,0:T(8,128)(2,1)S(1)} %slice.12), channel_id=1, source_target_pairs={{0,4},{4,0},{1,5},{5,1},{2,6},{6,2},{3,7},{7,3},{8,12},{12,8},{9,1... | collective-permute-start | bytes 1671176 | tf_op jit(solution)/shard_map/ppermute | solution.py:366
  35.4 20.3 %collective-permute-start.4 = (bf16[8,272,128]{2,1,0:T(8,128)(2,1)S(1)}, bf16[8,272,128]{2,1,0:T(8,128)(2,1)S(1)}, u32[]{:S(2)}, u32[]{:S(2)}) collective-permute-start(bf16[8,272,128]{2,1,0:T(8,128)(2,1)S(1)} %slice.12), channel_id=1, source_target_pairs={{0,64},{64,128},{128,192},{1,65},{65,129},{129,193},{2,66},{66,130... | collective-permute-start | bytes 1671176 | tf_op jit(solution)/shard_map/ppermute | solution.py:365
  40.8 13.3 %collective-permute-start.2 = (f32[136,128]{1,0:T(8,128)S(1)}, f32[136,128]{1,0:T(8,128)S(1)}, u32[]{:S(2)}, u32[]{:S(2)}) collective-permute-start(f32[136,128]{1,0:T(8,128)S(1)} %get-tuple-element.41.state_ref), channel_id=1, source_target_pairs={{0,128},{64,192},{1,129},{65,193},{2,130},{66,194},{3,131},{67,195... | collective-permute-start | bytes 208904 | tf_op jit(solution)/shard_map/ppermute | solution.py:383
  42.1 13.5 %collective-permute-start.1 = (f32[136,128]{1,0:T(8,128)S(1)}, f32[136,128]{1,0:T(8,128)S(1)}, u32[]{:S(2)}, u32[]{:S(2)}) collective-permute-start(f32[136,128]{1,0:T(8,128)S(1)} %get-tuple-element.41.state_ref), channel_id=1, source_target_pairs={{0,64},{64,128},{128,192},{1,65},{65,129},{129,193},{2,66},{66,130... | collective-permute-start | bytes 208904 | tf_op jit(solution)/shard_map/ppermute | solution.py:382
  47.2 20.0 %collective-permute-start.3 = (bf16[8,272,128]{2,1,0:T(8,128)(2,1)S(1)}, bf16[8,272,128]{2,1,0:T(8,128)(2,1)S(1)}, u32[]{:S(2)}, u32[]{:S(2)}) collective-permute-start(bf16[8,272,128]{2,1,0:T(8,128)(2,1)S(1)} %slice.12), channel_id=1, source_target_pairs={{0,128},{64,192},{1,129},{65,193},{2,130},{66,194},{3,131},{67,195... | collective-permute-start | bytes 1671176 | tf_op jit(solution)/shard_map/ppermute | solution.py:388
  55.7 5.7 %collective-permute-start.6 = (bf16[4,272,128]{2,1,0:T(8,128)(2,1)S(1)}, bf16[4,272,128]{2,1,0:T(8,128)(2,1)S(1)}, u32[]{:S(2)}, u32[]{:S(2)}) collective-permute-start(bf16[4,272,128]{2,1,0:T(8,128)(2,1)S(1)} %get-tuple-element.73), channel_id=1, source_target_pairs={{0,4},{4,0},{1,5},{5,1},{2,6},{6,2},{3,7},{7,3},{8,12},{12,8},{9,1... | collective-permute-start | bytes 835592 | tf_op jit(solution)/shard_map/ppermute | solution.py:399
  55.8 5.6 %collective-permute-start.5 = (bf16[4,272,128]{2,1,0:T(8,128)(2,1)S(1)}, bf16[4,272,128]{2,1,0:T(8,128)(2,1)S(1)}, u32[]{:S(2)}, u32[]{:S(2)}) collective-permute-start(bf16[4,272,128]{2,1,0:T(8,128)(2,1)S(1)} %get-tuple-element.74), channel_id=1, source_target_pairs={{0,4},{4,0},{1,5},{5,1},{2,6},{6,2},{3,7},{7,3},{8,12},{12,8},{9,1... | collective-permute-start | bytes 835592 | tf_op jit(solution)/shard_map/ppermute | solution.py:399
  57.8 3.7 %collective-permute-start.7 = (f32[8,128]{1,0:T(8,128)S(1)}, f32[8,128]{1,0:T(8,128)S(1)}, u32[]{:S(2)}, u32[]{:S(2)}) collective-permute-start(f32[8,128]{1,0:T(8,128)S(1)} %get-tuple-element.63), channel_id=1, source_target_pairs={{0,1},{1,0},{2,3},{3,2},{4,5},{5,4},{6,7},{7,6},{8,9},{9,8},{10,11... | collective-permute-start | bytes 12296 | tf_op jit(solution)/shard_map/ppermute | solution.py:397
  67.2 5.8 %collective-permute-start.8 = (bf16[8,272,128]{2,1,0:T(8,128)(2,1)S(1)}, bf16[8,272,128]{2,1,0:T(8,128)(2,1)S(1)}, u32[]{:S(2)}, u32[]{:S(2)}) collective-permute-start(bf16[8,272,128]{2,1,0:T(8,128)(2,1)S(1)} %collective-permute-done.3.far_ref), channel_id=1, source_target_pairs={{0,4},{4,0},{1,5},{5,1},{2,6},{6,2},{3,7},{7,3},{8,12},{12,8},{9,1... | collective-permute-start | bytes 1671176 | tf_op jit(solution)/shard_map/ppermute | solution.py:405
  67.2 5.7 %collective-permute-start.9 = (f32[8,128]{1,0:T(8,128)S(1)}, f32[8,128]{1,0:T(8,128)S(1)}, u32[]{:S(2)}, u32[]{:S(2)}) collective-permute-start(f32[8,128]{1,0:T(8,128)S(1)} %add.10), channel_id=1, source_target_pairs={{0,3},{1,2},{2,1},{3,0},{4,7},{5,6},{6,5},{7,4},{8,11},{9,10},{10,... | collective-permute-start | bytes 12296 | tf_op jit(solution)/shard_map/ppermute | solution.py:404
  75.8 21.3 %copy-start.1 = (f32[1024]{0:T(1024)S(1)}, f32[1024]{0:T(1024)}, u32[]{:S(2)}) copy-start(f32[1024]{0:T(1024)} %param.14) | copy-start | bytes 12292

commit v7 on v6

--- a/solution.py
+++ b/solution.py
@@ -394,14 +394,14 @@
         [shape((HEADS, TOK, DH), BF16), shape((HEADS, TOK), F32), shape((2 * TILES,), jnp.int32)],
         outs=[VMEM, VMEM, SMEM],
     )(info, own, partial, weight, state, near_state, far_state)
-    square = square + lax.ppermute(square, "head", [(i, i ^ 1) for i in range(4)])
     near, own_part = lax.optimization_barrier((near, own_part))
     near_other = [lax.ppermute(near[at : at + TILES], "core", pair) for at in (0, TILES)]
+    squares = [lax.ppermute(square, "head", [(i, i ^ step) for i in range(4)]) for step in (1, 2, 3)]
     part = call(near_kernel, "near_window", [SMEM] + [VMEM] * 8, part_shapes)(
         need, own, mark, near, *near_other, *own_part
     )
-    far, part, square = lax.optimization_barrier((far, part, square))
-    square = square + lax.ppermute(square, "head", [(i, 3 - i) for i in range(4)])
+    far, part, squares = lax.optimization_barrier((far, part, squares))
+    square = square + squares[0] + (squares[1] + squares[2])
     far_other = lax.ppermute(far, "core", pair)
     part = call(far_own_kernel, "far_own", [SMEM] * 2 + [VMEM] * 6, part_shapes)(info, need, own, mark, far, *part)
     mixed = call(

time: 98.6 us -> 95.9 us (0.973)
  waiting for transfers between devices: 10.7 us -> 7.32 us
    ppermute x1, waiting for transfers between devices: 5.67 us -> 1.48 us  [body(): far_state = lax.ppermute(state, 'x', [(0, 2), (1, 3)])]
    ppermute x1, waiting for transfers between devices: 1.53 us -> 5.67 us  [body(): near_state = lax.ppermute(state, 'x', [(0, 1), (1, 2), (2, 3)])]
    ppermute x2 -> x3, waiting for transfers between devices: 2.03 us -> 0.09 us  [body(): lax.ppermute(square, 'head', [(i, i ^ step) for i in range(4)])]
    ppermute x1, waiting for transfers between devices: 1.44 us -> 0.06 us  [body(): far = lax.ppermute(sent, 'x', [(0, 2), (1, 3)])]
    ppermute x2 -> x3, starting transfers between devices: 4.68 us -> 4.79 us  [body(): lax.ppermute(square, 'head', [(i, i ^ step) for i in range(4)])]
  transfers between devices with their start and end apart: 10 -> 11, of which waited for: 4 -> 4; matrix products, arithmetic and copies ran while one was open for 0% -> 0% of each run, Pallas kernels for 14% -> 15%
where the time goes in v7:
time: 95.9 us; the launch traced here: 94.3 us
  blocking collectives  53 us (55%)
  Pallas kernels  20.6 us (21%)
  starting transfers between devices  13.1 us (14%)
  waiting for transfers between devices  7.32 us (8%)
    all_to_all x1, blocking collectives, body(): own = lax.all_to_all(packed, 'z', 0, 0, tiled=True)  32.3 us
    all_to_all x1, blocking collectives, body(): back = lax.all_to_all(mixed, 'z', 0, 0, tiled=True)  20.7 us
    ppermute x1, waiting for transfers between devices, body(): near_state = lax.ppermute(state, 'x', [(0, 1), (1, 2), (2, 3)])  5.67 us
    ppermute x3, starting transfers between devices, body(): lax.ppermute(square, 'head', [(i, i ^ step) for i in range(4)])  4.79 us
    pallas_call x1, Pallas kernels, body(): call(near_kernel, 'near_window', [SMEM] + [VMEM] * 8, part_shapes)  4.48 us
    pallas_call x1, Pallas kernels, body(): call(own_window_kernel, 'own_window', [SMEM] + [VMEM] * 3, part_shapes)  3.14 us
    ppermute x1, starting transfers between devices, body(): near = lax.ppermute(sent, 'x', [(0, 1), (1, 2), (2, 3)])  3.11 us
    pallas_call x1, Pallas kernels, body(): call(prepare_kernel, 'prepare', [SMEM, SMEM, HBM, HBM, HBM, VMEM, VMEM, V...  2.93 us
  transfers between devices with their start and end apart: 11, of which 4 were waited for; matrix products, arithmetic and copies ran while one was open for 0% of the time, Pallas kernels for 15%

profile of v7, /device:TPU:4, one launch (start us, length us, event | category | flops | bytes accessed | tf_op | source)
XLA Modules:
  0.0 94.3 jit_solution(2771657000710436681)
XLA Ops:
  0.0 2.9 %prepare.1 = bf16[8,400,128]{2,1,0:T(8,128)(2,1)} custom-call(f32[16]{0:T(128)} %table_ref.1, s32[8]{0:T(128)} %index_ref.1, bf16[128,1024]{1,0:T(8,128)(2,1)} %q_hbm.1, bf16[128,1024]{1,0:T(8,128)(2,1)} %k_hbm.1, bf16[128,1024]{1,0:T(8,128)(2,1)} %v_hbm.1, f32[8,128]{1,0:T(8,128)} %bitcast.8, f32[8,128]{1,0:T(8,128)} %bitcast.9, s32[1,128]{1,0:T(1,128)} %bitcast.10), custom_call_target="tpu_custom_call" | custom-call | tf_op jit(solution)/shard_map/prepare/pallas_call | solution.py:355
  2.9 32.3 %all_to_all.10.own_ref = bf16[8,400,128]{2,1,0:T(8,128)(2,1)S(1)} all-to-all(bf16[8,400,128]{2,1,0:T(8,128)(2,1)} %prepare.1), channel_id=1, replica_groups=mesh['x'=4,'z'=8,'core'=2,'head'=4] {'z'}, dimensions={0} | all-to-all | bytes 1638400 | tf_op jit(solution)/shard_map/all_to_all | solution.py:362
  35.3 0.1 collective-permute-start
  35.4 3.1 %collective-permute-start.4 = (bf16[8,272,128]{2,1,0:T(8,128)(2,1)S(1)}, bf16[8,272,128]{2,1,0:T(8,128)(2,1)S(1)}, u32[]{:S(2)}, u32[]{:S(2)}) collective-permute-start(bf16[8,272,128]{2,1,0:T(8,128)(2,1)S(1)} %slice.12), channel_id=1, source_target_pairs={{0,64},{64,128},{128,192},{1,65},{65,129},{129,193},{2,66},{66,130... | collective-permute-start | bytes 1671176 | tf_op jit(solution)/shard_map/ppermute | solution.py:365
  38.5 0.1 pad_add_fusion.info_ref
  38.6 2.2 %linear.1 = (f32[8,128,128]{2,1,0:T(8,128)S(1)}, f32[8,128,128]{2,1,0:T(8,128)S(1)}, f32[136,128]{1,0:T(8,128)S(1)}, bf16[8,128,128]{2,1,0:T(8,128)(2,1)S(1)}) custom-call(s32[3]{0:T(128)S(1)} %pad_add_fusion.info_ref, bf16[8,400,128]{2,1,0:T(8,128)(2,1)S(1)} %all_to_all.10.own_ref, bf16[8,272,128]{2,1,0:T(8,128)(2,1)S(1)} %collective-permute-done.other_ref, ...), custom_call_target="tpu_custom_call" | custom-call | tf_op jit(solution)/shard_map/linear/pallas_call | solution.py:371
  40.8 1.9 %collective-permute-start.1 = (f32[136,128]{1,0:T(8,128)S(1)}, f32[136,128]{1,0:T(8,128)S(1)}, u32[]{:S(2)}, u32[]{:S(2)}) collective-permute-start(f32[136,128]{1,0:T(8,128)S(1)} %get-tuple-element.43.state_ref), channel_id=1, source_target_pairs={{0,64},{64,128},{128,192},{1,65},{65,129},{129,193},{2,66},{66,130... | collective-permute-start | bytes 208904 | tf_op jit(solution)/shard_map/ppermute | solution.py:382
  42.8 1.3 %collective-permute-start.2 = (f32[136,128]{1,0:T(8,128)S(1)}, f32[136,128]{1,0:T(8,128)S(1)}, u32[]{:S(2)}, u32[]{:S(2)}) collective-permute-start(f32[136,128]{1,0:T(8,128)S(1)} %get-tuple-element.43.state_ref), channel_id=1, source_target_pairs={{0,128},{64,192},{1,129},{65,193},{2,130},{66,194},{3,131},{67,195... | collective-permute-start | bytes 208904 | tf_op jit(solution)/shard_map/ppermute | solution.py:383
  44.1 3.1 %own_window.1 = (f32[1024,128]{1,0:T(8,128)S(1)}, f32[1024,128]{1,0:T(8,128)S(1)}, f32[1024,128]{1,0:T(8,128)S(1)}) custom-call(s32[3]{0:T(128)S(1)} %pad_add_fusion.info_ref, bf16[8,400,128]{2,1,0:T(8,128)(2,1)S(1)} %all_to_all.10.own_ref, bf16[8,272,128]{2,1,0:T(8,128)(2,1)S(1)} %collective-permute-done.other_ref, ...), custom_call_target="tpu_custom_call" | custom-call | tf_op jit(solution)/shard_map/own_window/pallas_call | solution.py:384
  47.2 1.3 %collective-permute-start.3 = (bf16[8,272,128]{2,1,0:T(8,128)(2,1)S(1)}, bf16[8,272,128]{2,1,0:T(8,128)(2,1)S(1)}, u32[]{:S(2)}, u32[]{:S(2)}) collective-permute-start(bf16[8,272,128]{2,1,0:T(8,128)(2,1)S(1)} %slice.12), channel_id=1, source_target_pairs={{0,128},{64,192},{1,129},{65,193},{2,130},{66,194},{3,131},{67,195... | collective-permute-start | bytes 1671176 | tf_op jit(solution)/shard_map/ppermute | solution.py:388
  48.5 5.7 %collective-permute-done.1.near_ref = f32[136,128]{1,0:T(8,128)S(1)} collective-permute-done((f32[136,128]{1,0:T(8,128)S(1)}, f32[136,128]{1,0:T(8,128)S(1)}, u32[]{:S(2)}, u32[]{:S(2)}) %collective-permute-start.1) | collective-permute-done | bytes 69664 | tf_op jit(solution)/shard_map/ppermute | solution.py:382
  54.2 1.5 %collective-permute-done.2.far_ref = f32[136,128]{1,0:T(8,128)S(1)} collective-permute-done((f32[136,128]{1,0:T(8,128)S(1)}, f32[136,128]{1,0:T(8,128)S(1)}, u32[]{:S(2)}, u32[]{:S(2)}) %collective-permute-start.2) | collective-permute-done | bytes 69664 | tf_op jit(solution)/shard_map/ppermute | solution.py:383
  55.7 0.1 collective-permute-start.5
  55.8 0.5 collective-permute-start.6
  56.3 1.4 %enter.1 = (bf16[8,128,128]{2,1,0:T(8,128)(2,1)S(1)}, f32[8,128]{1,0:T(8,128)S(1)}, s32[8]{0:T(128)S(1)}) custom-call(s32[3]{0:T(128)S(1)} %pad_add_fusion.info_ref, bf16[8,400,128]{2,1,0:T(8,128)(2,1)S(1)} %all_to_all.10.own_ref, f32[8,128,128]{2,1,0:T(8,128)S(1)} %get-tuple-element.41.partial_ref, f32[8,128,128]{2,1,0:T(8,128)S(1)} %get-tuple-element.42.weight_ref, ...), custom_call_target="tpu_custom_call" | custom-call | tf_op jit(solution)/shard_map/enter/pallas_call | solution.py:390
  57.8 1.7 %collective-permute-start.7 = (f32[8,128]{1,0:T(8,128)S(1)}, f32[8,128]{1,0:T(8,128)S(1)}, u32[]{:S(2)}, u32[]{:S(2)}) collective-permute-start(f32[8,128]{1,0:T(8,128)S(1)} %get-tuple-element.65), channel_id=1, source_target_pairs={{0,1},{1,0},{2,3},{3,2},{4,5},{5,4},{6,7},{7,6},{8,9},{9,8},{10,11... | collective-permute-start | bytes 12296 | tf_op jit(solution)/shard_map/ppermute | solution.py:399
  59.4 2.9 %collective-permute-start.8 = (f32[8,128]{1,0:T(8,128)S(1)}, f32[8,128]{1,0:T(8,128)S(1)}, u32[]{:S(2)}, u32[]{:S(2)}) collective-permute-start(f32[8,128]{1,0:T(8,128)S(1)} %get-tuple-element.65), channel_id=1, source_target_pairs={{0,2},{1,3},{2,0},{3,1},{4,6},{5,7},{6,4},{7,5},{8,10},{9,11},{10,... | collective-permute-start | bytes 12296 | tf_op jit(solution)/shard_map/ppermute | solution.py:399
  62.3 0.2 collective-permute-start.9
  62.5 4.5 %near_window.1 = (f32[1024,128]{1,0:T(8,128)S(1)}, f32[1024,128]{1,0:T(8,128)S(1)}, f32[1024,128]{1,0:T(8,128)S(1)}) custom-call(s32[8]{0:T(128)S(1)} %get-tuple-element.53.need_ref, bf16[8,400,128]{2,1,0:T(8,128)(2,1)S(1)} %all_to_all.10.own_ref, bf16[8,128,128]{2,1,0:T(8,128)(2,1)S(1)} %get-tuple-element.44.mark_ref, ...), custom_call_target="tpu_custom_call" | custom-call | tf_op jit(solution)/shard_map/near_window/pallas_call | solution.py:400
  67.1 0.1 collective-permute-done.9
  67.2 2.7 %far_own.1 = (f32[1024,128]{1,0:T(8,128)S(1)}, f32[1024,128]{1,0:T(8,128)S(1)}, f32[1024,128]{1,0:T(8,128)S(1)}) custom-call(s32[3]{0:T(128)S(1)} %pad_add_fusion.info_ref, s32[8]{0:T(128)S(1)} %get-tuple-element.53.need_ref, bf16[8,400,128]{2,1,0:T(8,128)(2,1)S(1)} %all_to_all.10.own_ref, bf16[8,128,128]{2,1,0:T(8,128)(2,1)S(1)} %get-tuple-element.44.mark_ref, ...), custom_call_target="tpu_custom_call" | custom-call | tf_op jit(solution)/shard_map/far_own/pallas_call | solution.py:406
  69.9 2.8 %far_other.1 = bf16[8,272,128]{2,1,0:T(8,128)(2,1)S(1)} custom-call(s32[3]{0:T(128)S(1)} %pad_add_fusion.info_ref, s32[8]{0:T(128)S(1)} %get-tuple-element.53.need_ref, bf16[8,400,128]{2,1,0:T(8,128)(2,1)S(1)} %all_to_all.10.own_ref, bf16[8,128,128]{2,1,0:T(8,128)(2,1)S(1)} %get-tuple-element.44.mark_ref, ...), custom_call_target="tpu_custom_call" | custom-call | tf_op jit(solution)/shard_map/far_other/pallas_call | solution.py:407
  72.8 20.7 %all_to_all.11.got_ref = bf16[8,272,128]{2,1,0:T(8,128)(2,1)S(1)} all-to-all(bf16[8,272,128]{2,1,0:T(8,128)(2,1)S(1)} %far_other.1), channel_id=1, replica_groups=mesh['x'=4,'z'=8,'core'=2,'head'=4] {'z'}, dimensions={0} | all-to-all | bytes 1114112 | tf_op jit(solution)/shard_map/all_to_all | solution.py:414
  93.4 0.9 finish.1
  (17 shorter events, 0.2 us)
Async XLA Ops:
  0.0 38.6 %copy-start = (f32[8,128,128]{2,1,0:T(8,128)S(1)}, f32[8,128,128]{2,1,0:T(8,128)}, u32[]{:S(2)}) copy-start(f32[8,128,128]{2,1,0:T(8,128)} %param.13) | copy-start | bytes 1572868
  35.3 3.3 %collective-permute-start = (bf16[8,272,128]{2,1,0:T(8,128)(2,1)S(1)}, bf16[8,272,128]{2,1,0:T(8,128)(2,1)S(1)}, u32[]{:S(2)}, u32[]{:S(2)}) collective-permute-start(bf16[8,272,128]{2,1,0:T(8,128)(2,1)S(1)} %slice.12), channel_id=1, source_target_pairs={{0,4},{4,0},{1,5},{5,1},{2,6},{6,2},{3,7},{7,3},{8,12},{12,8},{9,1... | collective-permute-start | bytes 1671176 | tf_op jit(solution)/shard_map/ppermute | solution.py:366
  35.4 20.3 %collective-permute-start.4 = (bf16[8,272,128]{2,1,0:T(8,128)(2,1)S(1)}, bf16[8,272,128]{2,1,0:T(8,128)(2,1)S(1)}, u32[]{:S(2)}, u32[]{:S(2)}) collective-permute-start(bf16[8,272,128]{2,1,0:T(8,128)(2,1)S(1)} %slice.12), channel_id=1, source_target_pairs={{0,64},{64,128},{128,192},{1,65},{65,129},{129,193},{2,66},{66,130... | collective-permute-start | bytes 1671176 | tf_op jit(solution)/shard_map/ppermute | solution.py:365
  40.8 13.3 %collective-permute-start.1 = (f32[136,128]{1,0:T(8,128)S(1)}, f32[136,128]{1,0:T(8,128)S(1)}, u32[]{:S(2)}, u32[]{:S(2)}) collective-permute-start(f32[136,128]{1,0:T(8,128)S(1)} %get-tuple-element.43.state_ref), channel_id=1, source_target_pairs={{0,64},{64,128},{128,192},{1,65},{65,129},{129,193},{2,66},{66,130... | collective-permute-start | bytes 208904 | tf_op jit(solution)/shard_map/ppermute | solution.py:382
  42.8 12.9 %collective-permute-start.2 = (f32[136,128]{1,0:T(8,128)S(1)}, f32[136,128]{1,0:T(8,128)S(1)}, u32[]{:S(2)}, u32[]{:S(2)}) collective-permute-start(f32[136,128]{1,0:T(8,128)S(1)} %get-tuple-element.43.state_ref), channel_id=1, source_target_pairs={{0,128},{64,192},{1,129},{65,193},{2,130},{66,194},{3,131},{67,195... | collective-permute-start | bytes 208904 | tf_op jit(solution)/shard_map/ppermute | solution.py:383
  47.2 20.0 %collective-permute-start.3 = (bf16[8,272,128]{2,1,0:T(8,128)(2,1)S(1)}, bf16[8,272,128]{2,1,0:T(8,128)(2,1)S(1)}, u32[]{:S(2)}, u32[]{:S(2)}) collective-permute-start(bf16[8,272,128]{2,1,0:T(8,128)(2,1)S(1)} %slice.12), channel_id=1, source_target_pairs={{0,128},{64,192},{1,129},{65,193},{2,130},{66,194},{3,131},{67,195... | collective-permute-start | bytes 1671176 | tf_op jit(solution)/shard_map/ppermute | solution.py:388
  55.7 6.6 %collective-permute-start.5 = (bf16[4,272,128]{2,1,0:T(8,128)(2,1)S(1)}, bf16[4,272,128]{2,1,0:T(8,128)(2,1)S(1)}, u32[]{:S(2)}, u32[]{:S(2)}) collective-permute-start(bf16[4,272,128]{2,1,0:T(8,128)(2,1)S(1)} %get-tuple-element.78), channel_id=1, source_target_pairs={{0,4},{4,0},{1,5},{5,1},{2,6},{6,2},{3,7},{7,3},{8,12},{12,8},{9,1... | collective-permute-start | bytes 835592 | tf_op jit(solution)/shard_map/ppermute | solution.py:398
  55.8 6.7 %collective-permute-start.6 = (bf16[4,272,128]{2,1,0:T(8,128)(2,1)S(1)}, bf16[4,272,128]{2,1,0:T(8,128)(2,1)S(1)}, u32[]{:S(2)}, u32[]{:S(2)}) collective-permute-start(bf16[4,272,128]{2,1,0:T(8,128)(2,1)S(1)} %get-tuple-element.77), channel_id=1, source_target_pairs={{0,4},{4,0},{1,5},{5,1},{2,6},{6,2},{3,7},{7,3},{8,12},{12,8},{9,1... | collective-permute-start | bytes 835592 | tf_op jit(solution)/shard_map/ppermute | solution.py:398
  57.8 9.3 %collective-permute-start.7 = (f32[8,128]{1,0:T(8,128)S(1)}, f32[8,128]{1,0:T(8,128)S(1)}, u32[]{:S(2)}, u32[]{:S(2)}) collective-permute-start(f32[8,128]{1,0:T(8,128)S(1)} %get-tuple-element.65), channel_id=1, source_target_pairs={{0,1},{1,0},{2,3},{3,2},{4,5},{5,4},{6,7},{7,6},{8,9},{9,8},{10,11... | collective-permute-start | bytes 12296 | tf_op jit(solution)/shard_map/ppermute | solution.py:399
  59.4 7.6 %collective-permute-start.8 = (f32[8,128]{1,0:T(8,128)S(1)}, f32[8,128]{1,0:T(8,128)S(1)}, u32[]{:S(2)}, u32[]{:S(2)}) collective-permute-start(f32[8,128]{1,0:T(8,128)S(1)} %get-tuple-element.65), channel_id=1, source_target_pairs={{0,2},{1,3},{2,0},{3,1},{4,6},{5,7},{6,4},{7,5},{8,10},{9,11},{10,... | collective-permute-start | bytes 12296 | tf_op jit(solution)/shard_map/ppermute | solution.py:399
  62.3 4.8 %collective-permute-start.9 = (f32[8,128]{1,0:T(8,128)S(1)}, f32[8,128]{1,0:T(8,128)S(1)}, u32[]{:S(2)}, u32[]{:S(2)}) collective-permute-start(f32[8,128]{1,0:T(8,128)S(1)} %get-tuple-element.65), channel_id=1, source_target_pairs={{0,3},{1,2},{2,1},{3,0},{4,7},{5,6},{6,5},{7,4},{8,11},{9,10},{10,... | collective-permute-start | bytes 12296 | tf_op jit(solution)/shard_map/ppermute | solution.py:399
  67.2 2.7 %collective-permute-start.10 = (bf16[8,272,128]{2,1,0:T(8,128)(2,1)S(1)}, bf16[8,272,128]{2,1,0:T(8,128)(2,1)S(1)}, u32[]{:S(2)}, u32[]{:S(2)}) collective-permute-start(bf16[8,272,128]{2,1,0:T(8,128)(2,1)S(1)} %collective-permute-done.3.far_ref), channel_id=1, source_target_pairs={{0,4},{4,0},{1,5},{5,1},{2,6},{6,2},{3,7},{7,3},{8,12},{12,8},{9,1... | collective-permute-start | bytes 1671176 | tf_op jit(solution)/shard_map/ppermute | solution.py:405
  72.8 20.7 %copy-start.1 = (f32[1024]{0:T(1024)S(1)}, f32[1024]{0:T(1024)}, u32[]{:S(2)}) copy-start(f32[1024]{0:T(1024)} %param.14) | copy-start | bytes 12292

commit v8 on v7

--- a/solution.py
+++ b/solution.py
@@ -99,7 +99,7 @@
     return ref[i, META_AT:VALUE_AT, :].astype(F32)
 
 
-def linear_kernel(info_ref, own_ref, other_ref, init_ref, partial_ref, weight_ref, state_ref, mark_ref):
+def linear_kernel(info_ref, own_ref, low_ref, high_ref, init_ref, partial_ref, weight_ref, state_ref, mark_ref):
     x, core = info_ref[0], info_ref[2]
     first = core == 0
     state = jnp.where(x == 0, init_ref[0], 0.0)
@@ -113,7 +113,7 @@
     start_doc = None
 
     def read(swap, i):
-        mine, theirs = own_ref[i, 0:KV_ROWS, :], other_ref[i]
+        mine, theirs = own_ref[i, 0:KV_ROWS, :], (low_ref, high_ref)[i // TILES][i % TILES]
         got = jnp.where(swap, theirs, mine)
         rows = got[META_AT:VALUE_AT].astype(F32)
         cum, doc = rows[0:1] + rows[1:2] + rows[2:3], rows[3:4]
@@ -243,7 +243,7 @@
         ref[span, :] = jnp.broadcast_to(value, (CHUNK, TOK))
 
 
-def own_window_kernel(info_ref, own_ref, other_ref, mark_ref, *refs):
+def own_window_kernel(info_ref, own_ref, low_ref, high_ref, mark_ref, *refs):
     core = info_ref[2]
     masks = []
     for own in (True, False):
@@ -251,10 +251,9 @@
         masks.append(key <= at)
     for tile in range(TILES):
         queries = marked_queries(own_ref, mark_ref, tile)
-        pieces = [
-            (ref, m, mask if m == tile else None)
-            for ref, mask in zip((own_ref, other_ref), masks)
-            for m in range(tile + 1)
+        pieces = [(own_ref, m, masks[0] if m == tile else None) for m in range(tile + 1)]
+        pieces += [
+            ((low_ref, high_ref)[m // 2], m % 2, masks[1] if m == tile else None) for m in range(tile + 1)
         ]
         store_part(refs, tile, absorb(queries, pieces, None))
 
@@ -363,7 +362,7 @@
     sent = own[:, :KV_ROWS]
     pair = [(0, 1), (1, 0)]
     near = lax.ppermute(sent, "x", [(0, 1), (1, 2), (2, 3)])
-    other = lax.ppermute(sent, "core", pair)
+    other = [lax.ppermute(sent[at : at + TILES], "core", pair) for at in (0, TILES)]
 
     tokens = HEADS * TOK
     part_shapes = [shape((tokens, TOK), F32), shape((tokens, TOK), F32), shape((tokens, DH), F32)]
@@ -371,19 +370,19 @@
     partial, weight, state, mark = call(
         linear_kernel,
         "linear",
-        [SMEM] + [VMEM] * 3,
+        [SMEM] + [VMEM] * 4,
         [
             shape((HEADS, TOK, DH), F32),
             shape((HEADS, TOK, DH), F32),
             shape((DH + 8, DH), F32),
             shape((HEADS, TOK, TOK), BF16),
         ],
-    )(info, own, other, init)
+    )(info, own, *other, init)
     near_state = lax.ppermute(state, "x", [(0, 1), (1, 2), (2, 3)])
     far_state = lax.ppermute(state, "x", [(0, 2), (1, 3)])
     own_part = call(
-        own_window_kernel, "own_window", [SMEM] + [VMEM] * 3, part_shapes
-    )(info, own, other, mark)
+        own_window_kernel, "own_window", [SMEM] + [VMEM] * 4, part_shapes
+    )(info, own, *other, mark)
     sent, own_part = lax.optimization_barrier((sent, own_part))
     far = lax.ppermute(sent, "x", [(0, 2), (1, 3)])
     near_state, far_state, own_part = lax.optimization_barrier((near_state, far_state, own_part))

time: 95.9 us -> 96.2 us (level); the launches traced: 94.3 us -> 95.9 us
    ppermute x1, waiting for transfers between devices: 5.67 us -> 0.01 us  [body(): near_state = lax.ppermute(state, 'x', [(0, 1), (1, 2), (2, 3)])]
    ppermute x1, waiting for transfers between devices: 0.06 us -> 3.32 us  [body(): far = lax.ppermute(sent, 'x', [(0, 2), (1, 3)])]
    ppermute x1 -> x2, waiting for transfers between devices: 0.01 us -> 1.54 us  [body(): lax.ppermute(sent[at:at + TILES], 'core', pair)]
  transfers between devices with their start and end apart: 11 -> 12, of which waited for: 4 -> 4; matrix products, arithmetic and copies ran while one was open for 0% -> 1% of each run, Pallas kernels for 15% -> 15%
where the time goes in v8:
time: 96.2 us; the launch traced here: 95.9 us
  blocking collectives  53.8 us (56%)
  Pallas kernels  20.6 us (21%)
  starting transfers between devices  13.5 us (14%)
  waiting for transfers between devices  6.94 us (7%)
    all_to_all x1, blocking collectives, body(): own = lax.all_to_all(packed, 'z', 0, 0, tiled=True)  32.3 us
    all_to_all x1, blocking collectives, body(): back = lax.all_to_all(mixed, 'z', 0, 0, tiled=True)  21.5 us
    ppermute x3, starting transfers between devices, body(): lax.ppermute(square, 'head', [(i, i ^ step) for i in range(4)])  4.79 us
    pallas_call x1, Pallas kernels, body(): call(near_kernel, 'near_window', [SMEM] + [VMEM] * 8, part_shapes)  4.47 us
    ppermute x1, waiting for transfers between devices, body(): far = lax.ppermute(sent, 'x', [(0, 2), (1, 3)])  3.32 us
    pallas_call x1, Pallas kernels, body(): call(own_window_kernel, 'own_window', [SMEM] + [VMEM] * 4, part_shapes)  3.12 us
    ppermute x1, starting transfers between devices, body(): near = lax.ppermute(sent, 'x', [(0, 1), (1, 2), (2, 3)])  3.11 us
    pallas_call x1, Pallas kernels, body(): call(prepare_kernel, 'prepare', [SMEM, SMEM, HBM, HBM, HBM, VMEM, VMEM, V...  2.94 us
  transfers between devices with their start and end apart: 12, of which 4 were waited for; matrix products, arithmetic and copies ran while one was open for 1% of the time, Pallas kernels for 15%

profile of v8, /device:TPU:4, one launch (start us, length us, event | category | flops | bytes accessed | tf_op | source)
XLA Modules:
  0.0 95.9 jit_solution(8166106709996177361)
XLA Ops:
  0.0 2.9 %prepare.1 = bf16[8,400,128]{2,1,0:T(8,128)(2,1)} custom-call(f32[16]{0:T(128)} %table_ref.1, s32[8]{0:T(128)} %index_ref.1, bf16[128,1024]{1,0:T(8,128)(2,1)} %q_hbm.1, bf16[128,1024]{1,0:T(8,128)(2,1)} %k_hbm.1, bf16[128,1024]{1,0:T(8,128)(2,1)} %v_hbm.1, f32[8,128]{1,0:T(8,128)} %bitcast.8, f32[8,128]{1,0:T(8,128)} %bitcast.9, s32[1,128]{1,0:T(1,128)} %bitcast.10), custom_call_target="tpu_custom_call" | custom-call | tf_op jit(solution)/shard_map/prepare/pallas_call | solution.py:354
  3.0 32.3 %all_to_all.10.own_ref = bf16[8,400,128]{2,1,0:T(8,128)(2,1)S(1)} all-to-all(bf16[8,400,128]{2,1,0:T(8,128)(2,1)} %prepare.1), channel_id=1, replica_groups=mesh['x'=4,'z'=8,'core'=2,'head'=4] {'z'}, dimensions={0} | all-to-all | bytes 1638400 | tf_op jit(solution)/shard_map/all_to_all | solution.py:361
  35.3 3.1 %collective-permute-start.5 = (bf16[8,272,128]{2,1,0:T(8,128)(2,1)S(1)}, bf16[8,272,128]{2,1,0:T(8,128)(2,1)S(1)}, u32[]{:S(2)}, u32[]{:S(2)}) collective-permute-start(bf16[8,272,128]{2,1,0:T(8,128)(2,1)S(1)} %slice.24), channel_id=1, source_target_pairs={{0,64},{64,128},{128,192},{1,65},{65,129},{129,193},{2,66},{66,130... | collective-permute-start | bytes 1671176 | tf_op jit(solution)/shard_map/ppermute | solution.py:364
  38.4 0.7 fusion
  39.1 0.5 collective-permute-start.1
  39.7 1.5 %collective-permute-done.low_ref = bf16[4,272,128]{2,1,0:T(8,128)(2,1)S(1)} collective-permute-done((bf16[4,272,128]{2,1,0:T(8,128)(2,1)}, bf16[4,272,128]{2,1,0:T(8,128)(2,1)S(1)}, u32[]{:S(2)}, u32[]{:S(2)}) %collective-permute-start) | collective-permute-done | bytes 278560 | tf_op jit(solution)/shard_map/ppermute | solution.py:365
  41.3 2.2 %linear.1 = (f32[8,128,128]{2,1,0:T(8,128)S(1)}, f32[8,128,128]{2,1,0:T(8,128)S(1)}, f32[136,128]{1,0:T(8,128)S(1)}, bf16[8,128,128]{2,1,0:T(8,128)(2,1)S(1)}) custom-call(s32[3]{0:T(128)S(1)} %pad_add_fusion.info_ref, bf16[8,400,128]{2,1,0:T(8,128)(2,1)S(1)} %all_to_all.10.own_ref, bf16[4,272,128]{2,1,0:T(8,128)(2,1)S(1)} %collective-permute-done.low_ref, ...), custom_call_target="tpu_custom_call" | custom-call | tf_op jit(solution)/shard_map/linear/pallas_call | solution.py:370
  43.5 1.9 %collective-permute-start.2 = (f32[136,128]{1,0:T(8,128)S(1)}, f32[136,128]{1,0:T(8,128)S(1)}, u32[]{:S(2)}, u32[]{:S(2)}) collective-permute-start(f32[136,128]{1,0:T(8,128)S(1)} %get-tuple-element.43.state_ref), channel_id=1, source_target_pairs={{0,64},{64,128},{128,192},{1,65},{65,129},{129,193},{2,66},{66,130... | collective-permute-start | bytes 208904 | tf_op jit(solution)/shard_map/ppermute | solution.py:381
  45.4 1.3 %collective-permute-start.3 = (f32[136,128]{1,0:T(8,128)S(1)}, f32[136,128]{1,0:T(8,128)S(1)}, u32[]{:S(2)}, u32[]{:S(2)}) collective-permute-start(f32[136,128]{1,0:T(8,128)S(1)} %get-tuple-element.43.state_ref), channel_id=1, source_target_pairs={{0,128},{64,192},{1,129},{65,193},{2,130},{66,194},{3,131},{67,195... | collective-permute-start | bytes 208904 | tf_op jit(solution)/shard_map/ppermute | solution.py:382
  46.7 3.1 %own_window.1 = (f32[1024,128]{1,0:T(8,128)S(1)}, f32[1024,128]{1,0:T(8,128)S(1)}, f32[1024,128]{1,0:T(8,128)S(1)}) custom-call(s32[3]{0:T(128)S(1)} %pad_add_fusion.info_ref, bf16[8,400,128]{2,1,0:T(8,128)(2,1)S(1)} %all_to_all.10.own_ref, bf16[4,272,128]{2,1,0:T(8,128)(2,1)S(1)} %collective-permute-done.low_ref, ...), custom_call_target="tpu_custom_call" | custom-call | tf_op jit(solution)/shard_map/own_window/pallas_call | solution.py:383
  49.9 1.3 %collective-permute-start.4 = (bf16[8,272,128]{2,1,0:T(8,128)(2,1)S(1)}, bf16[8,272,128]{2,1,0:T(8,128)(2,1)S(1)}, u32[]{:S(2)}, u32[]{:S(2)}) collective-permute-start(bf16[8,272,128]{2,1,0:T(8,128)(2,1)S(1)} %slice.24), channel_id=1, source_target_pairs={{0,128},{64,192},{1,129},{65,193},{2,130},{66,194},{3,131},{67,195... | collective-permute-start | bytes 1671176 | tf_op jit(solution)/shard_map/ppermute | solution.py:387
  51.2 2.0 %collective-permute-done.3.far_ref = f32[136,128]{1,0:T(8,128)S(1)} collective-permute-done((f32[136,128]{1,0:T(8,128)S(1)}, f32[136,128]{1,0:T(8,128)S(1)}, u32[]{:S(2)}, u32[]{:S(2)}) %collective-permute-start.3) | collective-permute-done | bytes 69664 | tf_op jit(solution)/shard_map/ppermute | solution.py:382
  53.3 0.5 collective-permute-start.7
  53.8 1.4 %enter.1 = (bf16[8,128,128]{2,1,0:T(8,128)(2,1)S(1)}, f32[8,128]{1,0:T(8,128)S(1)}, s32[8]{0:T(128)S(1)}) custom-call(s32[3]{0:T(128)S(1)} %pad_add_fusion.info_ref, bf16[8,400,128]{2,1,0:T(8,128)(2,1)S(1)} %all_to_all.10.own_ref, f32[8,128,128]{2,1,0:T(8,128)S(1)} %get-tuple-element.41.partial_ref, f32[8,128,128]{2,1,0:T(8,128)S(1)} %get-tuple-element.42.weight_ref, ...), custom_call_target="tpu_custom_call" | custom-call | tf_op jit(solution)/shard_map/enter/pallas_call | solution.py:389
  55.2 1.7 %collective-permute-start.8 = (f32[8,128]{1,0:T(8,128)S(1)}, f32[8,128]{1,0:T(8,128)S(1)}, u32[]{:S(2)}, u32[]{:S(2)}) collective-permute-start(f32[8,128]{1,0:T(8,128)S(1)} %get-tuple-element.65), channel_id=1, source_target_pairs={{0,1},{1,0},{2,3},{3,2},{4,5},{5,4},{6,7},{7,6},{8,9},{9,8},{10,11... | collective-permute-start | bytes 12296 | tf_op jit(solution)/shard_map/ppermute | solution.py:398
  56.9 2.9 %collective-permute-start.9 = (f32[8,128]{1,0:T(8,128)S(1)}, f32[8,128]{1,0:T(8,128)S(1)}, u32[]{:S(2)}, u32[]{:S(2)}) collective-permute-start(f32[8,128]{1,0:T(8,128)S(1)} %get-tuple-element.65), channel_id=1, source_target_pairs={{0,2},{1,3},{2,0},{3,1},{4,6},{5,7},{6,4},{7,5},{8,10},{9,11},{10,... | collective-permute-start | bytes 12296 | tf_op jit(solution)/shard_map/ppermute | solution.py:398
  59.8 0.2 collective-permute-start.10
  60.0 4.5 %near_window.1 = (f32[1024,128]{1,0:T(8,128)S(1)}, f32[1024,128]{1,0:T(8,128)S(1)}, f32[1024,128]{1,0:T(8,128)S(1)}) custom-call(s32[8]{0:T(128)S(1)} %get-tuple-element.53.need_ref, bf16[8,400,128]{2,1,0:T(8,128)(2,1)S(1)} %all_to_all.10.own_ref, bf16[8,128,128]{2,1,0:T(8,128)(2,1)S(1)} %get-tuple-element.44.mark_ref, ...), custom_call_target="tpu_custom_call" | custom-call | tf_op jit(solution)/shard_map/near_window/pallas_call | solution.py:399
  64.5 0.1 collective-permute-done.10
  64.6 3.3 %collective-permute-done.4.far_ref = bf16[8,272,128]{2,1,0:T(8,128)(2,1)S(1)} collective-permute-done((bf16[8,272,128]{2,1,0:T(8,128)(2,1)S(1)}, bf16[8,272,128]{2,1,0:T(8,128)(2,1)S(1)}, u32[]{:S(2)}, u32[]{:S(2)}) %collective-permute-start.4) | collective-permute-done | bytes 557088 | tf_op jit(solution)/shard_map/ppermute | solution.py:387
  67.9 2.7 %far_own.1 = (f32[1024,128]{1,0:T(8,128)S(1)}, f32[1024,128]{1,0:T(8,128)S(1)}, f32[1024,128]{1,0:T(8,128)S(1)}) custom-call(s32[3]{0:T(128)S(1)} %pad_add_fusion.info_ref, s32[8]{0:T(128)S(1)} %get-tuple-element.53.need_ref, bf16[8,400,128]{2,1,0:T(8,128)(2,1)S(1)} %all_to_all.10.own_ref, bf16[8,128,128]{2,1,0:T(8,128)(2,1)S(1)} %get-tuple-element.44.mark_ref, ...), custom_call_target="tpu_custom_call" | custom-call | tf_op jit(solution)/shard_map/far_own/pallas_call | solution.py:405
  70.7 2.8 %far_other.1 = bf16[8,272,128]{2,1,0:T(8,128)(2,1)S(1)} custom-call(s32[3]{0:T(128)S(1)} %pad_add_fusion.info_ref, s32[8]{0:T(128)S(1)} %get-tuple-element.53.need_ref, bf16[8,400,128]{2,1,0:T(8,128)(2,1)S(1)} %all_to_all.10.own_ref, bf16[8,128,128]{2,1,0:T(8,128)(2,1)S(1)} %get-tuple-element.44.mark_ref, ...), custom_call_target="tpu_custom_call" | custom-call | tf_op jit(solution)/shard_map/far_other/pallas_call | solution.py:406
  73.5 21.5 %all_to_all.11.got_ref = bf16[8,272,128]{2,1,0:T(8,128)(2,1)S(1)} all-to-all(bf16[8,272,128]{2,1,0:T(8,128)(2,1)S(1)} %far_other.1), channel_id=1, replica_groups=mesh['x'=4,'z'=8,'core'=2,'head'=4] {'z'}, dimensions={0} | all-to-all | bytes 1114112 | tf_op jit(solution)/shard_map/all_to_all | solution.py:413
  95.0 0.9 finish.1
  (20 shorter events, 0.3 us)
Async XLA Ops:
  0.0 39.7 %copy-start = (f32[8,128,128]{2,1,0:T(8,128)S(1)}, f32[8,128,128]{2,1,0:T(8,128)}, u32[]{:S(2)}) copy-start(f32[8,128,128]{2,1,0:T(8,128)} %param.13) | copy-start | bytes 1572868
  35.3 17.9 %collective-permute-start.5 = (bf16[8,272,128]{2,1,0:T(8,128)(2,1)S(1)}, bf16[8,272,128]{2,1,0:T(8,128)(2,1)S(1)}, u32[]{:S(2)}, u32[]{:S(2)}) collective-permute-start(bf16[8,272,128]{2,1,0:T(8,128)(2,1)S(1)} %slice.24), channel_id=1, source_target_pairs={{0,64},{64,128},{128,192},{1,65},{65,129},{129,193},{2,66},{66,130... | collective-permute-start | bytes 1671176 | tf_op jit(solution)/shard_map/ppermute | solution.py:364
  39.1 2.1 %collective-permute-start = (bf16[4,272,128]{2,1,0:T(8,128)(2,1)}, bf16[4,272,128]{2,1,0:T(8,128)(2,1)S(1)}, u32[]{:S(2)}, u32[]{:S(2)}) collective-permute-start(bf16[4,272,128]{2,1,0:T(8,128)(2,1)} %get-tuple-element.78), channel_id=1, source_target_pairs={{0,4},{4,0},{1,5},{5,1},{2,6},{6,2},{3,7},{7,3},{8,12},{12,8},{9,1... | collective-permute-start | bytes 835592 | tf_op jit(solution)/shard_map/ppermute | solution.py:365
  39.1 2.1 %collective-permute-start.1 = (bf16[4,272,128]{2,1,0:T(8,128)(2,1)S(1)}, bf16[4,272,128]{2,1,0:T(8,128)(2,1)S(1)}, u32[]{:S(2)}, u32[]{:S(2)}) collective-permute-start(bf16[4,272,128]{2,1,0:T(8,128)(2,1)S(1)} %get-tuple-element.77), channel_id=1, source_target_pairs={{0,4},{4,0},{1,5},{5,1},{2,6},{6,2},{3,7},{7,3},{8,12},{12,8},{9,1... | collective-permute-start | bytes 835592 | tf_op jit(solution)/shard_map/ppermute | solution.py:365
  43.5 7.7 %collective-permute-start.2 = (f32[136,128]{1,0:T(8,128)S(1)}, f32[136,128]{1,0:T(8,128)S(1)}, u32[]{:S(2)}, u32[]{:S(2)}) collective-permute-start(f32[136,128]{1,0:T(8,128)S(1)} %get-tuple-element.43.state_ref), channel_id=1, source_target_pairs={{0,64},{64,128},{128,192},{1,65},{65,129},{129,193},{2,66},{66,130... | collective-permute-start | bytes 208904 | tf_op jit(solution)/shard_map/ppermute | solution.py:381
  45.4 7.7 %collective-permute-start.3 = (f32[136,128]{1,0:T(8,128)S(1)}, f32[136,128]{1,0:T(8,128)S(1)}, u32[]{:S(2)}, u32[]{:S(2)}) collective-permute-start(f32[136,128]{1,0:T(8,128)S(1)} %get-tuple-element.43.state_ref), channel_id=1, source_target_pairs={{0,128},{64,192},{1,129},{65,193},{2,130},{66,194},{3,131},{67,195... | collective-permute-start | bytes 208904 | tf_op jit(solution)/shard_map/ppermute | solution.py:382
  49.9 18.1 %collective-permute-start.4 = (bf16[8,272,128]{2,1,0:T(8,128)(2,1)S(1)}, bf16[8,272,128]{2,1,0:T(8,128)(2,1)S(1)}, u32[]{:S(2)}, u32[]{:S(2)}) collective-permute-start(bf16[8,272,128]{2,1,0:T(8,128)(2,1)S(1)} %slice.24), channel_id=1, source_target_pairs={{0,128},{64,192},{1,129},{65,193},{2,130},{66,194},{3,131},{67,195... | collective-permute-start | bytes 1671176 | tf_op jit(solution)/shard_map/ppermute | solution.py:387
  53.2 6.6 %collective-permute-start.6 = (bf16[4,272,128]{2,1,0:T(8,128)(2,1)S(1)}, bf16[4,272,128]{2,1,0:T(8,128)(2,1)S(1)}, u32[]{:S(2)}, u32[]{:S(2)}) collective-permute-start(bf16[4,272,128]{2,1,0:T(8,128)(2,1)S(1)} %get-tuple-element.80), channel_id=1, source_target_pairs={{0,4},{4,0},{1,5},{5,1},{2,6},{6,2},{3,7},{7,3},{8,12},{12,8},{9,1... | collective-permute-start | bytes 835592 | tf_op jit(solution)/shard_map/ppermute | solution.py:397
  53.3 6.7 %collective-permute-start.7 = (bf16[4,272,128]{2,1,0:T(8,128)(2,1)S(1)}, bf16[4,272,128]{2,1,0:T(8,128)(2,1)S(1)}, u32[]{:S(2)}, u32[]{:S(2)}) collective-permute-start(bf16[4,272,128]{2,1,0:T(8,128)(2,1)S(1)} %get-tuple-element.79), channel_id=1, source_target_pairs={{0,4},{4,0},{1,5},{5,1},{2,6},{6,2},{3,7},{7,3},{8,12},{12,8},{9,1... | collective-permute-start | bytes 835592 | tf_op jit(solution)/shard_map/ppermute | solution.py:397
  55.2 9.3 %collective-permute-start.8 = (f32[8,128]{1,0:T(8,128)S(1)}, f32[8,128]{1,0:T(8,128)S(1)}, u32[]{:S(2)}, u32[]{:S(2)}) collective-permute-start(f32[8,128]{1,0:T(8,128)S(1)} %get-tuple-element.65), channel_id=1, source_target_pairs={{0,1},{1,0},{2,3},{3,2},{4,5},{5,4},{6,7},{7,6},{8,9},{9,8},{10,11... | collective-permute-start | bytes 12296 | tf_op jit(solution)/shard_map/ppermute | solution.py:398
  56.9 7.6 %collective-permute-start.9 = (f32[8,128]{1,0:T(8,128)S(1)}, f32[8,128]{1,0:T(8,128)S(1)}, u32[]{:S(2)}, u32[]{:S(2)}) collective-permute-start(f32[8,128]{1,0:T(8,128)S(1)} %get-tuple-element.65), channel_id=1, source_target_pairs={{0,2},{1,3},{2,0},{3,1},{4,6},{5,7},{6,4},{7,5},{8,10},{9,11},{10,... | collective-permute-start | bytes 12296 | tf_op jit(solution)/shard_map/ppermute | solution.py:398
  59.8 4.8 %collective-permute-start.10 = (f32[8,128]{1,0:T(8,128)S(1)}, f32[8,128]{1,0:T(8,128)S(1)}, u32[]{:S(2)}, u32[]{:S(2)}) collective-permute-start(f32[8,128]{1,0:T(8,128)S(1)} %get-tuple-element.65), channel_id=1, source_target_pairs={{0,3},{1,2},{2,1},{3,0},{4,7},{5,6},{6,5},{7,4},{8,11},{9,10},{10,... | collective-permute-start | bytes 12296 | tf_op jit(solution)/shard_map/ppermute | solution.py:398
  67.9 2.7 %collective-permute-start.11 = (bf16[8,272,128]{2,1,0:T(8,128)(2,1)S(1)}, bf16[8,272,128]{2,1,0:T(8,128)(2,1)S(1)}, u32[]{:S(2)}, u32[]{:S(2)}) collective-permute-start(bf16[8,272,128]{2,1,0:T(8,128)(2,1)S(1)} %collective-permute-done.4.far_ref), channel_id=1, source_target_pairs={{0,4},{4,0},{1,5},{5,1},{2,6},{6,2},{3,7},{7,3},{8,12},{12,8},{9,1... | collective-permute-start | bytes 1671176 | tf_op jit(solution)/shard_map/ppermute | solution.py:404
  73.5 21.5 %copy-start.1 = (f32[1024]{0:T(1024)S(1)}, f32[1024]{0:T(1024)}, u32[]{:S(2)}) copy-start(f32[1024]{0:T(1024)} %param.14) | copy-start | bytes 12292

commit v9 on v8

--- a/solution.py
+++ b/solution.py
@@ -383,7 +383,7 @@
     own_part = call(
         own_window_kernel, "own_window", [SMEM] + [VMEM] * 4, part_shapes
     )(info, own, *other, mark)
-    sent, own_part = lax.optimization_barrier((sent, own_part))
+    sent, partial = lax.optimization_barrier((sent, partial))
     far = lax.ppermute(sent, "x", [(0, 2), (1, 3)])
     near_state, far_state, own_part = lax.optimization_barrier((near_state, far_state, own_part))
     linear, square, need = call(

time: 96.2 us -> 93.9 us (0.976)
  waiting for transfers between devices: 6.94 us -> 4.09 us
    ppermute x1, waiting for transfers between devices: 3.32 us -> 0.12 us  [body(): far = lax.ppermute(sent, 'x', [(0, 2), (1, 3)])]
where the time goes in v9:
time: 93.9 us; the launch traced here: 93.6 us
  blocking collectives  54.4 us (58%)
  Pallas kernels  20.6 us (22%)
  starting transfers between devices  13.5 us (14%)
  waiting for transfers between devices  4.09 us (4%)
    all_to_all x1, blocking collectives, body(): own = lax.all_to_all(packed, 'z', 0, 0, tiled=True)  32.3 us
    all_to_all x1, blocking collectives, body(): back = lax.all_to_all(mixed, 'z', 0, 0, tiled=True)  22.1 us
    ppermute x3, starting transfers between devices, body(): lax.ppermute(square, 'head', [(i, i ^ step) for i in range(4)])  4.79 us
    pallas_call x1, Pallas kernels, body(): call(near_kernel, 'near_window', [SMEM] + [VMEM] * 8, part_shapes)  4.47 us
    pallas_call x1, Pallas kernels, body(): call(own_window_kernel, 'own_window', [SMEM] + [VMEM] * 4, part_shapes)  3.12 us
    ppermute x1, starting transfers between devices, body(): near = lax.ppermute(sent, 'x', [(0, 1), (1, 2), (2, 3)])  3.11 us
    pallas_call x1, Pallas kernels, body(): call(prepare_kernel, 'prepare', [SMEM, SMEM, HBM, HBM, HBM, VMEM, VMEM, V...  2.94 us
    pallas_call x1, Pallas kernels, body(): call(far_other_kernel, 'far_other', [SMEM] * 2 + [VMEM] * 8, shape((HEADS...  2.81 us
  transfers between devices with their start and end apart: 12, of which 4 were waited for; matrix products, arithmetic and copies ran while one was open for 1% of the time, Pallas kernels for 15%

profile of v9, /device:TPU:4, one launch (start us, length us, event | category | flops | bytes accessed | tf_op | source)
XLA Modules:
  0.0 93.6 jit_solution(1262012894698232337)
XLA Ops:
  0.0 2.9 %prepare.1 = bf16[8,400,128]{2,1,0:T(8,128)(2,1)} custom-call(f32[16]{0:T(128)} %table_ref.1, s32[8]{0:T(128)} %index_ref.1, bf16[128,1024]{1,0:T(8,128)(2,1)} %q_hbm.1, bf16[128,1024]{1,0:T(8,128)(2,1)} %k_hbm.1, bf16[128,1024]{1,0:T(8,128)(2,1)} %v_hbm.1, f32[8,128]{1,0:T(8,128)} %bitcast.8, f32[8,128]{1,0:T(8,128)} %bitcast.9, s32[1,128]{1,0:T(1,128)} %bitcast.10), custom_call_target="tpu_custom_call" | custom-call | tf_op jit(solution)/shard_map/prepare/pallas_call | solution.py:354
  3.0 32.3 %all_to_all.10.own_ref = bf16[8,400,128]{2,1,0:T(8,128)(2,1)S(1)} all-to-all(bf16[8,400,128]{2,1,0:T(8,128)(2,1)} %prepare.1), channel_id=1, replica_groups=mesh['x'=4,'z'=8,'core'=2,'head'=4] {'z'}, dimensions={0} | all-to-all | bytes 1638400 | tf_op jit(solution)/shard_map/all_to_all | solution.py:361
  35.3 3.1 %collective-permute-start.5 = (bf16[8,272,128]{2,1,0:T(8,128)(2,1)S(1)}, bf16[8,272,128]{2,1,0:T(8,128)(2,1)S(1)}, u32[]{:S(2)}, u32[]{:S(2)}) collective-permute-start(bf16[8,272,128]{2,1,0:T(8,128)(2,1)S(1)} %slice.22), channel_id=1, source_target_pairs={{0,64},{64,128},{128,192},{1,65},{65,129},{129,193},{2,66},{66,130... | collective-permute-start | bytes 1671176 | tf_op jit(solution)/shard_map/ppermute | solution.py:364
  38.4 0.7 fusion
  39.1 0.5 collective-permute-start.1
  39.7 1.5 %collective-permute-done.low_ref = bf16[4,272,128]{2,1,0:T(8,128)(2,1)S(1)} collective-permute-done((bf16[4,272,128]{2,1,0:T(8,128)(2,1)}, bf16[4,272,128]{2,1,0:T(8,128)(2,1)S(1)}, u32[]{:S(2)}, u32[]{:S(2)}) %collective-permute-start) | collective-permute-done | bytes 278560 | tf_op jit(solution)/shard_map/ppermute | solution.py:365
  41.3 2.2 %linear.1 = (f32[8,128,128]{2,1,0:T(8,128)S(1)}, f32[8,128,128]{2,1,0:T(8,128)S(1)}, f32[136,128]{1,0:T(8,128)S(1)}, bf16[8,128,128]{2,1,0:T(8,128)(2,1)S(1)}) custom-call(s32[3]{0:T(128)S(1)} %pad_add_fusion.info_ref, bf16[8,400,128]{2,1,0:T(8,128)(2,1)S(1)} %all_to_all.10.own_ref, bf16[4,272,128]{2,1,0:T(8,128)(2,1)S(1)} %collective-permute-done.low_ref, ...), custom_call_target="tpu_custom_call" | custom-call | tf_op jit(solution)/shard_map/linear/pallas_call | solution.py:370
  43.5 1.9 %collective-permute-start.2 = (f32[136,128]{1,0:T(8,128)S(1)}, f32[136,128]{1,0:T(8,128)S(1)}, u32[]{:S(2)}, u32[]{:S(2)}) collective-permute-start(f32[136,128]{1,0:T(8,128)S(1)} %get-tuple-element.42.state_ref), channel_id=1, source_target_pairs={{0,64},{64,128},{128,192},{1,65},{65,129},{129,193},{2,66},{66,130... | collective-permute-start | bytes 208904 | tf_op jit(solution)/shard_map/ppermute | solution.py:381
  45.4 1.3 %collective-permute-start.3 = (f32[136,128]{1,0:T(8,128)S(1)}, f32[136,128]{1,0:T(8,128)S(1)}, u32[]{:S(2)}, u32[]{:S(2)}) collective-permute-start(f32[136,128]{1,0:T(8,128)S(1)} %get-tuple-element.42.state_ref), channel_id=1, source_target_pairs={{0,128},{64,192},{1,129},{65,193},{2,130},{66,194},{3,131},{67,195... | collective-permute-start | bytes 208904 | tf_op jit(solution)/shard_map/ppermute | solution.py:382
  46.7 1.3 %collective-permute-start.4 = (bf16[8,272,128]{2,1,0:T(8,128)(2,1)S(1)}, bf16[8,272,128]{2,1,0:T(8,128)(2,1)S(1)}, u32[]{:S(2)}, u32[]{:S(2)}) collective-permute-start(bf16[8,272,128]{2,1,0:T(8,128)(2,1)S(1)} %slice.22), channel_id=1, source_target_pairs={{0,128},{64,192},{1,129},{65,193},{2,130},{66,194},{3,131},{67,195... | collective-permute-start | bytes 1671176 | tf_op jit(solution)/shard_map/ppermute | solution.py:387
  48.0 3.1 %own_window.1 = (f32[1024,128]{1,0:T(8,128)S(1)}, f32[1024,128]{1,0:T(8,128)S(1)}, f32[1024,128]{1,0:T(8,128)S(1)}) custom-call(s32[3]{0:T(128)S(1)} %pad_add_fusion.info_ref, bf16[8,400,128]{2,1,0:T(8,128)(2,1)S(1)} %all_to_all.10.own_ref, bf16[4,272,128]{2,1,0:T(8,128)(2,1)S(1)} %collective-permute-done.low_ref, ...), custom_call_target="tpu_custom_call" | custom-call | tf_op jit(solution)/shard_map/own_window/pallas_call | solution.py:383
  51.2 2.3 %collective-permute-done.3.far_ref = f32[136,128]{1,0:T(8,128)S(1)} collective-permute-done((f32[136,128]{1,0:T(8,128)S(1)}, f32[136,128]{1,0:T(8,128)S(1)}, u32[]{:S(2)}, u32[]{:S(2)}) %collective-permute-start.3) | collective-permute-done | bytes 69664 | tf_op jit(solution)/shard_map/ppermute | solution.py:382
  53.5 0.1 collective-permute-start.6
  53.6 0.5 collective-permute-start.7
  54.1 1.4 %enter.1 = (bf16[8,128,128]{2,1,0:T(8,128)(2,1)S(1)}, f32[8,128]{1,0:T(8,128)S(1)}, s32[8]{0:T(128)S(1)}) custom-call(s32[3]{0:T(128)S(1)} %pad_add_fusion.info_ref, bf16[8,400,128]{2,1,0:T(8,128)(2,1)S(1)} %all_to_all.10.own_ref, f32[8,128,128]{2,1,0:T(8,128)S(1)} %get-tuple-element.40.partial_ref, f32[8,128,128]{2,1,0:T(8,128)S(1)} %get-tuple-element.41.weight_ref, ...), custom_call_target="tpu_custom_call" | custom-call | tf_op jit(solution)/shard_map/enter/pallas_call | solution.py:389
  55.6 1.7 %collective-permute-start.8 = (f32[8,128]{1,0:T(8,128)S(1)}, f32[8,128]{1,0:T(8,128)S(1)}, u32[]{:S(2)}, u32[]{:S(2)}) collective-permute-start(f32[8,128]{1,0:T(8,128)S(1)} %get-tuple-element.61), channel_id=1, source_target_pairs={{0,1},{1,0},{2,3},{3,2},{4,5},{5,4},{6,7},{7,6},{8,9},{9,8},{10,11... | collective-permute-start | bytes 12296 | tf_op jit(solution)/shard_map/ppermute | solution.py:398
  57.3 2.9 %collective-permute-start.9 = (f32[8,128]{1,0:T(8,128)S(1)}, f32[8,128]{1,0:T(8,128)S(1)}, u32[]{:S(2)}, u32[]{:S(2)}) collective-permute-start(f32[8,128]{1,0:T(8,128)S(1)} %get-tuple-element.61), channel_id=1, source_target_pairs={{0,2},{1,3},{2,0},{3,1},{4,6},{5,7},{6,4},{7,5},{8,10},{9,11},{10,... | collective-permute-start | bytes 12296 | tf_op jit(solution)/shard_map/ppermute | solution.py:398
  60.1 0.2 collective-permute-start.10
  60.4 4.5 %near_window.1 = (f32[1024,128]{1,0:T(8,128)S(1)}, f32[1024,128]{1,0:T(8,128)S(1)}, f32[1024,128]{1,0:T(8,128)S(1)}) custom-call(s32[8]{0:T(128)S(1)} %get-tuple-element.49.need_ref, bf16[8,400,128]{2,1,0:T(8,128)(2,1)S(1)} %all_to_all.10.own_ref, bf16[8,128,128]{2,1,0:T(8,128)(2,1)S(1)} %get-tuple-element.43.mark_ref, ...), custom_call_target="tpu_custom_call" | custom-call | tf_op jit(solution)/shard_map/near_window/pallas_call | solution.py:399
  65.0 0.1 collective-permute-done.4.far_ref
  65.1 2.7 %far_own.1 = (f32[1024,128]{1,0:T(8,128)S(1)}, f32[1024,128]{1,0:T(8,128)S(1)}, f32[1024,128]{1,0:T(8,128)S(1)}) custom-call(s32[3]{0:T(128)S(1)} %pad_add_fusion.info_ref, s32[8]{0:T(128)S(1)} %get-tuple-element.49.need_ref, bf16[8,400,128]{2,1,0:T(8,128)(2,1)S(1)} %all_to_all.10.own_ref, bf16[8,128,128]{2,1,0:T(8,128)(2,1)S(1)} %get-tuple-element.43.mark_ref, ...), custom_call_target="tpu_custom_call" | custom-call | tf_op jit(solution)/shard_map/far_own/pallas_call | solution.py:405
  67.8 2.8 %far_other.1 = bf16[8,272,128]{2,1,0:T(8,128)(2,1)S(1)} custom-call(s32[3]{0:T(128)S(1)} %pad_add_fusion.info_ref, s32[8]{0:T(128)S(1)} %get-tuple-element.49.need_ref, bf16[8,400,128]{2,1,0:T(8,128)(2,1)S(1)} %all_to_all.10.own_ref, bf16[8,128,128]{2,1,0:T(8,128)(2,1)S(1)} %get-tuple-element.43.mark_ref, ...), custom_call_target="tpu_custom_call" | custom-call | tf_op jit(solution)/shard_map/far_other/pallas_call | solution.py:406
  70.7 22.1 %all_to_all.11.got_ref = bf16[8,272,128]{2,1,0:T(8,128)(2,1)S(1)} all-to-all(bf16[8,272,128]{2,1,0:T(8,128)(2,1)S(1)} %far_other.1), channel_id=1, replica_groups=mesh['x'=4,'z'=8,'core'=2,'head'=4] {'z'}, dimensions={0} | all-to-all | bytes 1114112 | tf_op jit(solution)/shard_map/all_to_all | solution.py:413
  92.8 0.9 finish.1
  (20 shorter events, 0.3 us)
Async XLA Ops:
  0.0 39.7 %copy-start = (f32[8,128,128]{2,1,0:T(8,128)S(1)}, f32[8,128,128]{2,1,0:T(8,128)}, u32[]{:S(2)}) copy-start(f32[8,128,128]{2,1,0:T(8,128)} %param.13) | copy-start | bytes 1572868
  35.3 18.2 %collective-permute-start.5 = (bf16[8,272,128]{2,1,0:T(8,128)(2,1)S(1)}, bf16[8,272,128]{2,1,0:T(8,128)(2,1)S(1)}, u32[]{:S(2)}, u32[]{:S(2)}) collective-permute-start(bf16[8,272,128]{2,1,0:T(8,128)(2,1)S(1)} %slice.22), channel_id=1, source_target_pairs={{0,64},{64,128},{128,192},{1,65},{65,129},{129,193},{2,66},{66,130... | collective-permute-start | bytes 1671176 | tf_op jit(solution)/shard_map/ppermute | solution.py:364
  39.1 2.1 %collective-permute-start = (bf16[4,272,128]{2,1,0:T(8,128)(2,1)}, bf16[4,272,128]{2,1,0:T(8,128)(2,1)S(1)}, u32[]{:S(2)}, u32[]{:S(2)}) collective-permute-start(bf16[4,272,128]{2,1,0:T(8,128)(2,1)} %get-tuple-element.74), channel_id=1, source_target_pairs={{0,4},{4,0},{1,5},{5,1},{2,6},{6,2},{3,7},{7,3},{8,12},{12,8},{9,1... | collective-permute-start | bytes 835592 | tf_op jit(solution)/shard_map/ppermute | solution.py:365
  39.1 2.1 %collective-permute-start.1 = (bf16[4,272,128]{2,1,0:T(8,128)(2,1)S(1)}, bf16[4,272,128]{2,1,0:T(8,128)(2,1)S(1)}, u32[]{:S(2)}, u32[]{:S(2)}) collective-permute-start(bf16[4,272,128]{2,1,0:T(8,128)(2,1)S(1)} %get-tuple-element.73), channel_id=1, source_target_pairs={{0,4},{4,0},{1,5},{5,1},{2,6},{6,2},{3,7},{7,3},{8,12},{12,8},{9,1... | collective-permute-start | bytes 835592 | tf_op jit(solution)/shard_map/ppermute | solution.py:365
  43.5 7.7 %collective-permute-start.2 = (f32[136,128]{1,0:T(8,128)S(1)}, f32[136,128]{1,0:T(8,128)S(1)}, u32[]{:S(2)}, u32[]{:S(2)}) collective-permute-start(f32[136,128]{1,0:T(8,128)S(1)} %get-tuple-element.42.state_ref), channel_id=1, source_target_pairs={{0,64},{64,128},{128,192},{1,65},{65,129},{129,193},{2,66},{66,130... | collective-permute-start | bytes 208904 | tf_op jit(solution)/shard_map/ppermute | solution.py:381
  45.4 8.1 %collective-permute-start.3 = (f32[136,128]{1,0:T(8,128)S(1)}, f32[136,128]{1,0:T(8,128)S(1)}, u32[]{:S(2)}, u32[]{:S(2)}) collective-permute-start(f32[136,128]{1,0:T(8,128)S(1)} %get-tuple-element.42.state_ref), channel_id=1, source_target_pairs={{0,128},{64,192},{1,129},{65,193},{2,130},{66,194},{3,131},{67,195... | collective-permute-start | bytes 208904 | tf_op jit(solution)/shard_map/ppermute | solution.py:382
  46.7 18.3 %collective-permute-start.4 = (bf16[8,272,128]{2,1,0:T(8,128)(2,1)S(1)}, bf16[8,272,128]{2,1,0:T(8,128)(2,1)S(1)}, u32[]{:S(2)}, u32[]{:S(2)}) collective-permute-start(bf16[8,272,128]{2,1,0:T(8,128)(2,1)S(1)} %slice.22), channel_id=1, source_target_pairs={{0,128},{64,192},{1,129},{65,193},{2,130},{66,194},{3,131},{67,195... | collective-permute-start | bytes 1671176 | tf_op jit(solution)/shard_map/ppermute | solution.py:387
  53.5 6.6 %collective-permute-start.6 = (bf16[4,272,128]{2,1,0:T(8,128)(2,1)S(1)}, bf16[4,272,128]{2,1,0:T(8,128)(2,1)S(1)}, u32[]{:S(2)}, u32[]{:S(2)}) collective-permute-start(bf16[4,272,128]{2,1,0:T(8,128)(2,1)S(1)} %get-tuple-element.76), channel_id=1, source_target_pairs={{0,4},{4,0},{1,5},{5,1},{2,6},{6,2},{3,7},{7,3},{8,12},{12,8},{9,1... | collective-permute-start | bytes 835592 | tf_op jit(solution)/shard_map/ppermute | solution.py:397
  53.6 6.7 %collective-permute-start.7 = (bf16[4,272,128]{2,1,0:T(8,128)(2,1)S(1)}, bf16[4,272,128]{2,1,0:T(8,128)(2,1)S(1)}, u32[]{:S(2)}, u32[]{:S(2)}) collective-permute-start(bf16[4,272,128]{2,1,0:T(8,128)(2,1)S(1)} %get-tuple-element.75), channel_id=1, source_target_pairs={{0,4},{4,0},{1,5},{5,1},{2,6},{6,2},{3,7},{7,3},{8,12},{12,8},{9,1... | collective-permute-start | bytes 835592 | tf_op jit(solution)/shard_map/ppermute | solution.py:397
  55.6 9.3 %collective-permute-start.8 = (f32[8,128]{1,0:T(8,128)S(1)}, f32[8,128]{1,0:T(8,128)S(1)}, u32[]{:S(2)}, u32[]{:S(2)}) collective-permute-start(f32[8,128]{1,0:T(8,128)S(1)} %get-tuple-element.61), channel_id=1, source_target_pairs={{0,1},{1,0},{2,3},{3,2},{4,5},{5,4},{6,7},{7,6},{8,9},{9,8},{10,11... | collective-permute-start | bytes 12296 | tf_op jit(solution)/shard_map/ppermute | solution.py:398
  57.3 7.6 %collective-permute-start.9 = (f32[8,128]{1,0:T(8,128)S(1)}, f32[8,128]{1,0:T(8,128)S(1)}, u32[]{:S(2)}, u32[]{:S(2)}) collective-permute-start(f32[8,128]{1,0:T(8,128)S(1)} %get-tuple-element.61), channel_id=1, source_target_pairs={{0,2},{1,3},{2,0},{3,1},{4,6},{5,7},{6,4},{7,5},{8,10},{9,11},{10,... | collective-permute-start | bytes 12296 | tf_op jit(solution)/shard_map/ppermute | solution.py:398
  60.1 4.8 %collective-permute-start.10 = (f32[8,128]{1,0:T(8,128)S(1)}, f32[8,128]{1,0:T(8,128)S(1)}, u32[]{:S(2)}, u32[]{:S(2)}) collective-permute-start(f32[8,128]{1,0:T(8,128)S(1)} %get-tuple-element.61), channel_id=1, source_target_pairs={{0,3},{1,2},{2,1},{3,0},{4,7},{5,6},{6,5},{7,4},{8,11},{9,10},{10,... | collective-permute-start | bytes 12296 | tf_op jit(solution)/shard_map/ppermute | solution.py:398
  65.1 2.7 %collective-permute-start.11 = (bf16[8,272,128]{2,1,0:T(8,128)(2,1)S(1)}, bf16[8,272,128]{2,1,0:T(8,128)(2,1)S(1)}, u32[]{:S(2)}, u32[]{:S(2)}) collective-permute-start(bf16[8,272,128]{2,1,0:T(8,128)(2,1)S(1)} %collective-permute-done.4.far_ref), channel_id=1, source_target_pairs={{0,4},{4,0},{1,5},{5,1},{2,6},{6,2},{3,7},{7,3},{8,12},{12,8},{9,1... | collective-permute-start | bytes 1671176 | tf_op jit(solution)/shard_map/ppermute | solution.py:404
  70.6 22.1 %copy-start.1 = (f32[1024]{0:T(1024)S(1)}, f32[1024]{0:T(1024)}, u32[]{:S(2)}) copy-start(f32[1024]{0:T(1024)} %param.14) | copy-start | bytes 12292

commit v10 on v9

--- a/solution.py
+++ b/solution.py
@@ -362,7 +362,10 @@
     sent = own[:, :KV_ROWS]
     pair = [(0, 1), (1, 0)]
     near = lax.ppermute(sent, "x", [(0, 1), (1, 2), (2, 3)])
-    other = [lax.ppermute(sent[at : at + TILES], "core", pair) for at in (0, TILES)]
+    other = [
+        lax.ppermute(own[:TILES, :KV_ROWS], "core", pair),
+        lax.ppermute(lax.optimization_barrier(own)[TILES:, :KV_ROWS], "core", pair),
+    ]
 
     tokens = HEADS * TOK
     part_shapes = [shape((tokens, TOK), F32), shape((tokens, TOK), F32), shape((tokens, DH), F32)]

time: 93.9 us -> 93.4 us (level)
  blocking collectives: 54.4 us -> 53.4 us
    all_to_all x1, blocking collectives: 22.1 us -> 21.1 us  [body(): back = lax.all_to_all(mixed, 'z', 0, 0, tiled=True)]
  transfers between devices with their start and end apart: 12 -> 12, of which waited for: 4 -> 5; matrix products, arithmetic and copies ran while one was open for 1% -> 1% of each run, Pallas kernels for 15% -> 15%
where the time goes in v10:
time: 93.4 us; the launch traced here: 92.6 us
  blocking collectives  53.4 us (57%)
  Pallas kernels  20.6 us (22%)
  starting transfers between devices  13.6 us (15%)
  waiting for transfers between devices  3.98 us (4%)
    all_to_all x1, blocking collectives, body(): own = lax.all_to_all(packed, 'z', 0, 0, tiled=True)  32.3 us
    all_to_all x1, blocking collectives, body(): back = lax.all_to_all(mixed, 'z', 0, 0, tiled=True)  21.1 us
    ppermute x3, starting transfers between devices, body(): lax.ppermute(square, 'head', [(i, i ^ step) for i in range(4)])  4.79 us
    pallas_call x1, Pallas kernels, body(): call(near_kernel, 'near_window', [SMEM] + [VMEM] * 8, part_shapes)  4.47 us
    pallas_call x1, Pallas kernels, body(): call(own_window_kernel, 'own_window', [SMEM] + [VMEM] * 4, part_shapes)  3.14 us
    ppermute x1, starting transfers between devices, body(): near = lax.ppermute(sent, 'x', [(0, 1), (1, 2), (2, 3)])  3.11 us
    pallas_call x1, Pallas kernels, body(): call(prepare_kernel, 'prepare', [SMEM, SMEM, HBM, HBM, HBM, VMEM, VMEM, V...  2.93 us
    pallas_call x1, Pallas kernels, body(): call(far_other_kernel, 'far_other', [SMEM] * 2 + [VMEM] * 8, shape((HEADS...  2.81 us
  transfers between devices with their start and end apart: 12, of which 5 were waited for; matrix products, arithmetic and copies ran while one was open for 1% of the time, Pallas kernels for 15%

profile of v10, /device:TPU:4, one launch (start us, length us, event | category | flops | bytes accessed | tf_op | source)
XLA Modules:
  0.0 92.6 jit_solution(18038394587095198136)
XLA Ops:
  0.0 2.9 %prepare.1 = bf16[8,400,128]{2,1,0:T(8,128)(2,1)} custom-call(f32[16]{0:T(128)} %table_ref.1, s32[8]{0:T(128)} %index_ref.1, bf16[128,1024]{1,0:T(8,128)(2,1)} %q_hbm.1, bf16[128,1024]{1,0:T(8,128)(2,1)} %k_hbm.1, bf16[128,1024]{1,0:T(8,128)(2,1)} %v_hbm.1, f32[8,128]{1,0:T(8,128)} %bitcast.8, f32[8,128]{1,0:T(8,128)} %bitcast.9, s32[1,128]{1,0:T(1,128)} %bitcast.10), custom_call_target="tpu_custom_call" | custom-call | tf_op jit(solution)/shard_map/prepare/pallas_call | solution.py:354
  2.9 32.3 %all_to_all.10.own_ref = bf16[8,400,128]{2,1,0:T(8,128)(2,1)S(1)} all-to-all(bf16[8,400,128]{2,1,0:T(8,128)(2,1)} %prepare.1), channel_id=1, replica_groups=mesh['x'=4,'z'=8,'core'=2,'head'=4] {'z'}, dimensions={0} | all-to-all | bytes 1638400 | tf_op jit(solution)/shard_map/all_to_all | solution.py:361
  35.3 3.1 %collective-permute-start.5 = (bf16[8,272,128]{2,1,0:T(8,128)(2,1)S(1)}, bf16[8,272,128]{2,1,0:T(8,128)(2,1)S(1)}, u32[]{:S(2)}, u32[]{:S(2)}) collective-permute-start(bf16[8,272,128]{2,1,0:T(8,128)(2,1)S(1)} %slice.20), channel_id=1, source_target_pairs={{0,64},{64,128},{128,192},{1,65},{65,129},{129,193},{2,66},{66,130... | collective-permute-start | bytes 1671176 | tf_op jit(solution)/shard_map/ppermute | solution.py:364
  38.5 0.7 slice.22
  39.2 0.5 collective-permute-start.1
  39.8 0.2 collective-permute-done.low_ref
  40.1 1.1 %collective-permute-done.1.high_ref = bf16[4,272,128]{2,1,0:T(8,128)(2,1)S(1)} collective-permute-done((bf16[4,272,128]{2,1,0:T(8,128)(2,1)}, bf16[4,272,128]{2,1,0:T(8,128)(2,1)S(1)}, u32[]{:S(2)}, u32[]{:S(2)}) %collective-permute-start.1) | collective-permute-done | bytes 278560 | tf_op jit(solution)/shard_map/ppermute | solution.py:367
  41.1 2.2 %linear.1 = (f32[8,128,128]{2,1,0:T(8,128)S(1)}, f32[8,128,128]{2,1,0:T(8,128)S(1)}, f32[136,128]{1,0:T(8,128)S(1)}, bf16[8,128,128]{2,1,0:T(8,128)(2,1)S(1)}) custom-call(s32[3]{0:T(128)S(1)} %pad_add_fusion.info_ref, bf16[8,400,128]{2,1,0:T(8,128)(2,1)S(1)} %all_to_all.10.own_ref, bf16[4,272,128]{2,1,0:T(8,128)(2,1)S(1)} %collective-permute-done.low_ref, ...), custom_call_target="tpu_custom_call" | custom-call | tf_op jit(solution)/shard_map/linear/pallas_call | solution.py:373
  43.4 1.9 %collective-permute-start.2 = (f32[136,128]{1,0:T(8,128)S(1)}, f32[136,128]{1,0:T(8,128)S(1)}, u32[]{:S(2)}, u32[]{:S(2)}) collective-permute-start(f32[136,128]{1,0:T(8,128)S(1)} %get-tuple-element.42.state_ref), channel_id=1, source_target_pairs={{0,64},{64,128},{128,192},{1,65},{65,129},{129,193},{2,66},{66,130... | collective-permute-start | bytes 208904 | tf_op jit(solution)/shard_map/ppermute | solution.py:384
  45.3 1.3 %collective-permute-start.3 = (f32[136,128]{1,0:T(8,128)S(1)}, f32[136,128]{1,0:T(8,128)S(1)}, u32[]{:S(2)}, u32[]{:S(2)}) collective-permute-start(f32[136,128]{1,0:T(8,128)S(1)} %get-tuple-element.42.state_ref), channel_id=1, source_target_pairs={{0,128},{64,192},{1,129},{65,193},{2,130},{66,194},{3,131},{67,195... | collective-permute-start | bytes 208904 | tf_op jit(solution)/shard_map/ppermute | solution.py:385
  46.6 1.3 %collective-permute-start.4 = (bf16[8,272,128]{2,1,0:T(8,128)(2,1)S(1)}, bf16[8,272,128]{2,1,0:T(8,128)(2,1)S(1)}, u32[]{:S(2)}, u32[]{:S(2)}) collective-permute-start(bf16[8,272,128]{2,1,0:T(8,128)(2,1)S(1)} %slice.20), channel_id=1, source_target_pairs={{0,128},{64,192},{1,129},{65,193},{2,130},{66,194},{3,131},{67,195... | collective-permute-start | bytes 1671176 | tf_op jit(solution)/shard_map/ppermute | solution.py:390
  47.9 3.1 %own_window.1 = (f32[1024,128]{1,0:T(8,128)S(1)}, f32[1024,128]{1,0:T(8,128)S(1)}, f32[1024,128]{1,0:T(8,128)S(1)}) custom-call(s32[3]{0:T(128)S(1)} %pad_add_fusion.info_ref, bf16[8,400,128]{2,1,0:T(8,128)(2,1)S(1)} %all_to_all.10.own_ref, bf16[4,272,128]{2,1,0:T(8,128)(2,1)S(1)} %collective-permute-done.low_ref, ...), custom_call_target="tpu_custom_call" | custom-call | tf_op jit(solution)/shard_map/own_window/pallas_call | solution.py:386
  51.1 2.3 %collective-permute-done.3.far_ref = f32[136,128]{1,0:T(8,128)S(1)} collective-permute-done((f32[136,128]{1,0:T(8,128)S(1)}, f32[136,128]{1,0:T(8,128)S(1)}, u32[]{:S(2)}, u32[]{:S(2)}) %collective-permute-start.3) | collective-permute-done | bytes 69664 | tf_op jit(solution)/shard_map/ppermute | solution.py:385
  53.5 0.5 collective-permute-start.7
  54.0 1.4 %enter.1 = (bf16[8,128,128]{2,1,0:T(8,128)(2,1)S(1)}, f32[8,128]{1,0:T(8,128)S(1)}, s32[8]{0:T(128)S(1)}) custom-call(s32[3]{0:T(128)S(1)} %pad_add_fusion.info_ref, bf16[8,400,128]{2,1,0:T(8,128)(2,1)S(1)} %all_to_all.10.own_ref, f32[8,128,128]{2,1,0:T(8,128)S(1)} %get-tuple-element.40.partial_ref, f32[8,128,128]{2,1,0:T(8,128)S(1)} %get-tuple-element.41.weight_ref, ...), custom_call_target="tpu_custom_call" | custom-call | tf_op jit(solution)/shard_map/enter/pallas_call | solution.py:392
  55.5 1.7 %collective-permute-start.8 = (f32[8,128]{1,0:T(8,128)S(1)}, f32[8,128]{1,0:T(8,128)S(1)}, u32[]{:S(2)}, u32[]{:S(2)}) collective-permute-start(f32[8,128]{1,0:T(8,128)S(1)} %get-tuple-element.61), channel_id=1, source_target_pairs={{0,1},{1,0},{2,3},{3,2},{4,5},{5,4},{6,7},{7,6},{8,9},{9,8},{10,11... | collective-permute-start | bytes 12296 | tf_op jit(solution)/shard_map/ppermute | solution.py:401
  57.1 2.9 %collective-permute-start.9 = (f32[8,128]{1,0:T(8,128)S(1)}, f32[8,128]{1,0:T(8,128)S(1)}, u32[]{:S(2)}, u32[]{:S(2)}) collective-permute-start(f32[8,128]{1,0:T(8,128)S(1)} %get-tuple-element.61), channel_id=1, source_target_pairs={{0,2},{1,3},{2,0},{3,1},{4,6},{5,7},{6,4},{7,5},{8,10},{9,11},{10,... | collective-permute-start | bytes 12296 | tf_op jit(solution)/shard_map/ppermute | solution.py:401
  60.0 0.2 collective-permute-start.10
  60.3 4.5 %near_window.1 = (f32[1024,128]{1,0:T(8,128)S(1)}, f32[1024,128]{1,0:T(8,128)S(1)}, f32[1024,128]{1,0:T(8,128)S(1)}) custom-call(s32[8]{0:T(128)S(1)} %get-tuple-element.49.need_ref, bf16[8,400,128]{2,1,0:T(8,128)(2,1)S(1)} %all_to_all.10.own_ref, bf16[8,128,128]{2,1,0:T(8,128)(2,1)S(1)} %get-tuple-element.43.mark_ref, ...), custom_call_target="tpu_custom_call" | custom-call | tf_op jit(solution)/shard_map/near_window/pallas_call | solution.py:402
  64.9 0.2 collective-permute-done.4.far_ref
  65.1 2.7 %far_own.1 = (f32[1024,128]{1,0:T(8,128)S(1)}, f32[1024,128]{1,0:T(8,128)S(1)}, f32[1024,128]{1,0:T(8,128)S(1)}) custom-call(s32[3]{0:T(128)S(1)} %pad_add_fusion.info_ref, s32[8]{0:T(128)S(1)} %get-tuple-element.49.need_ref, bf16[8,400,128]{2,1,0:T(8,128)(2,1)S(1)} %all_to_all.10.own_ref, bf16[8,128,128]{2,1,0:T(8,128)(2,1)S(1)} %get-tuple-element.43.mark_ref, ...), custom_call_target="tpu_custom_call" | custom-call | tf_op jit(solution)/shard_map/far_own/pallas_call | solution.py:408
  67.8 2.8 %far_other.1 = bf16[8,272,128]{2,1,0:T(8,128)(2,1)S(1)} custom-call(s32[3]{0:T(128)S(1)} %pad_add_fusion.info_ref, s32[8]{0:T(128)S(1)} %get-tuple-element.49.need_ref, bf16[8,400,128]{2,1,0:T(8,128)(2,1)S(1)} %all_to_all.10.own_ref, bf16[8,128,128]{2,1,0:T(8,128)(2,1)S(1)} %get-tuple-element.43.mark_ref, ...), custom_call_target="tpu_custom_call" | custom-call | tf_op jit(solution)/shard_map/far_other/pallas_call | solution.py:409
  70.7 21.1 %all_to_all.11.got_ref = bf16[8,272,128]{2,1,0:T(8,128)(2,1)S(1)} all-to-all(bf16[8,272,128]{2,1,0:T(8,128)(2,1)S(1)} %far_other.1), channel_id=1, replica_groups=mesh['x'=4,'z'=8,'core'=2,'head'=4] {'z'}, dimensions={0} | all-to-all | bytes 1114112 | tf_op jit(solution)/shard_map/all_to_all | solution.py:416
  91.7 0.9 finish.1
  (21 shorter events, 0.5 us)
Async XLA Ops:
  0.0 39.8 %copy-start = (f32[8,128,128]{2,1,0:T(8,128)S(1)}, f32[8,128,128]{2,1,0:T(8,128)}, u32[]{:S(2)}) copy-start(f32[8,128,128]{2,1,0:T(8,128)} %param.13) | copy-start | bytes 1572868
  35.3 18.1 %collective-permute-start.5 = (bf16[8,272,128]{2,1,0:T(8,128)(2,1)S(1)}, bf16[8,272,128]{2,1,0:T(8,128)(2,1)S(1)}, u32[]{:S(2)}, u32[]{:S(2)}) collective-permute-start(bf16[8,272,128]{2,1,0:T(8,128)(2,1)S(1)} %slice.20), channel_id=1, source_target_pairs={{0,64},{64,128},{128,192},{1,65},{65,129},{129,193},{2,66},{66,130... | collective-permute-start | bytes 1671176 | tf_op jit(solution)/shard_map/ppermute | solution.py:364
  38.4 1.6 %collective-permute-start = (bf16[4,272,128]{2,1,0:T(8,128)(2,1)S(1)}, bf16[4,272,128]{2,1,0:T(8,128)(2,1)S(1)}, u32[]{:S(2)}, u32[]{:S(2)}) collective-permute-start(bf16[4,272,128]{2,1,0:T(8,128)(2,1)S(1)} %slice.21), channel_id=1, source_target_pairs={{0,4},{4,0},{1,5},{5,1},{2,6},{6,2},{3,7},{7,3},{8,12},{12,8},{9,1... | collective-permute-start | bytes 835592 | tf_op jit(solution)/shard_map/ppermute | solution.py:366
  39.2 1.9 %collective-permute-start.1 = (bf16[4,272,128]{2,1,0:T(8,128)(2,1)}, bf16[4,272,128]{2,1,0:T(8,128)(2,1)S(1)}, u32[]{:S(2)}, u32[]{:S(2)}) collective-permute-start(bf16[4,272,128]{2,1,0:T(8,128)(2,1)} %slice.22), channel_id=1, source_target_pairs={{0,4},{4,0},{1,5},{5,1},{2,6},{6,2},{3,7},{7,3},{8,12},{12,8},{9,1... | collective-permute-start | bytes 835592 | tf_op jit(solution)/shard_map/ppermute | solution.py:367
  43.4 7.7 %collective-permute-start.2 = (f32[136,128]{1,0:T(8,128)S(1)}, f32[136,128]{1,0:T(8,128)S(1)}, u32[]{:S(2)}, u32[]{:S(2)}) collective-permute-start(f32[136,128]{1,0:T(8,128)S(1)} %get-tuple-element.42.state_ref), channel_id=1, source_target_pairs={{0,64},{64,128},{128,192},{1,65},{65,129},{129,193},{2,66},{66,130... | collective-permute-start | bytes 208904 | tf_op jit(solution)/shard_map/ppermute | solution.py:384
  45.3 8.1 %collective-permute-start.3 = (f32[136,128]{1,0:T(8,128)S(1)}, f32[136,128]{1,0:T(8,128)S(1)}, u32[]{:S(2)}, u32[]{:S(2)}) collective-permute-start(f32[136,128]{1,0:T(8,128)S(1)} %get-tuple-element.42.state_ref), channel_id=1, source_target_pairs={{0,128},{64,192},{1,129},{65,193},{2,130},{66,194},{3,131},{67,195... | collective-permute-start | bytes 208904 | tf_op jit(solution)/shard_map/ppermute | solution.py:385
  46.6 18.5 %collective-permute-start.4 = (bf16[8,272,128]{2,1,0:T(8,128)(2,1)S(1)}, bf16[8,272,128]{2,1,0:T(8,128)(2,1)S(1)}, u32[]{:S(2)}, u32[]{:S(2)}) collective-permute-start(bf16[8,272,128]{2,1,0:T(8,128)(2,1)S(1)} %slice.20), channel_id=1, source_target_pairs={{0,128},{64,192},{1,129},{65,193},{2,130},{66,194},{3,131},{67,195... | collective-permute-start | bytes 1671176 | tf_op jit(solution)/shard_map/ppermute | solution.py:390
  53.4 6.6 %collective-permute-start.6 = (bf16[4,272,128]{2,1,0:T(8,128)(2,1)S(1)}, bf16[4,272,128]{2,1,0:T(8,128)(2,1)S(1)}, u32[]{:S(2)}, u32[]{:S(2)}) collective-permute-start(bf16[4,272,128]{2,1,0:T(8,128)(2,1)S(1)} %get-tuple-element.74), channel_id=1, source_target_pairs={{0,4},{4,0},{1,5},{5,1},{2,6},{6,2},{3,7},{7,3},{8,12},{12,8},{9,1... | collective-permute-start | bytes 835592 | tf_op jit(solution)/shard_map/ppermute | solution.py:400
  53.5 6.7 %collective-permute-start.7 = (bf16[4,272,128]{2,1,0:T(8,128)(2,1)S(1)}, bf16[4,272,128]{2,1,0:T(8,128)(2,1)S(1)}, u32[]{:S(2)}, u32[]{:S(2)}) collective-permute-start(bf16[4,272,128]{2,1,0:T(8,128)(2,1)S(1)} %get-tuple-element.73), channel_id=1, source_target_pairs={{0,4},{4,0},{1,5},{5,1},{2,6},{6,2},{3,7},{7,3},{8,12},{12,8},{9,1... | collective-permute-start | bytes 835592 | tf_op jit(solution)/shard_map/ppermute | solution.py:400
  55.5 9.3 %collective-permute-start.8 = (f32[8,128]{1,0:T(8,128)S(1)}, f32[8,128]{1,0:T(8,128)S(1)}, u32[]{:S(2)}, u32[]{:S(2)}) collective-permute-start(f32[8,128]{1,0:T(8,128)S(1)} %get-tuple-element.61), channel_id=1, source_target_pairs={{0,1},{1,0},{2,3},{3,2},{4,5},{5,4},{6,7},{7,6},{8,9},{9,8},{10,11... | collective-permute-start | bytes 12296 | tf_op jit(solution)/shard_map/ppermute | solution.py:401
  57.1 7.6 %collective-permute-start.9 = (f32[8,128]{1,0:T(8,128)S(1)}, f32[8,128]{1,0:T(8,128)S(1)}, u32[]{:S(2)}, u32[]{:S(2)}) collective-permute-start(f32[8,128]{1,0:T(8,128)S(1)} %get-tuple-element.61), channel_id=1, source_target_pairs={{0,2},{1,3},{2,0},{3,1},{4,6},{5,7},{6,4},{7,5},{8,10},{9,11},{10,... | collective-permute-start | bytes 12296 | tf_op jit(solution)/shard_map/ppermute | solution.py:401
  60.0 4.8 %collective-permute-start.10 = (f32[8,128]{1,0:T(8,128)S(1)}, f32[8,128]{1,0:T(8,128)S(1)}, u32[]{:S(2)}, u32[]{:S(2)}) collective-permute-start(f32[8,128]{1,0:T(8,128)S(1)} %get-tuple-element.61), channel_id=1, source_target_pairs={{0,3},{1,2},{2,1},{3,0},{4,7},{5,6},{6,5},{7,4},{8,11},{9,10},{10,... | collective-permute-start | bytes 12296 | tf_op jit(solution)/shard_map/ppermute | solution.py:401
  65.1 2.7 %collective-permute-start.11 = (bf16[8,272,128]{2,1,0:T(8,128)(2,1)S(1)}, bf16[8,272,128]{2,1,0:T(8,128)(2,1)S(1)}, u32[]{:S(2)}, u32[]{:S(2)}) collective-permute-start(bf16[8,272,128]{2,1,0:T(8,128)(2,1)S(1)} %collective-permute-done.4.far_ref), channel_id=1, source_target_pairs={{0,4},{4,0},{1,5},{5,1},{2,6},{6,2},{3,7},{7,3},{8,12},{12,8},{9,1... | collective-permute-start | bytes 1671176 | tf_op jit(solution)/shard_map/ppermute | solution.py:407
  70.7 21.1 %copy-start.1 = (f32[1024]{0:T(1024)S(1)}, f32[1024]{0:T(1024)}, u32[]{:S(2)}) copy-start(f32[1024]{0:T(1024)} %param.14) | copy-start | bytes 12292
